TPU v7x, 256 devices: a whole 4x4x8 slice. The times are simulated.
256 devices in a mesh: tm: 64 (over z, x, core), rows: 4 (over y).
Axes of the slice: x: 4, y: 4, z: 8, core: 2. Of those that a mesh axis runs over, the one named last changes fastest.
Arguments:
- sensed_flows_levels: float32 [256, 512], P('tm'), may hold values from -6 to 6
- reading_mask: int32 [256, 512], P('tm'), may hold values 0 or 1
- inventory_propagator: float32 [1024, 1024], replicated, may hold values from -1 to 1
- observation_matrix: float32 [512, 1024], replicated, may hold values from -0.1875 to 0.1875
- measurement_weight: float32 [512], replicated, may hold values from 0.05 to 0.3
- diagonal_blend_factor: float32 [256, 1024], P('tm', 'rows'), may hold values from 0 to 1
- prior_inventory_mean: float32 [1024], replicated, may hold values from -6 to 6
Outputs:
- updated_inventory_means: float32 [256, 1024], P('tm', 'rows')
- reconciled_inventories: float32 [256, 1024], P('tm', 'rows')
All inputs are finite; a program needn't handle non-finite values. No bound on the sum of `reading_mask` on one device may be relied on, other than what follows from the above.
Results may differ from a plain program's by a relative error of at most 0.0003.
Values sent between devices are 32-bit elements; how exact they have to be, the bound alone decides.
No kernel may reach another device: no remote copies, remote signals or barrier semaphores. Data moves between devices by JAX's collectives and lax.ppermute only.
A program may use at most 64 MiB of HBM per device.

v0:
```python
import jax
import jax.numpy as jnp
from jax import lax
from jax.sharding import PartitionSpec as P

precise = lax.Precision.HIGHEST


def from_behind(value, axis, steps):
    count = lax.axis_size(axis)
    initial, last = (max(0, -steps), min(count, count - steps))
    return lax.ppermute(value, axis, [(source, source + steps) for source in range(initial, last)])


def carried_in(part, axis, combine, identity):
    count = lax.axis_size(axis)
    place = lax.axis_index(axis)
    ahead = count - 1 - place
    gathered = jax.tree.map(lambda a: lax.all_gather(a, axis), part)
    state = jax.tree.map(lambda a, e: jnp.zeros_like(a) + jnp.asarray(e, a.dtype), part, identity)

    def one(lap, state):
        source = count - 1 - lap
        return combine(
            state, jax.tree.map(lambda a: lax.dynamic_index_in_dim(a, source, 0, False), gathered)
        )

    return lax.fori_loop(0, ahead, one, state)


def linear_map_apply(matrix, vector):
    return jnp.dot(matrix, vector, precision=precise, preferred_element_type=jnp.float32)


def kalman_recursion(
    initial, sensed_flows_levels, blending_coefficients, inventory_propagator, observation_matrix
):
    propagated_mean = linear_map_apply(inventory_propagator, initial)
    trajectory_record = []
    prior_means_sequence = []
    for epoch_position in range(sensed_flows_levels.shape[0]):
        innovation = blending_coefficients[epoch_position] * (
            sensed_flows_levels[epoch_position]
            - linear_map_apply(observation_matrix, propagated_mean)
        )
        current_mean = propagated_mean + jnp.dot(
            innovation, observation_matrix, precision=precise, preferred_element_type=jnp.float32
        )
        propagated_mean = linear_map_apply(inventory_propagator, current_mean)
        trajectory_record.append(current_mean)
        prior_means_sequence.append(propagated_mean)
    return (trajectory_record, prior_means_sequence)


def compose_rows(
    inventory_propagator,
    observation_matrix,
    blending_coefficients,
    sensed_flows_levels,
    first_entry_position,
    number_entries_in_column,
):
    width = inventory_propagator.shape[0]
    row_ids = (
        lax.broadcasted_iota(jnp.int32, (number_entries_in_column, width), 0) + first_entry_position
    )
    col_ids = lax.broadcasted_iota(jnp.int32, (number_entries_in_column, width), 1)
    product = (row_ids == col_ids).astype(jnp.float32)
    offset_rows = jnp.zeros((number_entries_in_column,), jnp.float32)
    number_epochs = blending_coefficients.shape[0]
    for epoch_position in reversed(range(number_epochs)):
        if epoch_position == number_epochs - 1:
            projected = jnp.transpose(
                lax.dynamic_slice_in_dim(
                    observation_matrix, first_entry_position, number_entries_in_column, 1
                )
            )
        else:
            projected = lax.dot_general(
                product,
                observation_matrix,
                (((1,), (1,)), ((), ())),
                precision=precise,
                preferred_element_type=jnp.float32,
            )
        offset_rows = offset_rows + linear_map_apply(
            projected, blending_coefficients[epoch_position] * sensed_flows_levels[epoch_position]
        )
        corrected = product - jnp.dot(
            projected * blending_coefficients[epoch_position],
            observation_matrix,
            precision=precise,
            preferred_element_type=jnp.float32,
        )
        product = jnp.dot(
            corrected, inventory_propagator, precision=precise, preferred_element_type=jnp.float32
        )
    return (product, offset_rows)


def pass_pair(map_pair, distance):
    return from_behind(map_pair, "tm", distance)


def fold_pair(own_map, received, with_matrix):
    number_entries_in_column = own_map.shape[0]
    initial = (jnp.zeros_like(own_map), jnp.zeros((number_entries_in_column,), jnp.float32))
    pieces = (
        lax.all_gather(received[0], "rows", axis=0, tiled=True),
        lax.all_gather(received[1], "rows", axis=0, tiled=True),
    )
    vector_total = linear_map_apply(own_map, pieces[1])
    if with_matrix:
        matrix_total = jnp.dot(
            own_map, pieces[0], precision=precise, preferred_element_type=jnp.float32
        )
    else:
        matrix_total = initial[0]
    return (matrix_total, vector_total)


def link(earlier, later):
    return (later[0] * earlier[0], later[0] * earlier[1] + later[1])


def body(
    sensed_flows_levels,
    reading_mask,
    inventory_propagator,
    observation_matrix,
    measurement_weight,
    diagonal_blend_factor,
    prior_inventory_mean,
):
    blending_coefficients = reading_mask.astype(jnp.float32) * measurement_weight[None, :]
    width = inventory_propagator.shape[0]
    number_entries_in_column = width // lax.axis_size("rows")
    first_entry_position = lax.axis_index("rows") * number_entries_in_column
    chain_pos = lax.axis_index("tm")
    chain_len = lax.axis_size("tm")
    group_map, offset_rows = compose_rows(
        inventory_propagator,
        observation_matrix,
        blending_coefficients,
        sensed_flows_levels,
        first_entry_position,
        number_entries_in_column,
    )
    prior_rows = lax.dynamic_slice_in_dim(
        prior_inventory_mean, first_entry_position, number_entries_in_column
    )
    shifted = pass_pair((group_map, offset_rows), 1)
    matrix_part = shifted[0]
    vector_part = jnp.where(chain_pos == 0, prior_rows, shifted[1])
    distance = 1
    while distance < chain_len:
        received = pass_pair((matrix_part, vector_part), distance)
        matrix_next, vector_next = fold_pair(matrix_part, received, 2 * distance < chain_len)
        matrix_part = matrix_next
        vector_part = vector_next + vector_part
        distance = distance * 2
    incoming_state = lax.all_gather(vector_part, "rows", axis=0, tiled=True)
    trajectory_record, prior_means_sequence = kalman_recursion(
        incoming_state,
        sensed_flows_levels,
        blending_coefficients,
        inventory_propagator,
        observation_matrix,
    )
    mean_grid = lax.dynamic_slice_in_dim(
        jnp.stack(trajectory_record), first_entry_position, number_entries_in_column, 1
    )
    prior_mean_grid = lax.dynamic_slice_in_dim(
        jnp.stack(prior_means_sequence), first_entry_position, number_entries_in_column, 1
    )
    number_epochs = mean_grid.shape[0]
    factor = jnp.ones((number_entries_in_column,), jnp.float32)
    constant = jnp.zeros((number_entries_in_column,), jnp.float32)
    for epoch_position in reversed(range(number_epochs)):
        constant = diagonal_blend_factor[epoch_position] * constant + (
            mean_grid[epoch_position]
            - diagonal_blend_factor[epoch_position] * prior_mean_grid[epoch_position]
        )
        factor = factor * diagonal_blend_factor[epoch_position]
    interval_edge = prior_mean_grid[number_epochs - 1]
    is_last = chain_pos == chain_len - 1
    element = (
        jnp.where(is_last, 0.0, factor),
        jnp.where(is_last, factor * interval_edge + constant, constant),
    )
    identity = (
        jnp.ones((number_entries_in_column,), jnp.float32),
        jnp.zeros((number_entries_in_column,), jnp.float32),
    )
    prefix = carried_in((element[0], element[1]), "tm", link, identity)
    current_mean = jnp.where(is_last, interval_edge, prefix[1])
    reconciled_inventories = []
    for epoch_position in reversed(range(number_epochs)):
        current_mean = mean_grid[epoch_position] + diagonal_blend_factor[epoch_position] * (
            current_mean - prior_mean_grid[epoch_position]
        )
        reconciled_inventories.insert(0, current_mean)
    return (mean_grid, jnp.stack(reconciled_inventories))


def solution(mesh):
    placed = (P("tm", None), P("tm", None), P(), P(), P(), P("tm", "rows"), P())
    return jax.shard_map(
        body,
        mesh=mesh,
        in_specs=placed,
        out_specs=(P("tm", "rows"), P("tm", "rows")),
        check_vma=False,
    )
```

profile of v0, /device:TPU:1, one launch (start us, length us, event | category | flops | bytes accessed | tf_op | source)
XLA Modules:
  0.0 712.4 jit_solution(11287476826315219716)
XLA Ops:
  7.9 3.8 convolution_subtract_fusion.3
  11.7 6.3 fusion.36
  23.1 3.7 fusion.38
  31.5 3.9 fusion.40
  40.1 3.7 fusion.42
  43.8 4.5 collective-permute-start
  48.3 11.7 %collective-permute-done = f32[256,1024]{1,0:T(8,128)S(1)} collective-permute-done((f32[256,1024]{1,0:T(8,128)S(1)}, f32[256,1024]{1,0:T(8,128)S(1)}, u32[]{:S(2)}, u32[]{:S(2)}) %collective-permute-start) | collective-permute-done | bytes 1048608 | tf_op jit(solution)/shard_map/ppermute | solution.py:12
  61.0 4.4 collective-permute-start.1
  65.4 11.7 %collective-permute-done.1 = f32[256,1024]{1,0:T(8,128)S(1)} collective-permute-done((f32[256,1024]{1,0:T(8,128)S(1)}, f32[256,1024]{1,0:T(8,128)S(1)}, u32[]{:S(2)}, u32[]{:S(2)}) %collective-permute-start.1) | collective-permute-done | bytes 1048608 | tf_op jit(solution)/shard_map/ppermute | solution.py:12
  78.2 58.8 %all-gather.15.cloned.1.call-done = f32[1024,1024]{1,0:T(8,128)} async-done(((f32[256,1024]{1,0:T(8,128)}), f32[1024,1024]{1,0:T(8,128)}) %all-gather.15.cloned.1.call-update) | async-done | bytes 4194320 | tf_op jit(solution)/shard_map/all_gather | solution.py:109
  137.0 6.0 fusion.43
  143.0 4.1 collective-permute-start.2
  147.1 20.8 %collective-permute-done.2 = f32[256,1024]{1,0:T(8,128)} collective-permute-done((f32[256,1024]{1,0:T(8,128)S(1)}, f32[256,1024]{1,0:T(8,128)}, u32[]{:S(2)}, u32[]{:S(2)}) %collective-permute-start.2) | collective-permute-done | bytes 1048608 | tf_op jit(solution)/shard_map/ppermute | solution.py:12
  168.0 54.2 %all-gather.17.cloned.1.call-done = f32[1024,1024]{1,0:T(8,128)} async-done(((f32[256,1024]{1,0:T(8,128)}), f32[1024,1024]{1,0:T(8,128)}) %all-gather.17.cloned.1.call-update) | async-done | bytes 4194320 | tf_op jit(solution)/shard_map/all_gather | solution.py:109
  222.2 6.1 fusion.44
  228.3 5.6 collective-permute-start.3
  233.9 20.8 %collective-permute-done.3 = f32[256,1024]{1,0:T(8,128)} collective-permute-done((f32[256,1024]{1,0:T(8,128)S(1)}, f32[256,1024]{1,0:T(8,128)}, u32[]{:S(2)}, u32[]{:S(2)}) %collective-permute-start.3) | collective-permute-done | bytes 1048608 | tf_op jit(solution)/shard_map/ppermute | solution.py:12
  254.8 53.9 %all-gather.19.cloned.1.call-done = f32[1024,1024]{1,0:T(8,128)} async-done(((f32[256,1024]{1,0:T(8,128)}), f32[1024,1024]{1,0:T(8,128)}) %all-gather.19.cloned.1.call-update) | async-done | bytes 4194320 | tf_op jit(solution)/shard_map/all_gather | solution.py:109
  308.7 6.0 fusion.45
  315.7 3.2 collective-permute-start.4
  318.9 21.7 %collective-permute-done.4 = f32[256,1024]{1,0:T(8,128)S(1)} collective-permute-done((f32[256,1024]{1,0:T(8,128)S(1)}, f32[256,1024]{1,0:T(8,128)S(1)}, u32[]{:S(2)}, u32[]{:S(2)}) %collective-permute-start.4) | collective-permute-done | bytes 1048608 | tf_op jit(solution)/shard_map/ppermute | solution.py:12
  341.7 54.3 %all-gather.21.cloned.1.call-done = f32[1024,1024]{1,0:T(8,128)} async-done(((f32[256,1024]{1,0:T(8,128)}), f32[1024,1024]{1,0:T(8,128)}) %all-gather.21.cloned.1.call-update) | async-done | bytes 4194320 | tf_op jit(solution)/shard_map/all_gather | solution.py:109
  396.0 6.0 fusion.46
  402.0 5.1 collective-permute-start.5
  407.1 20.9 %collective-permute-done.5 = f32[256,1024]{1,0:T(8,128)} collective-permute-done((f32[256,1024]{1,0:T(8,128)S(1)}, f32[256,1024]{1,0:T(8,128)}, u32[]{:S(2)}, u32[]{:S(2)}) %collective-permute-start.5) | collective-permute-done | bytes 1048608 | tf_op jit(solution)/shard_map/ppermute | solution.py:12
  433.2 4.5 collective-permute-start.6
  439.2 4.2 collective-permute-start.7
  444.1 6.0 all-gather
  452.3 3.3 collective-permute-start.8
  456.3 6.0 all-gather.1
  464.4 30.2 %collective-permute-start.9 = (f32[256]{0:T(256)S(1)}, f32[256]{0:T(256)S(1)}, u32[]{:S(2)}, u32[]{:S(2)}) collective-permute-start(f32[256]{0:T(256)S(1)} %add.114), channel_id=1, source_target_pairs={{0,16},{4,20},{8,24},{12,28},{16,32},{20,36},{24,40},{28,44},{32,4... | collective-permute-start | bytes 3080 | tf_op jit(solution)/shard_map/ppermute | solution.py:12
  495.4 6.8 all-gather.2
  503.1 6.0 collective-permute-start.10
  509.8 6.0 all-gather.3
  518.0 5.6 collective-permute-start.11
  524.3 6.0 all-gather.4
  531.2 14.3 %collective-permute-start.12 = (f32[256]{0:T(256)S(1)}, f32[256]{0:T(256)S(1)}, u32[]{:S(2)}, u32[]{:S(2)}) collective-permute-start(f32[256]{0:T(256)S(1)} %add.117), channel_id=1, source_target_pairs={{0,128},{4,132},{8,136},{12,140},{16,144},{20,148},{24,152},{28,15... | collective-permute-start | bytes 3080 | tf_op jit(solution)/shard_map/ppermute | solution.py:12
  545.5 59.3 %all-gather.7 = f32[64,1,256]{2,1,0:T(1,128)S(1)} all-gather(f32[1,1,256]{2,1,0:T(1,128)S(1)} %fusion.29), channel_id=1, replica_groups=mesh['tm'=64,'rows'=4] {'tm'}, dimensions={0}, use_global_device_ids=true | all-gather | bytes 66560 | tf_op jit(solution)/shard_map/all_gather | solution.py:19
  604.8 5.9 all-gather.5
  610.7 5.9 fusion.47
  617.5 6.2 all-gather.6
  623.7 3.5 fusion.57
  630.2 3.5 fusion.59
  636.7 3.7 fusion.61
  643.4 3.5 fusion.63
  649.9 3.5 fusion.65
  653.6 47.8 %all-gather.8 = f32[64,1,256]{2,1,0:T(1,128)S(1)} all-gather(f32[1,1,256]{2,1,0:T(1,128)S(1)} %get-tuple-element.111), channel_id=1, replica_groups=mesh['tm'=64,'rows'=4] {'tm'}, dimensions={0}, use_global_device_ids=true | all-gather | bytes 66560 | tf_op jit(solution)/shard_map/all_gather | solution.py:19
  701.4 3.6 while.14
  (232 shorter events, 52.5 us)
Async XLA Ops:
  7.2 129.9 %all-gather.15.cloned.1.call-start = ((), (), s32[]{:S(2)}) async-start(), calls=%async_computation | async-start | bytes 5242880 | tf_op jit(solution)/shard_map/all_gather | solution.py:109
  11.7 6.4 copy-start
  20.0 0.8 copy-start.7
  20.9 2.2 copy-start.1
  28.7 0.8 copy-start.8
  37.4 0.8 copy-start.9
  43.8 16.2 %collective-permute-start = (f32[256,1024]{1,0:T(8,128)S(1)}, f32[256,1024]{1,0:T(8,128)S(1)}, u32[]{:S(2)}, u32[]{:S(2)}) collective-permute-start(f32[256,1024]{1,0:T(8,128)S(1)} %fusion.42), channel_id=1, source_target_pairs={{0,4},{4,8},{8,12},{12,16},{16,20},{20,24},{24,28},{28,32},{32,36}... | collective-permute-start | bytes 3145736 | tf_op jit(solution)/shard_map/ppermute | solution.py:12
  60.0 1.0 copy-start.10
  61.0 16.1 %collective-permute-start.1 = (f32[256,1024]{1,0:T(8,128)S(1)}, f32[256,1024]{1,0:T(8,128)S(1)}, u32[]{:S(2)}, u32[]{:S(2)}) collective-permute-start(f32[256,1024]{1,0:T(8,128)S(1)} %collective-permute-done), channel_id=1, source_target_pairs={{0,4},{4,8},{8,12},{12,16},{16,20},{20,24},{24,28},{28,32},{32,36}... | collective-permute-start | bytes 3145736 | tf_op jit(solution)/shard_map/ppermute | solution.py:12
  77.1 1.0 copy-start.11
  78.2 144.0 %all-gather.17.cloned.1.call-start = ((), (), s32[]{:S(2)}) async-start(), calls=%async_computation.1 | async-start | bytes 5242880 | tf_op jit(solution)/shard_map/all_gather | solution.py:109
  143.0 85.3 %copy-start.3 = (f32[256,1024]{1,0:T(8,128)}, f32[256,1024]{1,0:T(8,128)S(1)}, u32[]{:S(2)}) copy-start(f32[256,1024]{1,0:T(8,128)S(1)} %fusion.43) | copy-start | bytes 3145732
  143.0 24.9 %collective-permute-start.2 = (f32[256,1024]{1,0:T(8,128)S(1)}, f32[256,1024]{1,0:T(8,128)}, u32[]{:S(2)}, u32[]{:S(2)}) collective-permute-start(f32[256,1024]{1,0:T(8,128)S(1)} %fusion.43), channel_id=1, source_target_pairs={{0,8},{4,12},{8,16},{12,20},{16,24},{20,28},{24,32},{28,36},{32,40... | collective-permute-start | bytes 3145736 | tf_op jit(solution)/shard_map/ppermute | solution.py:12
  167.9 140.7 %all-gather.19.cloned.1.call-start = ((), (), s32[]{:S(2)}) async-start(), calls=%async_computation.2 | async-start | bytes 5242880 | tf_op jit(solution)/shard_map/all_gather | solution.py:109
  228.3 5.7 copy-start.4
  228.3 26.4 %collective-permute-start.3 = (f32[256,1024]{1,0:T(8,128)S(1)}, f32[256,1024]{1,0:T(8,128)}, u32[]{:S(2)}, u32[]{:S(2)}) collective-permute-start(f32[256,1024]{1,0:T(8,128)S(1)} %fusion.44), channel_id=1, source_target_pairs={{0,16},{4,20},{8,24},{12,28},{16,32},{20,36},{24,40},{28,44},{32,4... | collective-permute-start | bytes 3145736 | tf_op jit(solution)/shard_map/ppermute | solution.py:12
  254.7 141.3 %all-gather.21.cloned.1.call-start = ((), (), s32[]{:S(2)}) async-start(), calls=%async_computation.3 | async-start | bytes 5242880 | tf_op jit(solution)/shard_map/all_gather | solution.py:109
  314.7 1.0 copy-start.6
  315.7 25.0 %collective-permute-start.4 = (f32[256,1024]{1,0:T(8,128)S(1)}, f32[256,1024]{1,0:T(8,128)S(1)}, u32[]{:S(2)}, u32[]{:S(2)}) collective-permute-start(f32[256,1024]{1,0:T(8,128)S(1)} %fusion.45), channel_id=1, source_target_pairs={{0,32},{4,36},{8,40},{12,44},{16,48},{20,52},{24,56},{28,60},{32,6... | collective-permute-start | bytes 3145736 | tf_op jit(solution)/shard_map/ppermute | solution.py:12
  340.7 1.0 copy-start.12
  341.7 86.4 %copy-start.15 = (f32[4,512]{1,0:T(4,128)S(1)}, f32[4,512]{1,0:T(4,128)}, u32[]{:S(2)}) copy-start(f32[4,512]{1,0:T(4,128)} %param.9) | copy-start | bytes 24580
  341.7 269.0 %all-gather.23.cloned.1.call-start = ((), (), s32[]{:S(2)}) async-start(), calls=%async_computation.4 | async-start | bytes 5242880 | tf_op jit(solution)/shard_map/all_gather | solution.py:109
  402.0 26.0 %collective-permute-start.5 = (f32[256,1024]{1,0:T(8,128)S(1)}, f32[256,1024]{1,0:T(8,128)}, u32[]{:S(2)}, u32[]{:S(2)}) collective-permute-start(f32[256,1024]{1,0:T(8,128)S(1)} %fusion.46), channel_id=1, source_target_pairs={{0,64},{4,68},{8,72},{12,76},{16,80},{20,84},{24,88},{28,92},{32,9... | collective-permute-start | bytes 3145736 | tf_op jit(solution)/shard_map/ppermute | solution.py:12
  433.2 5.2 collective-permute-start.6
  437.8 64.4 %copy-start.5 = (f32[256,1024]{1,0:T(8,128)S(1)}, f32[256,1024]{1,0:T(8,128)}, u32[]{:S(2)}) copy-start(f32[256,1024]{1,0:T(8,128)} %copy-done.4) | copy-start | bytes 3145732
  439.2 4.9 collective-permute-start.7
  450.1 73.4 %copy-start.14 = (f32[4,256]{1,0:T(4,128)S(1)}, f32[4,256]{1,0:T(4,128)}, u32[]{:S(2)}) copy-start(f32[4,256]{1,0:T(4,128)} %param.14) | copy-start | bytes 12292
  452.3 4.0 collective-permute-start.8
  464.4 30.9 %collective-permute-start.9 = (f32[256]{0:T(256)S(1)}, f32[256]{0:T(256)S(1)}, u32[]{:S(2)}, u32[]{:S(2)}) collective-permute-start(f32[256]{0:T(256)S(1)} %add.114), channel_id=1, source_target_pairs={{0,16},{4,20},{8,24},{12,28},{16,32},{20,36},{24,40},{28,44},{32,4... | collective-permute-start | bytes 3080 | tf_op jit(solution)/shard_map/ppermute | solution.py:12
  503.1 6.7 collective-permute-start.10
  518.0 6.3 collective-permute-start.11
  531.2 73.6 %collective-permute-start.12 = (f32[256]{0:T(256)S(1)}, f32[256]{0:T(256)S(1)}, u32[]{:S(2)}, u32[]{:S(2)}) collective-permute-start(f32[256]{0:T(256)S(1)} %add.117), channel_id=1, source_target_pairs={{0,128},{4,132},{8,136},{12,140},{16,144},{20,148},{24,152},{28,15... | collective-permute-start | bytes 3080 | tf_op jit(solution)/shard_map/ppermute | solution.py:12
  610.7 13.0 %copy-start.2 = (f32[1024,1024]{1,0:T(8,128)S(1)}, f32[1024,1024]{1,0:T(8,128)}, u32[]{:S(2)}) copy-start(f32[1024,1024]{1,0:T(8,128)} %param.11) | copy-start | bytes 12582916
  653.5 52.1 %copy-start.13 = (f32[4,256]{1,0:T(4,128)}, f32[4,256]{1,0:T(4,128)S(1)}, u32[]{:S(2)}) copy-start(f32[4,256]{1,0:T(4,128)S(1)} %get-tuple-element.125) | copy-start | bytes 12292
Sparse Core Ops, SparseCore 0:
  78.3 58.6 all-gather.14
  168.1 54.0 all-gather.16
  254.9 53.7 all-gather.18
  341.8 54.1 all-gather.20
  428.2 76.6 all-gather.22
where the time goes:
time: 717 us; the launch traced here: 712 us
  waiting for transfers between devices  333 us (46%)
  blocking collectives  150 us (21%)
  matrix products  107 us (15%)
  starting transfers between devices  95.2 us (13%)
  between operations  14.5 us (2%)
  local copies, waits for them, and re-layouts  7.39 us (1%)
    all_gather x5, waiting for transfers between devices, fold_pair(): lax.all_gather(received[0], 'rows', axis=0, tiled=True)  221 us
    ppermute x13, waiting for transfers between devices, from_behind(): lax.ppermute(value, axis, [(source, source + steps) for source in range(i...  112 us
    all_gather x2, blocking collectives, carried_in(): gathered = jax.tree.map(lambda a: lax.all_gather(a, axis), part)  107 us
    ppermute x13, starting transfers between devices, from_behind(): lax.ppermute(value, axis, [(source, source + steps) for source in range(i...  95 us
    dot_general x19, matrix products, linear_map_apply(): jnp.dot(matrix, vector, precision=precise, preferred_element_type=jnp.flo...  39.5 us
    all_gather x6, blocking collectives, fold_pair(): lax.all_gather(received[1], 'rows', axis=0, tiled=True)  36.7 us
    dot_general x5, matrix products, fold_pair(): jnp.dot(own_map, pieces[0], precision=precise, preferred_element_type=jnp...  29.9 us
    dot_general x4, matrix products, compose_rows(): jnp.dot(corrected, inventory_propagator, precision=precise, preferred_ele...  17.7 us
  transfers between devices with their start and end apart: 18, of which 16 were waited for; matrix products, arithmetic and copies ran while one was open for 2% of the time, Pallas kernels for 0%

commit v1 on v0

v1 whole, which is shorter than its diff:
```python
import functools

import jax
import jax.numpy as jnp
from jax import lax
from jax.experimental import pallas as pl
from jax.experimental.pallas import tpu as pltpu
from jax.sharding import Mesh, PartitionSpec as P

F32 = jnp.float32
TIME = ("z", "x", "c")
ALL = TIME + ("y",)
VMEM = pl.BlockSpec(memory_space=pltpu.VMEM)
SMEM = pl.BlockSpec(memory_space=pltpu.SMEM)


def wide(row):
    return jnp.broadcast_to(row, (8, 128))


def tree(terms):
    while len(terms) > 1:
        terms = [a + b for a, b in zip(terms[::2], terms[1::2])]
    return terms[0]


def column_sums(blocks):
    return jnp.concatenate([jnp.sum(b, axis=0, keepdims=True) for b in blocks], 0)


def propagate(f_ref, x, diff):
    xs = [wide(x[t : t + 1]) for t in range(8)]
    out = []
    for t in range(8):
        spread = None
        for b in range(16):
            i = 8 * (16 * t + b)
            s = tree([f_ref[i : i + 8, 128 * u : 128 * u + 128] * xs[u] for u in range(8)])
            s = wide(jnp.sum(s, axis=1, keepdims=True))
            spread = jnp.where(diff == 8 * b, s, 0.0 if spread is None else spread)
        out.append(spread)
    return column_sums(out)


def update(h_ref, hw_ref, bits_ref, group, bit, z, p, diff):
    ps = [wide(p[t : t + 1]) for t in range(8)]
    zs = [wide(z[q : q + 1]) for q in range(4)]
    acc = [jnp.zeros((8, 128), F32) for _ in range(8)]
    for i in range(64):
        r = slice(8 * i, 8 * i + 8)
        s = tree([h_ref[r, 128 * t : 128 * t + 128] * ps[t] for t in range(8)])
        s = jnp.where(diff == 8 * (i % 16), zs[i // 16], 0.0) - s
        s = wide(jnp.sum(s, axis=1, keepdims=True))
        v = jnp.where((bits_ref[group, r, :] & bit) != 0, s, 0.0)
        acc = [acc[t] + hw_ref[r, 128 * t : 128 * t + 128] * v for t in range(8)]
    return p + column_sums(acc)


def filter_kernel(steps, at_ref, z_ref, bits_ref, f_ref, h_ref, hw_ref, s_ref, x_out, f_out, xh, ph):
    diff = lax.broadcasted_iota(jnp.int32, (8, 128), 1) - lax.broadcasted_iota(jnp.int32, (8, 128), 0)

    def step(k, x):
        p = propagate(f_ref, x, diff)
        ph[k] = p
        x = update(h_ref, hw_ref, bits_ref, k // 32, jnp.int32(1) << (k % 32), z_ref[k], p, diff)
        xh[k] = x
        return x

    x = lax.fori_loop(0, steps, step, s_ref[...])
    ph[steps] = propagate(f_ref, x, diff)
    at = at_ref[0]
    for j in range(4):
        x_out[j] = xh[at + j]
        f_out[j] = ph[at + j + 1]


def run_filter(at, z, bits, f, h, hw, s):
    steps = z.shape[0]
    return pl.pallas_call(
        functools.partial(filter_kernel, steps),
        out_shape=(jax.ShapeDtypeStruct((4, 8, 128), F32),) * 2,
        in_specs=[SMEM] + [VMEM] * 6,
        out_specs=(VMEM, VMEM),
        scratch_shapes=[pltpu.VMEM((steps, 8, 128), F32), pltpu.VMEM((steps + 1, 8, 128), F32)],
        compiler_params=pltpu.CompilerParams(vmem_limit_bytes=40 * 2**20),
        name="filter_all",
    )(at, z, bits, f, h, hw, s)


def smooth_kernel(at_ref, parts_ref, d_ref, x_ref, f_ref, out_ref):
    at = at_ref[0]
    later = f_ref[3]
    count = parts_ref.shape[0]

    def one(i, later):
        j = count - 1 - i
        e = parts_ref[j]
        return jnp.where(j > at, e[0:2] * later + e[2:4], later)

    later = lax.fori_loop(0, count, one, later)
    for j in reversed(range(4)):
        later = x_ref[j] + d_ref[j] * (later - f_ref[j])
        out_ref[j] = later


def body(z, mask, f, h, weight, d, prior):
    at = lax.axis_index(TIME)
    y = lax.axis_index("y")
    own = jnp.concatenate([z, mask.astype(F32)], 0)
    own = lax.dynamic_slice_in_dim(own, 128 * y, 128, 1)
    sent = jnp.broadcast_to(own[None], (256, 8, 128))
    got = lax.all_to_all(sent, ALL, 0, 0, tiled=True)
    got = got.reshape(64, 4, 2, 4, 128)
    z_all = jnp.transpose(got[:, :, 0], (0, 2, 1, 3)).reshape(256, 4, 128)
    m_all = jnp.transpose(got[:, :, 1], (0, 2, 1, 3)).reshape(8, 32, 512).astype(jnp.int32)
    bits = jnp.sum(m_all << lax.broadcasted_iota(jnp.int32, (8, 32, 512), 1), axis=1)
    bits = jnp.broadcast_to(bits[:, :, None], (8, 512, 128))
    x4, f4 = run_filter(
        (4 * at).reshape(1), z_all, bits, f, h, h * weight[:, None], prior.reshape(8, 128)
    )
    x4 = lax.dynamic_slice_in_dim(x4, 2 * y, 2, 1)
    f4 = lax.dynamic_slice_in_dim(f4, 2 * y, 2, 1)
    d4 = d.reshape(4, 2, 128)
    last = at == 63
    factor = jnp.ones((2, 128), F32)
    const = jnp.where(last, f4[3], 0.0)
    for j in reversed(range(4)):
        const = x4[j] + d4[j] * (const - f4[j])
        factor = factor * d4[j]
    element = jnp.concatenate([jnp.where(last, 0.0, factor), const], 0)
    parts = lax.all_to_all(jnp.broadcast_to(element[None], (64, 4, 128)), TIME, 0, 0, tiled=True)
    smooth = pl.pallas_call(
        smooth_kernel,
        out_shape=jax.ShapeDtypeStruct((4, 2, 128), F32),
        in_specs=[SMEM] + [VMEM] * 4,
        out_specs=VMEM,
        name="smooth_own",
    )(at.reshape(1), parts, d4, x4, f4)
    return x4.reshape(4, 256), smooth.reshape(4, 256)


def solution(mesh):
    fine = Mesh(mesh.devices.reshape(8, 4, 2, 4), ALL)
    t = P(TIME, None)
    ty = P(TIME, "y")
    return jax.shard_map(
        body,
        mesh=fine,
        in_specs=(t, t, P(), P(), P(), ty, P()),
        out_specs=(ty, ty),
        check_vma=False,
    )
```

time: 717 us -> 245 us (0.34)
  waiting for transfers between devices: 333 us -> 38.6 us
  Pallas kernels: 0 us -> 170 us
  blocking collectives: 150 us -> 0 us
  matrix products: 107 us -> 0 us
  starting transfers between devices: 95.2 us -> 21.1 us
  between operations: 14.5 us -> 0.81 us
    all_gather x5 -> x0, waiting for transfers between devices: 221 us -> none  [fold_pair(): lax.all_gather(received[0], 'rows', axis=0, tiled=True)]
    pallas_call x0 -> x2, Pallas kernels: none -> 170 us  [the longest x1 168 us: run_filter(): pl.pallas_call(functools.partial(filter_kernel, steps), out_shape=(jax.Sh...]
    all_gather x9 -> x0, blocking collectives: 150 us -> none  [the longest x2 107 us: carried_in(): gathered = jax.tree.map(lambda a: lax.all_gather(a, axis), part)]
    ppermute x13 -> x0, waiting for transfers between devices: 112 us -> none  [from_behind(): lax.ppermute(value, axis, [(source, source + steps) for source in range(i...]
    dot_general x39 -> x0, matrix products: 107 us -> none  [the longest x19 39.5 us: linear_map_apply(): jnp.dot(matrix, vector, precision=precise, preferred_element_type=jnp.flo...]
    ppermute x13 -> x0, starting transfers between devices: 95 us -> none  [from_behind(): lax.ppermute(value, axis, [(source, source + steps) for source in range(i...]
    all_to_all x0 -> x2, waiting for transfers between devices: none -> 38.6 us  [the longest x1 29.3 us: body(): got = lax.all_to_all(sent, ALL, 0, 0, tiled=True)]
    all_to_all x0 -> x2, starting transfers between devices: none -> 21.1 us  [the longest x1 15.7 us: body(): got = lax.all_to_all(sent, ALL, 0, 0, tiled=True)]
  transfers between devices with their start and end apart: 18 -> 2, of which waited for: 16 -> 2; matrix products, arithmetic and copies ran while one was open for 2% -> 1% of each run, Pallas kernels for 0% -> 0%
where the time goes in v1:
time: 245 us; the launch traced here: 244 us
  Pallas kernels  170 us (69%)
  waiting for transfers between devices  38.6 us (16%)
  starting transfers between devices  21.1 us (9%)
  local copies, waits for them, and re-layouts  10.5 us (4%)
  other arithmetic  3.74 us (2%)
    pallas_call x1, Pallas kernels, run_filter(): pl.pallas_call(functools.partial(filter_kernel, steps), out_shape=(jax.Sh...  168 us
    all_to_all x1, waiting for transfers between devices, body(): got = lax.all_to_all(sent, ALL, 0, 0, tiled=True)  29.3 us
    all_to_all x1, starting transfers between devices, body(): got = lax.all_to_all(sent, ALL, 0, 0, tiled=True)  15.7 us
    all_to_all x1, waiting for transfers between devices, body(): lax.all_to_all(jnp.broadcast_to(element[None], (64, 4, 128)), TIME, 0, 0,...  9.31 us
    all_to_all x1, starting transfers between devices, body(): lax.all_to_all(jnp.broadcast_to(element[None], (64, 4, 128)), TIME, 0, 0,...  5.48 us
  transfers between devices with their start and end apart: 2, of which 2 were waited for; matrix products, arithmetic and copies ran while one was open for 1% of the time, Pallas kernels for 0%

profile of v1, /device:TPU:1, one launch (start us, length us, event | category | flops | bytes accessed | tf_op | source)
XLA Modules:
  0.0 244.4 jit_solution(2019082866717673449)
XLA Ops:
  0.6 0.0 copy-start.6
  0.6 0.0 copy-start
  0.7 0.0 copy-start.7
  0.7 0.8 convert_element_type.11
  1.5 0.8 fusion.3
  2.3 1.1 broadcast_in_dim.11
  3.3 15.7 %all-to-all-start = ((f32[256,8,128]{2,1,0:T(8,128)}), f32[256,8,128]{2,1,0:T(8,128)S(1)}, u32[]{:S(2)}, u32[]{:S(2)}) async-start(f32[256,8,128]{2,1,0:T(8,128)} %broadcast_in_dim.11), calls=%async_computation | async-start | bytes 2097152 | tf_op jit(solution)/shard_map/all_to_all | solution.py:112
  19.0 0.0 copy-done.6
  19.1 0.0 copy-done
  19.1 0.0 copy-done.7
  19.1 1.5 broadcast_multiply_fusion.hw_ref
  20.6 29.3 %all-to-all-done = f32[256,8,128]{2,1,0:T(8,128)S(1)} async-done(((f32[256,8,128]{2,1,0:T(8,128)}), f32[256,8,128]{2,1,0:T(8,128)S(1)}, u32[]{:S(2)}, u32[]{:S(2)}) %all-to-all-start) | async-done | bytes 1048608 | tf_op jit(solution)/shard_map/all_to_all | solution.py:112
  49.9 0.9 slice_bitcast_fusion
  50.8 0.0 copy-start.3
  50.8 0.5 fusion.2
  51.4 0.1 reduce_sum.14
  51.5 0.0 copy-start.1
  51.5 1.3 copy.10
  52.8 0.6 broadcast_in_dim.13.bits_ref
  53.4 0.0 copy-done.3
  53.4 0.0 copy-done.1
  53.4 0.0 copy-start.2
  53.4 2.2 copy-done.2
  55.6 167.7 %filter_all.1 = (f32[4,8,128]{2,1,0:T(8,128)S(1)}, f32[4,8,128]{2,1,0:T(8,128)S(1)}) custom-call(s32[1]{0:T(128)} %bitcast.at_ref, f32[256,4,128]{2,1,0:T(4,128)S(1)} %bitcast.79, s32[8,512,128]{2,1,0:T(8,128)S(1)} %broadcast_in_dim.13.bits_ref, f32[1024,1024]{1,0:T(8,128)S(1)} %copy-done.2, f32[512,1024]{1,0:T(8,128)S(1)} %copy-done, ...), custom_call_target="tpu_custom_call" | custom-call | tf_op jit(solution)/shard_map/filter_all/pallas_call | solution.py:79
  223.4 0.7 broadcast_in_dim.15
  224.0 5.5 %all-to-all-start.1 = ((f32[64,4,128]{2,1,0:T(4,128)}), f32[64,4,128]{2,1,0:T(4,128)S(1)}, u32[]{:S(2)}, u32[]{:S(2)}) async-start(f32[64,4,128]{2,1,0:T(4,128)} %broadcast_in_dim.15), calls=%async_computation.1 | async-start | bytes 262144 | tf_op jit(solution)/shard_map/all_to_all | solution.py:131
  229.5 0.6 reshape.52.d_ref
  230.1 0.6 constant_dynamic-slice_fusion.7
  230.7 0.0 copy-start.5
  230.7 0.6 copy.16
  231.3 9.3 %all-to-all-done.1.parts_ref = f32[64,4,128]{2,1,0:T(4,128)S(1)} async-done(((f32[64,4,128]{2,1,0:T(4,128)}), f32[64,4,128]{2,1,0:T(4,128)S(1)}, u32[]{:S(2)}, u32[]{:S(2)}) %all-to-all-start.1) | async-done | bytes 131104 | tf_op jit(solution)/shard_map/all_to_all | solution.py:131
  240.6 0.0 copy-start.4
  240.6 0.0 copy-done.5
  240.6 0.6 copy-done.4
  241.3 1.9 smooth_own.1
  243.1 1.3 copy.15
  (6 shorter events, 0.1 us)
Async XLA Ops:
  0.6 18.4 %copy-start.6 = (f32[4,256]{1,0:T(4,128)S(1)}, f32[4,256]{1,0:T(4,128)}, u32[]{:S(2)}) copy-start(f32[4,256]{1,0:T(4,128)} %param.12) | copy-start | bytes 12292
  0.6 18.4 %copy-start = (f32[512,1024]{1,0:T(8,128)S(1)}, f32[512,1024]{1,0:T(8,128)}, u32[]{:S(2)}) copy-start(f32[512,1024]{1,0:T(8,128)} %h_ref.1) | copy-start | bytes 6291460
  0.7 18.4 %copy-start.7 = (f32[512]{0:T(512)S(1)}, f32[512]{0:T(512)}, u32[]{:S(2)}) copy-start(f32[512]{0:T(512)} %param.11) | copy-start | bytes 6148
  3.3 46.6 %all-to-all-start = ((f32[256,8,128]{2,1,0:T(8,128)}), f32[256,8,128]{2,1,0:T(8,128)S(1)}, u32[]{:S(2)}, u32[]{:S(2)}) async-start(f32[256,8,128]{2,1,0:T(8,128)} %broadcast_in_dim.11), calls=%async_computation | async-start | bytes 2097152 | tf_op jit(solution)/shard_map/all_to_all | solution.py:112
  50.8 2.6 %copy-start.3 = (f32[1024]{0:T(1024)S(1)}, f32[1024]{0:T(1024)}, u32[]{:S(2)}) copy-start(f32[1024]{0:T(1024)} %param.13) | copy-start | bytes 12292
  51.5 2.0 copy-start.1
  53.4 2.2 copy-start.2
  224.0 16.6 %all-to-all-start.1 = ((f32[64,4,128]{2,1,0:T(4,128)}), f32[64,4,128]{2,1,0:T(4,128)S(1)}, u32[]{:S(2)}, u32[]{:S(2)}) async-start(f32[64,4,128]{2,1,0:T(4,128)} %broadcast_in_dim.15), calls=%async_computation.1 | async-start | bytes 262144 | tf_op jit(solution)/shard_map/all_to_all | solution.py:131
  230.7 9.9 %copy-start.5 = (f32[4,2,128]{2,1,0:T(2,128)}, f32[4,2,128]{2,1,0:T(2,128)S(1)}, u32[]{:S(2)}) copy-start(f32[4,2,128]{2,1,0:T(2,128)S(1)} %get-tuple-element.13.x_ref) | copy-start | bytes 12292
  240.6 0.6 copy-start.4

commit v2 on v1

v2 whole, which is shorter than its diff:
```python
import functools

import jax
import jax.numpy as jnp
from jax import lax
from jax.experimental import pallas as pl
from jax.experimental.pallas import tpu as pltpu
from jax.sharding import Mesh, PartitionSpec as P

F32 = jnp.float32
HALF = ("l", "x", "c", "y")
PLANE = ("x", "c", "y")
TIME = ("h", "l", "x", "c")
BF16 = jnp.bfloat16
VMEM = pl.BlockSpec(memory_space=pltpu.VMEM)
SMEM = pl.BlockSpec(memory_space=pltpu.SMEM)


def wide(row):
    return jnp.broadcast_to(row, (8, 128))


def tree(terms):
    while len(terms) > 1:
        terms = [a + b for a, b in zip(terms[::2], terms[1::2])]
    return terms[0]


def column_sums(blocks):
    return jnp.concatenate([jnp.sum(b, axis=0, keepdims=True) for b in blocks], 0)


def propagate(f_ref, x, diff):
    xs = [wide(x[t : t + 1]) for t in range(8)]
    out = []
    for t in range(8):
        spread = None
        for b in range(16):
            i = 8 * (16 * t + b)
            s = tree([f_ref[i : i + 8, 128 * u : 128 * u + 128] * xs[u] for u in range(8)])
            s = wide(jnp.sum(s, axis=1, keepdims=True))
            spread = jnp.where(diff == 8 * b, s, 0.0 if spread is None else spread)
        out.append(spread)
    return column_sums(out)


def update(h_ref, hw_ref, bits_ref, bit, z, p, diff):
    ps = [wide(p[t : t + 1]) for t in range(8)]
    zs = [wide(z[q : q + 1]) for q in range(4)]
    acc = [jnp.zeros((8, 128), F32) for _ in range(8)]
    for i in range(64):
        r = slice(8 * i, 8 * i + 8)
        s = tree([h_ref[r, 128 * t : 128 * t + 128] * ps[t] for t in range(8)])
        s = jnp.where(diff == 8 * (i % 16), zs[i // 16], 0.0) - s
        s = wide(jnp.sum(s, axis=1, keepdims=True))
        v = jnp.where((bits_ref[r, :] & bit) != 0, s, 0.0)
        acc = [acc[t] + hw_ref[r, 128 * t : 128 * t + 128] * v for t in range(8)]
    return p + column_sums(acc)


def spread_index():
    return lax.broadcasted_iota(jnp.int32, (8, 128), 1) - lax.broadcasted_iota(jnp.int32, (8, 128), 0)


def halves(x):
    hi = x.astype(BF16)
    return hi, (x - hi.astype(F32)).astype(BF16)


def product(x, hi_ref, lo_ref):
    n = x.shape[0]
    hi, lo = halves(x)
    both = jnp.dot(jnp.concatenate([hi, lo], 0), hi_ref[...], preferred_element_type=F32)
    return both[:n] + both[n:] + jnp.dot(hi, lo_ref[...], preferred_element_type=F32)


def on_rows(words, i, diff):
    q = i // 16
    return wide(jnp.sum(jnp.where(diff == 8 * (i % 16), wide(words[q : q + 1]), 0.0), axis=1, keepdims=True))


def store_bits(bits_ref, words, diff):
    for i in range(64):
        bits_ref[8 * i : 8 * i + 8, :] = on_rows(words, i, diff).astype(jnp.int32)


def store_weighted(hw_ref, h_ref, weight, diff):
    for i in range(64):
        r = slice(8 * i, 8 * i + 8)
        w = on_rows(weight, i, diff)
        for t in range(8):
            c = slice(128 * t, 128 * t + 128)
            hw_ref[r, c] = h_ref[r, c] * w


def prepare_kernel(f_ref, h_ref, gp_hi, gp_lo, gy_hi, gy_lo, h_hi, h_lo, diag_ref, t_hi, t_lo):
    h_hi[...], h_lo[...] = halves(h_ref[...])
    for j in range(8):
        r = slice(128 * j, 128 * j + 128)
        t_hi[r, :], t_lo[r, :] = halves(jnp.transpose(h_ref[:, r]))
    for j in range(4):
        r = slice(256 * j, 256 * j + 256)
        ft = jnp.transpose(f_ref[:, r])
        on = lax.broadcasted_iota(jnp.int32, ft.shape, 0) + 256 * j == lax.broadcasted_iota(jnp.int32, ft.shape, 1)
        gy_hi[r, :], gy_lo[r, :] = halves(product(ft, t_hi, t_lo))
        gp_hi[r, :], gp_lo[r, :] = halves(jnp.where(on, 0.0, ft))
        diag_ref[:, r] = jnp.sum(jnp.where(on, ft, 0.0), axis=0, keepdims=True)[:, r]


def prepare(f, h):
    return pl.pallas_call(
        prepare_kernel,
        out_shape=(
            jax.ShapeDtypeStruct((1024, 1024), BF16),
            jax.ShapeDtypeStruct((1024, 1024), BF16),
            jax.ShapeDtypeStruct((1024, 512), BF16),
            jax.ShapeDtypeStruct((1024, 512), BF16),
            jax.ShapeDtypeStruct((512, 1024), BF16),
            jax.ShapeDtypeStruct((512, 1024), BF16),
            jax.ShapeDtypeStruct((1, 1024), F32),
        ),
        in_specs=[VMEM] * 2,
        out_specs=(VMEM,) * 7,
        scratch_shapes=[pltpu.VMEM((1024, 512), BF16), pltpu.VMEM((1024, 512), BF16)],
        compiler_params=pltpu.CompilerParams(vmem_limit_bytes=32 * 2**20),
        cost_estimate=pl.CostEstimate(flops=3 * 2**30, bytes_accessed=14 * 2**20, transcendentals=0),
        name="prepare",
    )(f, h)


def flat(rows):
    return jnp.concatenate([rows[q : q + 1] for q in range(4)], 1)


def block_kernel(
    at_ref, got0, got1, got2, got3, f_ref, h_ref, s_ref, weight_ref, gp_hi, gp_lo, gy_hi, gy_lo, h_hi, h_lo, diag_ref,
    x_own, x_end, maps, map_ends, state, bits_ref, hw_ref, got_ref,
):
    second, own, plane, place = at_ref[0], at_ref[1], at_ref[2], at_ref[3]
    for n, part in enumerate((got0, got1, got2, got3)):
        got_ref[pl.ds(32 * ((plane + 4 - n) % 4), 32)] = part[...]

    @pl.when(second == 0)
    def _():
        diff = spread_index()
        maps[...] = jnp.zeros_like(maps)
        map_ends[...] = jnp.zeros_like(map_ends)
        store_weighted(hw_ref, h_ref, weight_ref[...], diff)

        def group(g, x):
            words = sum(got_ref[16 * g + j][4:8] * float(2**j) for j in range(16))
            store_bits(bits_ref, words, diff)

            def step(j, x):
                k = 16 * g + j

                @pl.when(k == own)
                def _():
                    x_own[...] = x

                p = propagate(f_ref, x, diff)
                return update(h_ref, hw_ref, bits_ref, jnp.int32(1) << j, got_ref[k][0:4], p, diff)

            return lax.fori_loop(0, 16, step, x)

        x_end[...] = lax.fori_loop(0, 8, group, s_ref[...])

    @pl.when(second == 1)
    def _():
        x_own[...] = jnp.zeros_like(x_own)
        x_end[...] = jnp.zeros_like(x_end)
        unit = (
            lax.broadcasted_iota(jnp.int32, (32, 1024), 1)
            == lax.broadcasted_iota(jnp.int32, (32, 1024), 0) + 32 * place
        ).astype(F32)
        state[0:32, :] = unit
        state[32:64, :] = unit
        state[64:72, :] = jnp.zeros((8, 1024), F32)
        row = lax.broadcasted_iota(jnp.int32, (8, 512), 0)
        weight = flat(weight_ref[...])

        def step(k, carry):
            @pl.when(jnp.logical_and(k // 32 == plane % 2, k % 4 == 0))
            def _():
                q = (k % 32) // 4
                early = plane < 2
                maps[q, 0:32, :] = jnp.where(early, state[0:32, :], state[32:64, :])
                maps[q, 32:40, :] = jnp.where(early, state[64:72, :], pltpu.roll(state[64:72, :], 7, 0))

            x = state[...]
            y = product(x, gy_hi, gy_lo)
            p = product(x, gp_hi, gp_lo) + x * diag_ref[...]
            a, b = got_ref[k], got_ref[64 + k]
            wa, wb = flat(a[4:8]) * weight, flat(b[4:8]) * weight
            zs = jnp.where(row == 0, flat(a[0:4]), jnp.where(row == 1, flat(b[0:4]), 0.0))
            v = jnp.concatenate(
                [
                    -wa * y[0:32],
                    -wb * y[32:64],
                    jnp.where(row == 0, wa, wb) * (zs - y[64:72]),
                ],
                0,
            )
            state[...] = p + product(v, h_hi, h_lo)
            return carry

        lax.fori_loop(0, 64, step, 0)
        map_ends[0:32, :] = state[0:32, :]
        map_ends[32:40, :] = state[64:72, :]


def run_blocks(*args):
    return pl.pallas_call(
        block_kernel,
        out_shape=(
            jax.ShapeDtypeStruct((8, 128), F32),
            jax.ShapeDtypeStruct((8, 128), F32),
            jax.ShapeDtypeStruct((8, 40, 1024), F32),
            jax.ShapeDtypeStruct((40, 1024), F32),
        ),
        in_specs=[SMEM] + [VMEM] * 15,
        out_specs=(VMEM,) * 4,
        scratch_shapes=[pltpu.VMEM((72, 1024), F32), pltpu.VMEM((512, 128), jnp.int32), pltpu.VMEM((512, 1024), F32), pltpu.VMEM((128, 8, 128), F32)],
        compiler_params=pltpu.CompilerParams(vmem_limit_bytes=28 * 2**20),
        name="blocks",
    )(*args)


def own_kernel(z_ref, m_ref, f_ref, h_ref, weight_ref, s_ref, x_out, f_out, bits_ref, hw_ref):
    diff = spread_index()
    store_weighted(hw_ref, h_ref, weight_ref[...], diff)
    store_bits(bits_ref, sum(m_ref[j] * float(2**j) for j in range(4)), diff)

    def step(k, x):
        p = propagate(f_ref, x, diff)

        @pl.when(k > 0)
        def _():
            f_out[k - 1] = p

        x = update(h_ref, hw_ref, bits_ref, jnp.int32(1) << k, z_ref[k], p, diff)
        x_out[k] = x
        return x

    x = lax.fori_loop(0, 4, step, s_ref[...])
    f_out[3] = propagate(f_ref, x, diff)


def run_own(*args):
    return pl.pallas_call(
        own_kernel,
        out_shape=(jax.ShapeDtypeStruct((4, 8, 128), F32),) * 2,
        in_specs=[VMEM] * 6,
        out_specs=(VMEM, VMEM),
        scratch_shapes=[pltpu.VMEM((512, 128), jnp.int32), pltpu.VMEM((512, 1024), F32)],
        compiler_params=pltpu.CompilerParams(vmem_limit_bytes=16 * 2**20),
        name="own_steps",
    )(*args)


def smooth_kernel(at_ref, parts_ref, d_ref, x_ref, f_ref, out_ref):
    at = at_ref[0]
    later = f_ref[3]
    count = parts_ref.shape[0]

    def one(i, later):
        j = count - 1 - i
        e = parts_ref[j]
        return jnp.where(j > at, e[0:2] * later + e[2:4], later)

    later = lax.fori_loop(0, count, one, later)
    for j in reversed(range(4)):
        later = x_ref[j] + d_ref[j] * (later - f_ref[j])
        out_ref[j] = later


def body(z, mask, f, h, weight, d, prior):
    h_at, l_at = lax.axis_index("h"), lax.axis_index("l")
    at = lax.axis_index(TIME)
    place = lax.axis_index(PLANE)
    y = lax.axis_index("y")
    z = z.reshape(4, 4, 128)
    mask = mask.astype(F32).reshape(4, 4, 128)
    own = lax.dynamic_index_in_dim(jnp.concatenate([z, mask], 1), y, 0, True)
    flat_plane = lax.all_to_all(jnp.broadcast_to(own, (32, 8, 128)), PLANE, 0, 0, tiled=True)
    turned = [flat_plane] + [lax.ppermute(flat_plane, "l", [(i, (i + n) % 4) for i in range(4)]) for n in (1, 2, 3)]
    gp_hi, gp_lo, gy_hi, gy_lo, h_hi, h_lo, diag = prepare(f, h)
    weight = weight.reshape(4, 128)
    flags = jnp.stack([h_at, 4 * (at % 32), l_at, place]).astype(jnp.int32)
    x_own, x_end, maps, ends = run_blocks(
        flags, *turned, f, h, prior.reshape(8, 128), weight, gp_hi, gp_lo, gy_hi, gy_lo, h_hi, h_lo, diag
    )
    first = place == 0
    s1 = lax.ppermute(x_end, "h", [(0, 1)]).reshape(32, 32)
    mine = lax.dynamic_index_in_dim(s1, place, 0, False)
    part = jnp.sum(mine[:, None] * ends[:32], 0) + jnp.where(first, ends[32], 0.0)
    s2 = lax.all_to_all(part.reshape(32, 32), PLANE, 0, 0, tiled=True).sum(0)
    mine = jnp.where(l_at < 2, mine, s2)
    parts = jnp.sum(mine[None, :, None] * maps[:, :32], 1) + jnp.where(first, maps[:, 32], 0.0)
    parts = jnp.broadcast_to(parts[:, None], (8, 4, 1024)).reshape(32, 1024)
    begin = lax.all_to_all(parts, PLANE, 0, 0, tiled=True).sum(0).reshape(8, 128)
    begin = jnp.where(h_at == 0, x_own, begin)
    x4, f4 = run_own(z, mask, f, h, weight, begin)
    x4 = lax.dynamic_slice_in_dim(x4, 2 * y, 2, 1)
    f4 = lax.dynamic_slice_in_dim(f4, 2 * y, 2, 1)
    d4 = d.reshape(4, 2, 128)
    last = at == 63
    factor = jnp.ones((2, 128), F32)
    const = jnp.where(last, f4[3], 0.0)
    for j in reversed(range(4)):
        const = x4[j] + d4[j] * (const - f4[j])
        factor = factor * d4[j]
    element = jnp.concatenate([jnp.where(last, 0.0, factor), const], 0)
    parts = lax.all_to_all(jnp.broadcast_to(element[None], (64, 4, 128)), TIME, 0, 0, tiled=True)
    smooth = pl.pallas_call(
        smooth_kernel,
        out_shape=jax.ShapeDtypeStruct((4, 2, 128), F32),
        in_specs=[SMEM] + [VMEM] * 4,
        out_specs=VMEM,
        name="smooth_own",
    )(at.reshape(1), parts, d4, x4, f4)
    return x4.reshape(4, 256), smooth.reshape(4, 256)


def solution(mesh):
    fine = Mesh(mesh.devices.reshape(2, 4, 4, 2, 4), TIME + ("y",))
    t = P(TIME, None)
    ty = P(TIME, "y")
    return jax.shard_map(
        body,
        mesh=fine,
        in_specs=(t, t, P(), P(), P(), ty, P()),
        out_specs=(ty, ty),
        check_vma=False,
    )
```

time: 245 us -> 219 us (0.89)
  Pallas kernels: 170 us -> 96.5 us
  starting transfers between devices: 21.1 us -> 43.4 us
  local copies, waits for them, and re-layouts: 10.5 us -> 31.2 us
  blocking collectives: 0 us -> 16 us
  waiting for transfers between devices: 38.6 us -> 24.7 us
    pallas_call x1 -> x3, Pallas kernels: 168 us -> 94.6 us  [the longest x1 87 us: run_blocks(): pl.pallas_call(block_kernel, out_shape=(jax.ShapeDtypeStruct((8, 128), F3...]
    ppermute x0 -> x4, starting transfers between devices: none -> 24.4 us  [the longest x1 19.1 us: body(): s1 = lax.ppermute(x_end, 'h', [(0, 1)]).reshape(32, 32)]
    unnamed x18 -> x57, local copies, waits for them, and re-layouts: 4.71 us -> 27.5 us
    all_to_all x0 -> x1, blocking collectives: none -> 16 us  [body(): lax.all_to_all(jnp.broadcast_to(own, (32, 8, 128)), PLANE, 0, 0, tiled=True)]
    all_to_all x1 -> x2, waiting for transfers between devices: 29.3 us -> 14.6 us  [the longest x1 7.64 us: body(): lax.all_to_all(parts, PLANE, 0, 0, tiled=True).sum(0).reshape(8, 128)]
    all_to_all x1 -> x2, starting transfers between devices: 15.7 us -> 9.76 us  [the longest x1 5.73 us: body(): s2 = lax.all_to_all(part.reshape(32, 32), PLANE, 0, 0, tiled=True).sum(0)]
    all_to_all x1, starting transfers between devices: 5.48 us -> 9.21 us  [body(): lax.all_to_all(jnp.broadcast_to(element[None], (64, 4, 128)), TIME, 0, 0,...]
  transfers between devices with their start and end apart: 2 -> 7, of which waited for: 2 -> 4; matrix products, arithmetic and copies ran while one was open for 1% -> 1% of each run, Pallas kernels for 0% -> 2%
where the time goes in v2:
time: 219 us; the launch traced here: 218 us
  Pallas kernels  96.5 us (44%)
  starting transfers between devices  43.4 us (20%)
  local copies, waits for them, and re-layouts  31.2 us (14%)
  waiting for transfers between devices  24.7 us (11%)
  blocking collectives  16 us (7%)
  other arithmetic  5.04 us (2%)
    pallas_call x1, Pallas kernels, run_blocks(): pl.pallas_call(block_kernel, out_shape=(jax.ShapeDtypeStruct((8, 128), F3...  87 us
    unnamed x57, local copies, waits for them, and re-layouts  27.5 us
    ppermute x1, starting transfers between devices, body(): s1 = lax.ppermute(x_end, 'h', [(0, 1)]).reshape(32, 32)  19.1 us
    all_to_all x1, blocking collectives, body(): lax.all_to_all(jnp.broadcast_to(own, (32, 8, 128)), PLANE, 0, 0, tiled=True)  16 us
    all_to_all x1, waiting for transfers between devices, body(): lax.all_to_all(jnp.broadcast_to(element[None], (64, 4, 128)), TIME, 0, 0,...  9.32 us
    all_to_all x1, starting transfers between devices, body(): lax.all_to_all(jnp.broadcast_to(element[None], (64, 4, 128)), TIME, 0, 0,...  9.21 us
    all_to_all x1, waiting for transfers between devices, body(): lax.all_to_all(parts, PLANE, 0, 0, tiled=True).sum(0).reshape(8, 128)  7.64 us
    all_to_all x1, waiting for transfers between devices, body(): s2 = lax.all_to_all(part.reshape(32, 32), PLANE, 0, 0, tiled=True).sum(0)  6.92 us
  transfers between devices with their start and end apart: 7, of which 4 were waited for; matrix products, arithmetic and copies ran while one was open for 1% of the time, Pallas kernels for 2%

profile of v2, /device:TPU:1, one launch (start us, length us, event | category | flops | bytes accessed | tf_op | source)
XLA Modules:
  0.0 217.7 jit_solution(10779878554697606463)
XLA Ops:
  0.6 0.7 convert_element_type.3
  1.4 0.7 reshape.85.z_ref
  2.1 16.0 %all_to_all.25.got0 = f32[32,8,128]{2,1,0:T(8,128)S(1)} all-to-all(f32[32,8,128]{2,1,0:T(8,128)S(1)} %broadcast_in_dim.38), channel_id=1, replica_groups=mesh['h'=2,'l'=4,'x'=4,'c'=2,'y'=4] {'x','c','y'}, dimensions={0} | all-to-all | bytes 262144 | tf_op jit(solution)/shard_map/all_to_all | solution.py:285
  18.1 1.6 collective-permute-start
  19.7 3.0 %collective-permute-start.1 = (f32[32,8,128]{2,1,0:T(8,128)S(1)}, f32[32,8,128]{2,1,0:T(8,128)S(1)}, u32[]{:S(2)}, u32[]{:S(2)}) collective-permute-start(f32[32,8,128]{2,1,0:T(8,128)S(1)} %all_to_all.25.got0), channel_id=1, source_target_pairs={{0,64},{32,96},{64,0},{96,32},{1,65},{33,97},{65,1},{97,33},{2,66}... | collective-permute-start | bytes 393224 | tf_op jit(solution)/shard_map/ppermute | solution.py:286
  22.7 0.7 collective-permute-start.2
  23.4 2.2 %copy-done = f32[1024,1024]{1,0:T(8,128)S(1)} copy-done((f32[1024,1024]{1,0:T(8,128)S(1)}, f32[1024,1024]{1,0:T(8,128)}, u32[]{:S(2)}) %copy-start) | copy-done | bytes 4194328
  25.6 1.6 copy-done.3
  27.2 4.4 %prepare.1 = (bf16[1024,1024]{1,0:T(8,128)(2,1)S(1)}, bf16[1024,1024]{1,0:T(8,128)(2,1)S(1)}, bf16[1024,512]{1,0:T(8,128)(2,1)S(1)}, bf16[1024,512]{1,0:T(8,128)...) custom-call(f32[1024,1024]{1,0:T(8,128)S(1)} %copy-done, ...), custom_call_target="tpu_custom_call" | custom-call | flops 3221225472 | bytes 14680064 | tf_op jit(solution)/shard_map/prepare/pallas_call | solution.py:111
  31.6 1.3 copy-done.5
  32.9 1.3 copy-done.7
  34.2 1.0 copy-done.9
  35.2 1.0 copy-done.11
  36.2 1.0 copy-done.13
  37.2 0.6 copy-done.20
  37.9 2.2 %copy-done.1 = f32[1024,1024]{1,0:T(8,128)S(1)} copy-done((f32[1024,1024]{1,0:T(8,128)S(1)}, f32[1024,1024]{1,0:T(8,128)}, u32[]{:S(2)}) %copy-start.1) | copy-done | bytes 4194328
  40.0 1.6 copy-done.6
  41.6 1.6 copy-done.8
  43.2 1.2 copy-done.10
  44.5 1.2 copy-done.12
  45.7 1.2 copy-done.14
  46.9 0.7 copy-done.17
  47.6 0.7 copy-done.19
  48.3 0.7 copy-done.21
  49.0 87.0 %blocks.1 = (f32[8,128]{1,0:T(8,128)S(1)}, f32[8,128]{1,0:T(8,128)}, f32[8,40,1024]{2,1,0:T(8,128)S(1)}, f32[40,1024]{1,0:T(8,128)S(1)}) custom-call(s32[4]{0:T(128)S(1)} %pad_add_fusion.at_ref, f32[32,8,128]{2,1,0:T(8,128)S(1)} %all_to_all.25.got0, f32[32,8,128]{2,1,0:T(8,128)S(1)} %collective-permute-done.got1, ...), custom_call_target="tpu_custom_call" | custom-call | tf_op jit(solution)/shard_map/blocks/pallas_call | solution.py:213
  136.0 1.1 copy-done.15
  137.7 19.1 %collective-permute-start.3 = (f32[8,128]{1,0:T(8,128)}, f32[8,128]{1,0:T(8,128)S(1)}, u32[]{:S(2)}, u32[]{:S(2)}) collective-permute-start(f32[8,128]{1,0:T(8,128)} %get-tuple-element.23), channel_id=1, source_target_pairs={{0,128},{1,129},{2,130},{3,131},{4,132},{5,133},{6,134},{7,135},{8... | collective-permute-start | bytes 12296 | tf_op jit(solution)/shard_map/ppermute | solution.py:294
  156.8 0.8 collective-permute-done.3
  157.8 1.0 multiply_reduce_fusion.1
  158.9 0.6 add.66
  159.5 5.7 %all-to-all-start.1 = ((f32[32,1,32]{2,1,0:T(1,128)}), f32[32,1,32]{2,1,0:T(1,128)S(1)}, u32[]{:S(2)}, u32[]{:S(2)}) async-start(f32[32,1,32]{2,1,0:T(1,128)} %add.66), calls=%async_computation.1 | async-start | bytes 32768 | tf_op jit(solution)/shard_map/all_to_all | solution.py:297
  165.2 6.9 %all-to-all-done.1 = f32[32,1,32]{2,1,0:T(1,128)S(1)} async-done(((f32[32,1,32]{2,1,0:T(1,128)}), f32[32,1,32]{2,1,0:T(1,128)S(1)}, u32[]{:S(2)}, u32[]{:S(2)}) %all-to-all-start.1) | async-done | bytes 4128 | tf_op jit(solution)/shard_map/all_to_all | solution.py:297
  172.2 1.4 multiply_reduce_fusion
  173.7 1.0 fusion
  174.7 0.8 all_to_all.18
  175.5 4.0 %all-to-all-start.2 = ((f32[32,1,1024]{2,1,0:T(1,128)}), f32[32,1,1024]{2,1,0:T(1,128)S(1)}, u32[]{:S(2)}, u32[]{:S(2)}) async-start(f32[32,1,1024]{2,1,0:T(1,128)} %all_to_all.18), calls=%async_computation.2 | async-start | bytes 262144 | tf_op jit(solution)/shard_map/all_to_all | solution.py:301
  179.6 7.6 %all-to-all-done.2 = f32[32,1,1024]{2,1,0:T(1,128)S(1)} async-done(((f32[32,1,1024]{2,1,0:T(1,128)}), f32[32,1,1024]{2,1,0:T(1,128)S(1)}, u32[]{:S(2)}, u32[]{:S(2)}) %all-to-all-start.2) | async-done | bytes 131104 | tf_op jit(solution)/shard_map/all_to_all | solution.py:301
  187.4 2.2 %copy-done.2 = f32[1024,1024]{1,0:T(8,128)S(1)} copy-done((f32[1024,1024]{1,0:T(8,128)S(1)}, f32[1024,1024]{1,0:T(8,128)}, u32[]{:S(2)}) %copy-start.2) | copy-done | bytes 4194328
  189.6 3.3 %own_steps.1 = (f32[4,8,128]{2,1,0:T(8,128)S(1)}, f32[4,8,128]{2,1,0:T(8,128)S(1)}) custom-call(f32[4,4,128]{2,1,0:T(4,128)S(1)} %reshape.85.z_ref, f32[4,4,128]{2,1,0:T(4,128)S(1)} %reshape.86.m_ref, f32[1024,1024]{1,0:T(8,128)S(1)} %copy-done.2, f32[512,1024]{1,0:T(8,128)S(1)} %copy-done.4, f32[4,128]{1,0:T(4,128)S(1)} %bitcast.82, ...), custom_call_target="tpu_custom_call" | custom-call | tf_op jit(solution)/shard_map/own_steps/pallas_call | solution.py:250
  192.9 0.7 broadcast_in_dim.44
  193.5 9.2 %all-to-all-start.3 = ((f32[64,4,128]{2,1,0:T(4,128)}), f32[64,4,128]{2,1,0:T(4,128)S(1)}, u32[]{:S(2)}, u32[]{:S(2)}) async-start(f32[64,4,128]{2,1,0:T(4,128)} %broadcast_in_dim.44), calls=%async_computation.3 | async-start | bytes 262144 | tf_op jit(solution)/shard_map/all_to_all | solution.py:314
  202.8 0.6 reshape.93.d_ref
  203.4 0.6 constant_dynamic-slice_fusion.7
  204.0 0.6 copy.18
  204.6 9.3 %all-to-all-done.3.parts_ref = f32[64,4,128]{2,1,0:T(4,128)S(1)} async-done(((f32[64,4,128]{2,1,0:T(4,128)}), f32[64,4,128]{2,1,0:T(4,128)S(1)}, u32[]{:S(2)}, u32[]{:S(2)}) %all-to-all-start.3) | async-done | bytes 131104 | tf_op jit(solution)/shard_map/all_to_all | solution.py:314
  213.9 0.7 copy-done.24
  214.5 1.9 smooth_own.1
  216.4 1.3 copy.17
  (55 shorter events, 1.3 us)
Async XLA Ops:
  18.1 19.8 %collective-permute-start = (f32[32,8,128]{2,1,0:T(8,128)S(1)}, f32[32,8,128]{2,1,0:T(8,128)S(1)}, u32[]{:S(2)}, u32[]{:S(2)}) collective-permute-start(f32[32,8,128]{2,1,0:T(8,128)S(1)} %all_to_all.25.got0), channel_id=1, source_target_pairs={{0,32},{32,64},{64,96},{96,0},{1,33},{33,65},{65,97},{97,1},{2,34}... | collective-permute-start | bytes 393224 | tf_op jit(solution)/shard_map/ppermute | solution.py:286
  19.7 18.1 %collective-permute-start.1 = (f32[32,8,128]{2,1,0:T(8,128)S(1)}, f32[32,8,128]{2,1,0:T(8,128)S(1)}, u32[]{:S(2)}, u32[]{:S(2)}) collective-permute-start(f32[32,8,128]{2,1,0:T(8,128)S(1)} %all_to_all.25.got0), channel_id=1, source_target_pairs={{0,64},{32,96},{64,0},{96,32},{1,65},{33,97},{65,1},{97,33},{2,66}... | collective-permute-start | bytes 393224 | tf_op jit(solution)/shard_map/ppermute | solution.py:286
  22.7 15.2 %collective-permute-start.2 = (f32[32,8,128]{2,1,0:T(8,128)S(1)}, f32[32,8,128]{2,1,0:T(8,128)}, u32[]{:S(2)}, u32[]{:S(2)}) collective-permute-start(f32[32,8,128]{2,1,0:T(8,128)S(1)} %all_to_all.25.got0), channel_id=1, source_target_pairs={{0,96},{32,0},{64,32},{96,64},{1,97},{33,1},{65,33},{97,65},{2,98}... | collective-permute-start | bytes 393224 | tf_op jit(solution)/shard_map/ppermute | solution.py:286
  23.4 2.2 %copy-start = (f32[1024,1024]{1,0:T(8,128)S(1)}, f32[1024,1024]{1,0:T(8,128)}, u32[]{:S(2)}) copy-start(f32[1024,1024]{1,0:T(8,128)} %f_ref.5) | copy-start | bytes 12582916
  25.6 1.6 copy-start.3
  27.2 10.7 %copy-start.4 = (f32[512,1024]{1,0:T(8,128)S(1)}, f32[512,1024]{1,0:T(8,128)}, u32[]{:S(2)}) copy-start(f32[512,1024]{1,0:T(8,128)} %h_ref.5) | copy-start | bytes 6291460
  31.6 1.3 copy-start.5
  32.9 1.3 copy-start.7
  34.2 1.0 copy-start.9
  35.2 1.0 copy-start.11
  36.2 1.0 copy-start.13
  37.2 0.6 copy-start.20
  37.9 2.2 %copy-start.1 = (f32[1024,1024]{1,0:T(8,128)S(1)}, f32[1024,1024]{1,0:T(8,128)}, u32[]{:S(2)}) copy-start(f32[1024,1024]{1,0:T(8,128)} %f_ref.5) | copy-start | bytes 12582916
  40.0 1.6 copy-start.6
  41.6 1.6 copy-start.8
  43.2 1.2 copy-start.10
  44.5 1.2 copy-start.12
  45.7 1.2 copy-start.14
  46.9 0.7 copy-start.17
  47.6 0.7 copy-start.19
  48.3 0.7 copy-start.21
  136.0 1.1 copy-start.15
  137.1 0.6 copy-start.22
  137.7 19.1 %copy-start.16 = (f32[40,1024]{1,0:T(8,128)}, f32[40,1024]{1,0:T(8,128)S(1)}, u32[]{:S(2)}) copy-start(f32[40,1024]{1,0:T(8,128)S(1)} %get-tuple-element.24) | copy-start | bytes 491524
  137.7 41.9 %copy-start.26 = (f32[4,256]{1,0:T(4,128)S(1)}, f32[4,256]{1,0:T(4,128)}, u32[]{:S(2)}) copy-start(f32[4,256]{1,0:T(4,128)} %param.12) | copy-start | bytes 12292
  137.7 49.7 %copy-start.18 = (f32[512]{0:T(512)S(1)}, f32[512]{0:T(512)}, u32[]{:S(2)}) copy-start(f32[512]{0:T(512)} %param.11) | copy-start | bytes 6148
  137.7 49.7 %copy-start.23 = (f32[8,128]{1,0:T(8,128)S(1)}, f32[8,128]{1,0:T(8,128)}, u32[]{:S(2)}) copy-start(f32[8,128]{1,0:T(8,128)} %copy-done.22) | copy-start | bytes 12292
  137.7 20.0 %collective-permute-start.3 = (f32[8,128]{1,0:T(8,128)}, f32[8,128]{1,0:T(8,128)S(1)}, u32[]{:S(2)}, u32[]{:S(2)}) collective-permute-start(f32[8,128]{1,0:T(8,128)} %get-tuple-element.23), channel_id=1, source_target_pairs={{0,128},{1,129},{2,130},{3,131},{4,132},{5,133},{6,134},{7,135},{8... | collective-permute-start | bytes 12296 | tf_op jit(solution)/shard_map/ppermute | solution.py:294
  159.5 12.7 %all-to-all-start.1 = ((f32[32,1,32]{2,1,0:T(1,128)}), f32[32,1,32]{2,1,0:T(1,128)S(1)}, u32[]{:S(2)}, u32[]{:S(2)}) async-start(f32[32,1,32]{2,1,0:T(1,128)} %add.66), calls=%async_computation.1 | async-start | bytes 32768 | tf_op jit(solution)/shard_map/all_to_all | solution.py:297
  175.5 11.7 %all-to-all-start.2 = ((f32[32,1,1024]{2,1,0:T(1,128)}), f32[32,1,1024]{2,1,0:T(1,128)S(1)}, u32[]{:S(2)}, u32[]{:S(2)}) async-start(f32[32,1,1024]{2,1,0:T(1,128)} %all_to_all.18), calls=%async_computation.2 | async-start | bytes 262144 | tf_op jit(solution)/shard_map/all_to_all | solution.py:301
  187.4 2.2 %copy-start.2 = (f32[1024,1024]{1,0:T(8,128)S(1)}, f32[1024,1024]{1,0:T(8,128)}, u32[]{:S(2)}) copy-start(f32[1024,1024]{1,0:T(8,128)} %f_ref.5) | copy-start | bytes 12582916
  193.5 20.3 %all-to-all-start.3 = ((f32[64,4,128]{2,1,0:T(4,128)}), f32[64,4,128]{2,1,0:T(4,128)S(1)}, u32[]{:S(2)}, u32[]{:S(2)}) async-start(f32[64,4,128]{2,1,0:T(4,128)} %broadcast_in_dim.44), calls=%async_computation.3 | async-start | bytes 262144 | tf_op jit(solution)/shard_map/all_to_all | solution.py:314
  204.0 9.9 %copy-start.25 = (f32[4,2,128]{2,1,0:T(2,128)}, f32[4,2,128]{2,1,0:T(2,128)S(1)}, u32[]{:S(2)}) copy-start(f32[4,2,128]{2,1,0:T(2,128)S(1)} %get-tuple-element.35.x_ref) | copy-start | bytes 12292
  213.9 0.7 copy-start.24

commit v3 on v2

--- a/solution.py
+++ b/solution.py
@@ -93,7 +93,7 @@
             hw_ref[r, c] = h_ref[r, c] * w
 
 
-def prepare_kernel(f_ref, h_ref, gp_hi, gp_lo, gy_hi, gy_lo, h_hi, h_lo, diag_ref, t_hi, t_lo):
+def prepare(f_ref, h_ref, gp_hi, gp_lo, gy_hi, gy_lo, h_hi, h_lo, diag_ref, t_hi, t_lo):
     h_hi[...], h_lo[...] = halves(h_ref[...])
     for j in range(8):
         r = slice(128 * j, 128 * j + 128)
@@ -101,40 +101,21 @@
     for j in range(4):
         r = slice(256 * j, 256 * j + 256)
         ft = jnp.transpose(f_ref[:, r])
-        on = lax.broadcasted_iota(jnp.int32, ft.shape, 0) + 256 * j == lax.broadcasted_iota(jnp.int32, ft.shape, 1)
+        row = lax.broadcasted_iota(jnp.int32, ft.shape, 0) + 256 * j
+        on = row == lax.broadcasted_iota(jnp.int32, ft.shape, 1)
         gy_hi[r, :], gy_lo[r, :] = halves(product(ft, t_hi, t_lo))
         gp_hi[r, :], gp_lo[r, :] = halves(jnp.where(on, 0.0, ft))
         diag_ref[:, r] = jnp.sum(jnp.where(on, ft, 0.0), axis=0, keepdims=True)[:, r]
 
 
-def prepare(f, h):
-    return pl.pallas_call(
-        prepare_kernel,
-        out_shape=(
-            jax.ShapeDtypeStruct((1024, 1024), BF16),
-            jax.ShapeDtypeStruct((1024, 1024), BF16),
-            jax.ShapeDtypeStruct((1024, 512), BF16),
-            jax.ShapeDtypeStruct((1024, 512), BF16),
-            jax.ShapeDtypeStruct((512, 1024), BF16),
-            jax.ShapeDtypeStruct((512, 1024), BF16),
-            jax.ShapeDtypeStruct((1, 1024), F32),
-        ),
-        in_specs=[VMEM] * 2,
-        out_specs=(VMEM,) * 7,
-        scratch_shapes=[pltpu.VMEM((1024, 512), BF16), pltpu.VMEM((1024, 512), BF16)],
-        compiler_params=pltpu.CompilerParams(vmem_limit_bytes=32 * 2**20),
-        cost_estimate=pl.CostEstimate(flops=3 * 2**30, bytes_accessed=14 * 2**20, transcendentals=0),
-        name="prepare",
-    )(f, h)
-
-
 def flat(rows):
     return jnp.concatenate([rows[q : q + 1] for q in range(4)], 1)
 
 
 def block_kernel(
-    at_ref, got0, got1, got2, got3, f_ref, h_ref, s_ref, weight_ref, gp_hi, gp_lo, gy_hi, gy_lo, h_hi, h_lo, diag_ref,
+    at_ref, got0, got1, got2, got3, f_ref, h_ref, s_ref, weight_ref,
     x_own, x_end, maps, map_ends, state, bits_ref, hw_ref, got_ref,
+    gp_hi, gp_lo, gy_hi, gy_lo, h_hi, h_lo, diag_ref, t_hi, t_lo,
 ):
     second, own, plane, place = at_ref[0], at_ref[1], at_ref[2], at_ref[3]
     for n, part in enumerate((got0, got1, got2, got3)):
@@ -169,6 +150,7 @@
     def _():
         x_own[...] = jnp.zeros_like(x_own)
         x_end[...] = jnp.zeros_like(x_end)
+        prepare(f_ref, h_ref, gp_hi, gp_lo, gy_hi, gy_lo, h_hi, h_lo, diag_ref, t_hi, t_lo)
         unit = (
             lax.broadcasted_iota(jnp.int32, (32, 1024), 1)
             == lax.broadcasted_iota(jnp.int32, (32, 1024), 0) + 32 * place
@@ -218,15 +200,52 @@
             jax.ShapeDtypeStruct((8, 40, 1024), F32),
             jax.ShapeDtypeStruct((40, 1024), F32),
         ),
-        in_specs=[SMEM] + [VMEM] * 15,
+        in_specs=[SMEM] + [VMEM] * 8,
         out_specs=(VMEM,) * 4,
-        scratch_shapes=[pltpu.VMEM((72, 1024), F32), pltpu.VMEM((512, 128), jnp.int32), pltpu.VMEM((512, 1024), F32), pltpu.VMEM((128, 8, 128), F32)],
-        compiler_params=pltpu.CompilerParams(vmem_limit_bytes=28 * 2**20),
+        scratch_shapes=[
+            pltpu.VMEM((72, 1024), F32),
+            pltpu.VMEM((512, 128), jnp.int32),
+            pltpu.VMEM((512, 1024), F32),
+            pltpu.VMEM((128, 8, 128), F32),
+            *[pltpu.VMEM((1024, 1024), BF16)] * 2,
+            *[pltpu.VMEM((1024, 512), BF16)] * 2,
+            *[pltpu.VMEM((512, 1024), BF16)] * 2,
+            pltpu.VMEM((1, 1024), F32),
+            *[pltpu.VMEM((1024, 512), BF16)] * 2,
+        ],
+        compiler_params=pltpu.CompilerParams(vmem_limit_bytes=36 * 2**20),
         name="blocks",
     )(*args)
 
 
-def own_kernel(z_ref, m_ref, f_ref, h_ref, weight_ref, s_ref, x_out, f_out, bits_ref, hw_ref):
+def parts_kernel(at_ref, s1_ref, s2_ref, maps_ref, out_ref):
+    s2 = jnp.sum(s2_ref[...], axis=0, keepdims=True)
+    s = jnp.where(at_ref[2] < 2, s1_ref[...], s2)
+    s = jnp.broadcast_to(s, (32, 32))
+    on = lax.broadcasted_iota(jnp.int32, (32, 32), 0) == lax.broadcasted_iota(jnp.int32, (32, 32), 1)
+    s = jnp.sum(jnp.where(on, s, 0.0), axis=1, keepdims=True)
+    once = (at_ref[3] == 0).astype(F32)
+    for q in range(8):
+        total = jnp.sum(s * maps_ref[q, 0:32, :], axis=0, keepdims=True) + once * maps_ref[q, 32:33, :]
+        for j in range(4):
+            for t in range(8):
+                out_ref[4 * q + j, t : t + 1, :] = total[:, 128 * t : 128 * t + 128]
+
+
+def run_parts(*args):
+    return pl.pallas_call(
+        parts_kernel,
+        out_shape=jax.ShapeDtypeStruct((32, 8, 128), F32),
+        in_specs=[SMEM] + [VMEM] * 3,
+        out_specs=VMEM,
+        name="parts",
+    )(*args)
+
+
+def own_kernel(
+    at_ref, z_ref, m_ref, f_ref, h_ref, weight_ref, d_ref, x_own, got_ref,
+    x_out, f_out, e_out, bits_ref, hw_ref, xs, fs,
+):
     diff = spread_index()
     store_weighted(hw_ref, h_ref, weight_ref[...], diff)
     store_bits(bits_ref, sum(m_ref[j] * float(2**j) for j in range(4)), diff)
@@ -236,30 +255,53 @@
 
         @pl.when(k > 0)
         def _():
-            f_out[k - 1] = p
+            fs[k - 1] = p
 
         x = update(h_ref, hw_ref, bits_ref, jnp.int32(1) << k, z_ref[k], p, diff)
-        x_out[k] = x
+        xs[k] = x
         return x
 
-    x = lax.fori_loop(0, 4, step, s_ref[...])
-    f_out[3] = propagate(f_ref, x, diff)
+    begin = jnp.where(at_ref[0] == 0, x_own[...], jnp.sum(got_ref[...], axis=0))
+    x = lax.fori_loop(0, 4, step, begin)
+    fs[3] = propagate(f_ref, x, diff)
+    shift = (8 - 2 * at_ref[4]) % 8
+    x4 = [pltpu.roll(xs[j], shift, 0)[0:2] for j in range(4)]
+    f4 = [pltpu.roll(fs[j], shift, 0)[0:2] for j in range(4)]
+    last = at_ref[5] == 63
+    factor = jnp.ones((2, 128), F32)
+    const = jnp.where(last, f4[3], 0.0)
+    for j in reversed(range(4)):
+        const = x4[j] + d_ref[j] * (const - f4[j])
+        factor = factor * d_ref[j]
+        x_out[j] = x4[j]
+        f_out[j] = f4[j]
+    element = jnp.concatenate([jnp.where(last, 0.0, factor), const], 0)
+    e_out[...] = jnp.broadcast_to(element[None], e_out.shape)
 
 
 def run_own(*args):
     return pl.pallas_call(
         own_kernel,
-        out_shape=(jax.ShapeDtypeStruct((4, 8, 128), F32),) * 2,
-        in_specs=[VMEM] * 6,
-        out_specs=(VMEM, VMEM),
-        scratch_shapes=[pltpu.VMEM((512, 128), jnp.int32), pltpu.VMEM((512, 1024), F32)],
-        compiler_params=pltpu.CompilerParams(vmem_limit_bytes=16 * 2**20),
+        out_shape=(
+            jax.ShapeDtypeStruct((4, 2, 128), F32),
+            jax.ShapeDtypeStruct((4, 2, 128), F32),
+            jax.ShapeDtypeStruct((64, 4, 128), F32),
+        ),
+        in_specs=[SMEM] + [VMEM] * 8,
+        out_specs=(VMEM,) * 3,
+        scratch_shapes=[
+            pltpu.VMEM((512, 128), jnp.int32),
+            pltpu.VMEM((512, 1024), F32),
+            pltpu.VMEM((4, 8, 128), F32),
+            pltpu.VMEM((4, 8, 128), F32),
+        ],
+        compiler_params=pltpu.CompilerParams(vmem_limit_bytes=20 * 2**20),
         name="own_steps",
     )(*args)
 
 
-def smooth_kernel(at_ref, parts_ref, d_ref, x_ref, f_ref, out_ref):
-    at = at_ref[0]
+def smooth_kernel(at_ref, parts_ref, d_ref, x_ref, f_ref, x_out, r_out):
+    at = at_ref[5]
     later = f_ref[3]
     count = parts_ref.shape[0]
 
@@ -270,8 +312,21 @@
 
     later = lax.fori_loop(0, count, one, later)
     for j in reversed(range(4)):
-        later = x_ref[j] + d_ref[j] * (later - f_ref[j])
-        out_ref[j] = later
+        x = x_ref[j]
+        later = x + d_ref[j] * (later - f_ref[j])
+        for q in range(2):
+            x_out[j : j + 1, 128 * q : 128 * q + 128] = x[q : q + 1]
+            r_out[j : j + 1, 128 * q : 128 * q + 128] = later[q : q + 1]
+
+
+def run_smooth(*args):
+    return pl.pallas_call(
+        smooth_kernel,
+        out_shape=(jax.ShapeDtypeStruct((4, 256), F32),) * 2,
+        in_specs=[SMEM] + [VMEM] * 4,
+        out_specs=(VMEM, VMEM),
+        name="smooth_own",
+    )(*args)
 
 
 def body(z, mask, f, h, weight, d, prior):
@@ -279,47 +334,25 @@
     at = lax.axis_index(TIME)
     place = lax.axis_index(PLANE)
     y = lax.axis_index("y")
-    z = z.reshape(4, 4, 128)
-    mask = mask.astype(F32).reshape(4, 4, 128)
-    own = lax.dynamic_index_in_dim(jnp.concatenate([z, mask], 1), y, 0, True)
-    flat_plane = lax.all_to_all(jnp.broadcast_to(own, (32, 8, 128)), PLANE, 0, 0, tiled=True)
-    turned = [flat_plane] + [lax.ppermute(flat_plane, "l", [(i, (i + n) % 4) for i in range(4)]) for n in (1, 2, 3)]
-    gp_hi, gp_lo, gy_hi, gy_lo, h_hi, h_lo, diag = prepare(f, h)
+    flags = jnp.stack([h_at, 4 * (at % 32), l_at, place, y, at]).astype(jnp.int32)
+    own_z = lax.dynamic_slice_in_dim(z, y, 1, 0).reshape(4, 128)
+    own_m = lax.dynamic_slice_in_dim(mask, y, 1, 0).astype(F32).reshape(4, 128)
+    own = jnp.broadcast_to(jnp.concatenate([own_z, own_m], 0)[None], (32, 8, 128))
+    got = lax.all_to_all(own, PLANE, 0, 0, tiled=True)
+    turned = [got] + [lax.ppermute(got, "l", [(i, (i + n) % 4) for i in range(4)]) for n in (1, 2, 3)]
     weight = weight.reshape(4, 128)
-    flags = jnp.stack([h_at, 4 * (at % 32), l_at, place]).astype(jnp.int32)
-    x_own, x_end, maps, ends = run_blocks(
-        flags, *turned, f, h, prior.reshape(8, 128), weight, gp_hi, gp_lo, gy_hi, gy_lo, h_hi, h_lo, diag
-    )
-    first = place == 0
+    x_own, x_end, maps, ends = run_blocks(flags, *turned, f, h, prior.reshape(8, 128), weight)
     s1 = lax.ppermute(x_end, "h", [(0, 1)]).reshape(32, 32)
-    mine = lax.dynamic_index_in_dim(s1, place, 0, False)
-    part = jnp.sum(mine[:, None] * ends[:32], 0) + jnp.where(first, ends[32], 0.0)
-    s2 = lax.all_to_all(part.reshape(32, 32), PLANE, 0, 0, tiled=True).sum(0)
-    mine = jnp.where(l_at < 2, mine, s2)
-    parts = jnp.sum(mine[None, :, None] * maps[:, :32], 1) + jnp.where(first, maps[:, 32], 0.0)
-    parts = jnp.broadcast_to(parts[:, None], (8, 4, 1024)).reshape(32, 1024)
-    begin = lax.all_to_all(parts, PLANE, 0, 0, tiled=True).sum(0).reshape(8, 128)
-    begin = jnp.where(h_at == 0, x_own, begin)
-    x4, f4 = run_own(z, mask, f, h, weight, begin)
-    x4 = lax.dynamic_slice_in_dim(x4, 2 * y, 2, 1)
-    f4 = lax.dynamic_slice_in_dim(f4, 2 * y, 2, 1)
+    s1 = lax.dynamic_slice_in_dim(s1, place, 1, 0)
+    part = jnp.sum(s1.reshape(32, 1) * ends[:32], 0) + jnp.where(place == 0, ends[32], 0.0)
+    s2 = lax.all_to_all(part.reshape(32, 32), PLANE, 0, 0, tiled=True)
+    parts = lax.all_to_all(run_parts(flags, s1, s2, maps), PLANE, 0, 0, tiled=True)
+    z4 = z.reshape(4, 4, 128)
+    m4 = mask.astype(F32).reshape(4, 4, 128)
     d4 = d.reshape(4, 2, 128)
-    last = at == 63
-    factor = jnp.ones((2, 128), F32)
-    const = jnp.where(last, f4[3], 0.0)
-    for j in reversed(range(4)):
-        const = x4[j] + d4[j] * (const - f4[j])
-        factor = factor * d4[j]
-    element = jnp.concatenate([jnp.where(last, 0.0, factor), const], 0)
-    parts = lax.all_to_all(jnp.broadcast_to(element[None], (64, 4, 128)), TIME, 0, 0, tiled=True)
-    smooth = pl.pallas_call(
-        smooth_kernel,
-        out_shape=jax.ShapeDtypeStruct((4, 2, 128), F32),
-        in_specs=[SMEM] + [VMEM] * 4,
-        out_specs=VMEM,
-        name="smooth_own",
-    )(at.reshape(1), parts, d4, x4, f4)
-    return x4.reshape(4, 256), smooth.reshape(4, 256)
+    x4, f4, element = run_own(flags, z4, m4, f, h, weight, d4, x_own, parts)
+    elements = lax.all_to_all(element, TIME, 0, 0, tiled=True)
+    return run_smooth(flags, elements, d4, x4, f4)
 
 
 def solution(mesh):

time: 219 us -> 207 us (0.945)
  blocking collectives: 16 us -> 37.8 us
  local copies, waits for them, and re-layouts: 31.2 us -> 11.3 us
  starting transfers between devices: 43.4 us -> 38.1 us
  other arithmetic: 5.04 us -> 1.45 us
  Pallas kernels: 96.5 us -> 94.1 us
    all_to_all x1 -> x2, blocking collectives: 16 us -> 37.8 us  [the longest x1 21.9 us: body(): elements = lax.all_to_all(element, TIME, 0, 0, tiled=True)]
    unnamed x57 -> x34, local copies, waits for them, and re-layouts: 27.5 us -> 9.65 us
    all_to_all x3 -> x2, waiting for transfers between devices: 23.9 us -> 14.1 us  [the longest x1 7.57 us: body(): lax.all_to_all(run_parts(flags, s1, s2, maps), PLANE, 0, 0, tiled=True)]
    all_to_all x3 -> x2, starting transfers between devices: 19 us -> 9.41 us  [the longest x1 5.24 us: body(): s2 = lax.all_to_all(part.reshape(32, 32), PLANE, 0, 0, tiled=True)]
    ppermute x3, waiting for transfers between devices: 0.01 us -> 8.48 us  [body(): lax.ppermute(got, 'l', [(i, (i + n) % 4) for i in range(4)])]
    ppermute x1, starting transfers between devices: 19.1 us -> 23.4 us  [body(): s1 = lax.ppermute(x_end, 'h', [(0, 1)]).reshape(32, 32)]
    reduce_sum x4 -> x1, other arithmetic: 2.58 us -> 0.09 us  [body(): jnp.sum(s1.reshape(32, 1) * ends[:32], 0)]
  transfers between devices with their start and end apart: 7 -> 6, of which waited for: 4 -> 5; matrix products, arithmetic and copies ran while one was open for 1% -> 0% of each run, Pallas kernels for 2% -> 0%
where the time goes in v3:
time: 207 us
  Pallas kernels  94.1 us (45%)
  starting transfers between devices  38.1 us (18%)
  blocking collectives  37.8 us (18%)
  waiting for transfers between devices  23.2 us (11%)
  local copies, waits for them, and re-layouts  11.3 us (5%)
    pallas_call x1, Pallas kernels, run_blocks(): pl.pallas_call(block_kernel, out_shape=(jax.ShapeDtypeStruct((8, 128), F3...  86.1 us
    ppermute x1, starting transfers between devices, body(): s1 = lax.ppermute(x_end, 'h', [(0, 1)]).reshape(32, 32)  23.4 us
    all_to_all x1, blocking collectives, body(): elements = lax.all_to_all(element, TIME, 0, 0, tiled=True)  21.9 us
    all_to_all x1, blocking collectives, body(): got = lax.all_to_all(own, PLANE, 0, 0, tiled=True)  16 us
    unnamed x34, local copies, waits for them, and re-layouts  9.65 us
    ppermute x3, waiting for transfers between devices, body(): lax.ppermute(got, 'l', [(i, (i + n) % 4) for i in range(4)])  8.48 us
    all_to_all x1, waiting for transfers between devices, body(): lax.all_to_all(run_parts(flags, s1, s2, maps), PLANE, 0, 0, tiled=True)  7.57 us
    all_to_all x1, waiting for transfers between devices, body(): s2 = lax.all_to_all(part.reshape(32, 32), PLANE, 0, 0, tiled=True)  6.48 us
  transfers between devices with their start and end apart: 6, of which 5 were waited for; matrix products, arithmetic and copies ran while one was open for 0% of the time, Pallas kernels for 0%

profile of v3, /device:TPU:1, one launch (start us, length us, event | category | flops | bytes accessed | tf_op | source)
XLA Modules:
  0.0 206.8 jit_solution(11795776469055864206)
XLA Ops:
  0.6 0.7 constant_dynamic-slice_fusion.1
  1.3 0.7 dynamic-slice_convert_fusion
  2.1 16.0 %all_to_all.23.got0 = f32[32,8,128]{2,1,0:T(8,128)S(1)} all-to-all(f32[32,8,128]{2,1,0:T(8,128)S(1)} %broadcast_in_dim.10), channel_id=1, replica_groups=mesh['h'=2,'l'=4,'x'=4,'c'=2,'y'=4] {'x','c','y'}, dimensions={0} | all-to-all | bytes 262144 | tf_op jit(solution)/shard_map/all_to_all | solution.py:341
  18.0 1.6 collective-permute-start
  19.7 3.0 %collective-permute-start.1 = (f32[32,8,128]{2,1,0:T(8,128)S(1)}, f32[32,8,128]{2,1,0:T(8,128)S(1)}, u32[]{:S(2)}, u32[]{:S(2)}) collective-permute-start(f32[32,8,128]{2,1,0:T(8,128)S(1)} %all_to_all.23.got0), channel_id=1, source_target_pairs={{0,64},{32,96},{64,0},{96,32},{1,65},{33,97},{65,1},{97,33},{2,66}... | collective-permute-start | bytes 393224 | tf_op jit(solution)/shard_map/ppermute | solution.py:342
  22.7 0.7 collective-permute-start.2
  23.4 0.1 stack.27.at_ref
  23.5 2.4 %collective-permute-done.got1 = f32[32,8,128]{2,1,0:T(8,128)S(1)} collective-permute-done((f32[32,8,128]{2,1,0:T(8,128)S(1)}, f32[32,8,128]{2,1,0:T(8,128)S(1)}, u32[]{:S(2)}, u32[]{:S(2)}) %collective-permute-start) | collective-permute-done | bytes 131104 | tf_op jit(solution)/shard_map/ppermute | solution.py:342
  25.9 6.1 %collective-permute-done.1.got2 = f32[32,8,128]{2,1,0:T(8,128)S(1)} collective-permute-done((f32[32,8,128]{2,1,0:T(8,128)S(1)}, f32[32,8,128]{2,1,0:T(8,128)S(1)}, u32[]{:S(2)}, u32[]{:S(2)}) %collective-permute-start.1) | collective-permute-done | bytes 131104 | tf_op jit(solution)/shard_map/ppermute | solution.py:342
  32.0 0.0 collective-permute-done.2.got3
  32.0 2.2 %copy-done = f32[1024,1024]{1,0:T(8,128)S(1)} copy-done((f32[1024,1024]{1,0:T(8,128)S(1)}, f32[1024,1024]{1,0:T(8,128)}, u32[]{:S(2)}) %copy-start) | copy-done | bytes 4194328
  34.2 1.6 copy-done.2
  35.7 0.7 copy-done.8
  36.4 0.7 copy-done.12
  37.1 0.0 copy-start.9
  37.1 86.1 %blocks.1 = (f32[8,128]{1,0:T(8,128)S(1)}, f32[8,128]{1,0:T(8,128)S(1)}, f32[8,40,1024]{2,1,0:T(8,128)S(1)}, f32[40,1024]{1,0:T(8,128)S(1)}) custom-call(s32[6]{0:T(128)S(1)} %stack.27.at_ref, f32[32,8,128]{2,1,0:T(8,128)S(1)} %all_to_all.23.got0, f32[32,8,128]{2,1,0:T(8,128)S(1)} %collective-permute-done.got1, ...), custom_call_target="tpu_custom_call" | custom-call | tf_op jit(solution)/shard_map/blocks/pallas_call | solution.py:195
  123.2 0.0 copy-done.6
  123.2 0.0 copy-start.4
  123.2 1.1 copy-done.4
  124.3 23.4 %collective-permute-start.3 = (f32[8,128]{1,0:T(8,128)S(1)}, f32[8,128]{1,0:T(8,128)S(1)}, u32[]{:S(2)}, u32[]{:S(2)}) collective-permute-start(f32[8,128]{1,0:T(8,128)S(1)} %get-tuple-element.10), channel_id=1, source_target_pairs={{0,128},{1,129},{2,130},{3,131},{4,132},{5,133},{6,134},{7,135},{8... | collective-permute-start | bytes 12296 | tf_op jit(solution)/shard_map/ppermute | solution.py:345
  147.7 0.1 select_n.38
  147.8 0.6 collective-permute-done.3
  148.4 0.1 reshape.66
  148.5 0.1 multiply_reduce_fusion
  148.6 0.1 reduce_sum.12
  148.7 0.6 add.45
  149.3 5.2 %all-to-all-start.1 = ((f32[32,1,32]{2,1,0:T(1,128)}), f32[32,1,32]{2,1,0:T(1,128)S(1)}, u32[]{:S(2)}, u32[]{:S(2)}) async-start(f32[32,1,32]{2,1,0:T(1,128)} %add.45), calls=%async_computation.1 | async-start | bytes 32768 | tf_op jit(solution)/shard_map/all_to_all | solution.py:348
  154.5 0.5 constant_dynamic-slice_fusion.s1_ref
  155.1 6.5 %all-to-all-done.1 = f32[32,1,32]{2,1,0:T(1,128)S(1)} async-done(((f32[32,1,32]{2,1,0:T(1,128)}), f32[32,1,32]{2,1,0:T(1,128)S(1)}, u32[]{:S(2)}, u32[]{:S(2)}) %all-to-all-start.1) | async-done | bytes 4128 | tf_op jit(solution)/shard_map/all_to_all | solution.py:348
  161.6 0.6 copy-done.13
  162.2 2.2 %parts.1 = f32[32,8,128]{2,1,0:T(8,128)} custom-call(s32[6]{0:T(128)} %copy-done.6, f32[1,32]{1,0:T(1,128)} %constant_dynamic-slice_fusion.s1_ref, f32[32,32]{1,0:T(8,128)} %bitcast.17, f32[8,40,1024]{2,1,0:T(8,128)} %copy-done.4), custom_call_target="tpu_custom_call" | custom-call | tf_op jit(solution)/shard_map/parts/pallas_call | solution.py:236
  164.4 4.2 %all-to-all-start.2 = ((f32[32,8,128]{2,1,0:T(8,128)}), f32[32,8,128]{2,1,0:T(8,128)S(1)}, u32[]{:S(2)}, u32[]{:S(2)}) async-start(f32[32,8,128]{2,1,0:T(8,128)} %parts.1), calls=%async_computation.2 | async-start | bytes 262144 | tf_op jit(solution)/shard_map/all_to_all | solution.py:349
  168.6 0.0 copy-done.14
  168.6 0.0 copy-done.15
  168.6 0.0 copy-done.16
  168.7 7.6 %all-to-all-done.2.got_ref = f32[32,8,128]{2,1,0:T(8,128)S(1)} async-done(((f32[32,8,128]{2,1,0:T(8,128)}), f32[32,8,128]{2,1,0:T(8,128)S(1)}, u32[]{:S(2)}, u32[]{:S(2)}) %all-to-all-start.2) | async-done | bytes 131104 | tf_op jit(solution)/shard_map/all_to_all | solution.py:349
  176.3 0.0 copy-done.3
  176.3 0.0 copy-done.9
  176.3 2.2 %copy-done.1 = f32[1024,1024]{1,0:T(8,128)S(1)} copy-done((f32[1024,1024]{1,0:T(8,128)S(1)}, f32[1024,1024]{1,0:T(8,128)}, u32[]{:S(2)}) %copy-start.1) | copy-done | bytes 4194328
  178.5 0.6 copy-done.7
  179.1 3.8 %own_steps.1 = (f32[4,2,128]{2,1,0:T(2,128)S(1)}, f32[4,2,128]{2,1,0:T(2,128)S(1)}, f32[64,4,128]{2,1,0:T(4,128)S(1)}) custom-call(s32[6]{0:T(128)S(1)} %copy-done.7, f32[4,4,128]{2,1,0:T(4,128)S(1)} %reshape.59.z_ref, f32[4,4,128]{2,1,0:T(4,128)S(1)} %reshape.60.m_ref, f32[1024,1024]{1,0:T(8,128)S(1)} %copy-done.1, f32[512,1024]{1,0:T(8,128)S(1)} %copy-done.3, ...), custom_call_target="tpu_custom_call" | custom-call | tf_op jit(solution)/shard_map/own_steps/pallas_call | solution.py:283
  182.9 0.0 copy-done.5
  182.9 0.0 copy-start.10
  182.9 0.0 copy-start.11
  182.9 21.9 %all_to_all.24.parts_ref = f32[64,4,128]{2,1,0:T(4,128)} all-to-all(f32[64,4,128]{2,1,0:T(4,128)S(1)} %get-tuple-element.13), channel_id=1, replica_groups=mesh['h'=2,'l'=4,'x'=4,'c'=2,'y'=4] {'h','l','x','c'}, dimensions={0} | all-to-all | bytes 262144 | tf_op jit(solution)/shard_map/all_to_all | solution.py:354
  204.8 0.0 copy-done.10
  204.8 0.0 copy-done.11
  204.8 2.0 smooth_own.1
  (21 shorter events, 0.1 us)
Async XLA Ops:
  18.0 7.8 %collective-permute-start = (f32[32,8,128]{2,1,0:T(8,128)S(1)}, f32[32,8,128]{2,1,0:T(8,128)S(1)}, u32[]{:S(2)}, u32[]{:S(2)}) collective-permute-start(f32[32,8,128]{2,1,0:T(8,128)S(1)} %all_to_all.23.got0), channel_id=1, source_target_pairs={{0,32},{32,64},{64,96},{96,0},{1,33},{33,65},{65,97},{97,1},{2,34}... | collective-permute-start | bytes 393224 | tf_op jit(solution)/shard_map/ppermute | solution.py:342
  19.7 12.3 %collective-permute-start.1 = (f32[32,8,128]{2,1,0:T(8,128)S(1)}, f32[32,8,128]{2,1,0:T(8,128)S(1)}, u32[]{:S(2)}, u32[]{:S(2)}) collective-permute-start(f32[32,8,128]{2,1,0:T(8,128)S(1)} %all_to_all.23.got0), channel_id=1, source_target_pairs={{0,64},{32,96},{64,0},{96,32},{1,65},{33,97},{65,1},{97,33},{2,66}... | collective-permute-start | bytes 393224 | tf_op jit(solution)/shard_map/ppermute | solution.py:342
  22.7 9.3 %collective-permute-start.2 = (f32[32,8,128]{2,1,0:T(8,128)S(1)}, f32[32,8,128]{2,1,0:T(8,128)S(1)}, u32[]{:S(2)}, u32[]{:S(2)}) collective-permute-start(f32[32,8,128]{2,1,0:T(8,128)S(1)} %all_to_all.23.got0), channel_id=1, source_target_pairs={{0,96},{32,0},{64,32},{96,64},{1,97},{33,1},{65,33},{97,65},{2,98}... | collective-permute-start | bytes 393224 | tf_op jit(solution)/shard_map/ppermute | solution.py:342
  23.5 99.7 %copy-start.6 = (s32[6]{0:T(128)}, s32[6]{0:T(128)S(1)}, u32[]{:S(2)}) copy-start(s32[6]{0:T(128)S(1)} %stack.27.at_ref) | copy-start | bytes 76
  32.0 2.2 %copy-start = (f32[1024,1024]{1,0:T(8,128)S(1)}, f32[1024,1024]{1,0:T(8,128)}, u32[]{:S(2)}) copy-start(f32[1024,1024]{1,0:T(8,128)} %f_ref.3) | copy-start | bytes 12582916
  34.2 1.6 copy-start.2
  35.7 0.7 copy-start.8
  36.4 0.7 copy-start.12
  37.1 131.5 %copy-start.14 = (s32[4,512]{1,0:T(4,128)S(1)}, s32[4,512]{1,0:T(4,128)}, u32[]{:S(2)}) copy-start(s32[4,512]{1,0:T(4,128)} %param.8) | copy-start | bytes 24580
  37.1 131.5 %copy-start.15 = (f32[4,512]{1,0:T(4,128)S(1)}, f32[4,512]{1,0:T(4,128)}, u32[]{:S(2)}) copy-start(f32[4,512]{1,0:T(4,128)} %param.7) | copy-start | bytes 24580
  37.1 131.5 %copy-start.16 = (f32[4,256]{1,0:T(4,128)S(1)}, f32[4,256]{1,0:T(4,128)}, u32[]{:S(2)}) copy-start(f32[4,256]{1,0:T(4,128)} %param.12) | copy-start | bytes 12292
  37.1 139.1 %copy-start.3 = (f32[512,1024]{1,0:T(8,128)S(1)}, f32[512,1024]{1,0:T(8,128)}, u32[]{:S(2)}) copy-start(f32[512,1024]{1,0:T(8,128)} %h_ref.3) | copy-start | bytes 6291460
  37.1 139.1 %copy-start.9 = (f32[512]{0:T(512)S(1)}, f32[512]{0:T(512)}, u32[]{:S(2)}) copy-start(f32[512]{0:T(512)} %param.11) | copy-start | bytes 6148
  123.2 1.1 copy-start.4
  124.3 24.1 %collective-permute-start.3 = (f32[8,128]{1,0:T(8,128)S(1)}, f32[8,128]{1,0:T(8,128)S(1)}, u32[]{:S(2)}, u32[]{:S(2)}) collective-permute-start(f32[8,128]{1,0:T(8,128)S(1)} %get-tuple-element.10), channel_id=1, source_target_pairs={{0,128},{1,129},{2,130},{3,131},{4,132},{5,133},{6,134},{7,135},{8... | collective-permute-start | bytes 12296 | tf_op jit(solution)/shard_map/ppermute | solution.py:345
  149.3 12.3 %all-to-all-start.1 = ((f32[32,1,32]{2,1,0:T(1,128)}), f32[32,1,32]{2,1,0:T(1,128)S(1)}, u32[]{:S(2)}, u32[]{:S(2)}) async-start(f32[32,1,32]{2,1,0:T(1,128)} %add.45), calls=%async_computation.1 | async-start | bytes 32768 | tf_op jit(solution)/shard_map/all_to_all | solution.py:348
  161.6 0.6 copy-start.13
  164.4 11.8 %all-to-all-start.2 = ((f32[32,8,128]{2,1,0:T(8,128)}), f32[32,8,128]{2,1,0:T(8,128)S(1)}, u32[]{:S(2)}, u32[]{:S(2)}) async-start(f32[32,8,128]{2,1,0:T(8,128)} %parts.1), calls=%async_computation.2 | async-start | bytes 262144 | tf_op jit(solution)/shard_map/all_to_all | solution.py:349
  168.7 14.2 %copy-start.5 = (f32[4,2,128]{2,1,0:T(2,128)}, f32[4,2,128]{2,1,0:T(2,128)S(1)}, u32[]{:S(2)}) copy-start(f32[4,2,128]{2,1,0:T(2,128)S(1)} %reshape.62.d_ref) | copy-start | bytes 12292
  176.3 2.2 %copy-start.1 = (f32[1024,1024]{1,0:T(8,128)S(1)}, f32[1024,1024]{1,0:T(8,128)}, u32[]{:S(2)}) copy-start(f32[1024,1024]{1,0:T(8,128)} %f_ref.3) | copy-start | bytes 12582916
  178.4 0.6 copy-start.7
  182.9 21.9 %copy-start.10 = (f32[4,2,128]{2,1,0:T(2,128)}, f32[4,2,128]{2,1,0:T(2,128)S(1)}, u32[]{:S(2)}) copy-start(f32[4,2,128]{2,1,0:T(2,128)S(1)} %get-tuple-element.14.x_ref) | copy-start | bytes 12292
  182.9 21.9 %copy-start.11 = (f32[4,2,128]{2,1,0:T(2,128)}, f32[4,2,128]{2,1,0:T(2,128)S(1)}, u32[]{:S(2)}) copy-start(f32[4,2,128]{2,1,0:T(2,128)S(1)} %get-tuple-element.15.f_ref) | copy-start | bytes 12292

commit v4 on v3

--- a/solution.py
+++ b/solution.py
@@ -14,6 +14,7 @@
 BF16 = jnp.bfloat16
 VMEM = pl.BlockSpec(memory_space=pltpu.VMEM)
 SMEM = pl.BlockSpec(memory_space=pltpu.SMEM)
+ANY = pl.BlockSpec(memory_space=pl.ANY)
 
 
 def wide(row):
@@ -93,7 +94,7 @@
             hw_ref[r, c] = h_ref[r, c] * w
 
 
-def prepare(f_ref, h_ref, gp_hi, gp_lo, gy_hi, gy_lo, h_hi, h_lo, diag_ref, t_hi, t_lo):
+def prepare_kernel(f_ref, h_ref, gp_hi, gp_lo, gy_hi, gy_lo, h_hi, h_lo, diag_ref, t_hi, t_lo):
     h_hi[...], h_lo[...] = halves(h_ref[...])
     for j in range(8):
         r = slice(128 * j, 128 * j + 128)
@@ -108,28 +109,57 @@
         diag_ref[:, r] = jnp.sum(jnp.where(on, ft, 0.0), axis=0, keepdims=True)[:, r]
 
 
+def prepare(f, h):
+    return pl.pallas_call(
+        prepare_kernel,
+        out_shape=(
+            *[jax.ShapeDtypeStruct((1024, 1024), BF16)] * 2,
+            *[jax.ShapeDtypeStruct((1024, 512), BF16)] * 2,
+            *[jax.ShapeDtypeStruct((512, 1024), BF16)] * 2,
+            jax.ShapeDtypeStruct((1, 1024), F32),
+        ),
+        in_specs=[VMEM] * 2,
+        out_specs=(VMEM,) * 7,
+        scratch_shapes=[pltpu.VMEM((1024, 512), BF16)] * 2,
+        compiler_params=pltpu.CompilerParams(vmem_limit_bytes=26 * 2**20),
+        cost_estimate=pl.CostEstimate(flops=3 * 2**30, bytes_accessed=14 * 2**20, transcendentals=0),
+        name="prepare",
+    )(f, h)
+
+
 def flat(rows):
     return jnp.concatenate([rows[q : q + 1] for q in range(4)], 1)
 
 
 def block_kernel(
-    at_ref, got0, got1, got2, got3, f_ref, h_ref, s_ref, weight_ref,
-    x_own, x_end, maps, map_ends, state, bits_ref, hw_ref, got_ref,
-    gp_hi, gp_lo, gy_hi, gy_lo, h_hi, h_lo, diag_ref, t_hi, t_lo,
+    at_ref, got_ref, s_ref, weight_ref, diag_ref, f_any, h_any, *rest,
 ):
+    mats_any, (x_own, x_end, maps, map_ends), rest = rest[:6], rest[6:10], rest[10:]
+    state, bits_ref, hw_ref, f_ref, h_ref, *mats, sems = rest
+    gp_hi, gp_lo, gy_hi, gy_lo, h_hi, h_lo = mats
     second, own, plane, place = at_ref[0], at_ref[1], at_ref[2], at_ref[3]
-    for n, part in enumerate((got0, got1, got2, got3)):
-        got_ref[pl.ds(32 * ((plane + 4 - n) % 4), 32)] = part[...]
+
+    def fetch(pairs):
+        copies = [pltpu.make_async_copy(a, b, sems.at[i]) for i, (a, b) in enumerate(pairs)]
+        for c in copies:
+            c.start()
+        for c in copies:
+            c.wait()
+
+    def at_step(k):
+        return got_ref[k % 32, (plane + 4 - k // 32) % 4]
+
 
     @pl.when(second == 0)
     def _():
+        fetch([(f_any, f_ref), (h_any, h_ref)])
         diff = spread_index()
         maps[...] = jnp.zeros_like(maps)
         map_ends[...] = jnp.zeros_like(map_ends)
         store_weighted(hw_ref, h_ref, weight_ref[...], diff)
 
         def group(g, x):
-            words = sum(got_ref[16 * g + j][4:8] * float(2**j) for j in range(16))
+            words = sum(at_step(16 * g + j)[4:8] * float(2**j) for j in range(16))
             store_bits(bits_ref, words, diff)
 
             def step(j, x):
@@ -140,7 +170,7 @@
                     x_own[...] = x
 
                 p = propagate(f_ref, x, diff)
-                return update(h_ref, hw_ref, bits_ref, jnp.int32(1) << j, got_ref[k][0:4], p, diff)
+                return update(h_ref, hw_ref, bits_ref, jnp.int32(1) << j, at_step(k)[0:4], p, diff)
 
             return lax.fori_loop(0, 16, step, x)
 
@@ -150,7 +180,7 @@
     def _():
         x_own[...] = jnp.zeros_like(x_own)
         x_end[...] = jnp.zeros_like(x_end)
-        prepare(f_ref, h_ref, gp_hi, gp_lo, gy_hi, gy_lo, h_hi, h_lo, diag_ref, t_hi, t_lo)
+        fetch(list(zip(mats_any, mats)))
         unit = (
             lax.broadcasted_iota(jnp.int32, (32, 1024), 1)
             == lax.broadcasted_iota(jnp.int32, (32, 1024), 0) + 32 * place
@@ -172,7 +202,7 @@
             x = state[...]
             y = product(x, gy_hi, gy_lo)
             p = product(x, gp_hi, gp_lo) + x * diag_ref[...]
-            a, b = got_ref[k], got_ref[64 + k]
+            a, b = at_step(k), at_step(64 + k)
             wa, wb = flat(a[4:8]) * weight, flat(b[4:8]) * weight
             zs = jnp.where(row == 0, flat(a[0:4]), jnp.where(row == 1, flat(b[0:4]), 0.0))
             v = jnp.concatenate(
@@ -200,20 +230,20 @@
             jax.ShapeDtypeStruct((8, 40, 1024), F32),
             jax.ShapeDtypeStruct((40, 1024), F32),
         ),
-        in_specs=[SMEM] + [VMEM] * 8,
+        in_specs=[SMEM] + [VMEM] * 4 + [ANY] * 8,
         out_specs=(VMEM,) * 4,
         scratch_shapes=[
             pltpu.VMEM((72, 1024), F32),
             pltpu.VMEM((512, 128), jnp.int32),
             pltpu.VMEM((512, 1024), F32),
-            pltpu.VMEM((128, 8, 128), F32),
+            pltpu.VMEM((1024, 1024), F32),
+            pltpu.VMEM((512, 1024), F32),
             *[pltpu.VMEM((1024, 1024), BF16)] * 2,
             *[pltpu.VMEM((1024, 512), BF16)] * 2,
             *[pltpu.VMEM((512, 1024), BF16)] * 2,
-            pltpu.VMEM((1, 1024), F32),
-            *[pltpu.VMEM((1024, 512), BF16)] * 2,
+            pltpu.SemaphoreType.DMA((6,)),
         ],
-        compiler_params=pltpu.CompilerParams(vmem_limit_bytes=36 * 2**20),
+        compiler_params=pltpu.CompilerParams(vmem_limit_bytes=58 * 2**20),
         name="blocks",
     )(*args)
 
@@ -238,6 +268,7 @@
         out_shape=jax.ShapeDtypeStruct((32, 8, 128), F32),
         in_specs=[SMEM] + [VMEM] * 3,
         out_specs=VMEM,
+        compiler_params=pltpu.CompilerParams(vmem_limit_bytes=6 * 2**20),
         name="parts",
     )(*args)
 
@@ -295,7 +326,7 @@
             pltpu.VMEM((4, 8, 128), F32),
             pltpu.VMEM((4, 8, 128), F32),
         ],
-        compiler_params=pltpu.CompilerParams(vmem_limit_bytes=20 * 2**20),
+        compiler_params=pltpu.CompilerParams(vmem_limit_bytes=12 * 2**20),
         name="own_steps",
     )(*args)
 
@@ -325,6 +356,7 @@
         out_shape=(jax.ShapeDtypeStruct((4, 256), F32),) * 2,
         in_specs=[SMEM] + [VMEM] * 4,
         out_specs=(VMEM, VMEM),
+        compiler_params=pltpu.CompilerParams(vmem_limit_bytes=4 * 2**20),
         name="smooth_own",
     )(*args)
 
@@ -337,11 +369,13 @@
     flags = jnp.stack([h_at, 4 * (at % 32), l_at, place, y, at]).astype(jnp.int32)
     own_z = lax.dynamic_slice_in_dim(z, y, 1, 0).reshape(4, 128)
     own_m = lax.dynamic_slice_in_dim(mask, y, 1, 0).astype(F32).reshape(4, 128)
-    own = jnp.broadcast_to(jnp.concatenate([own_z, own_m], 0)[None], (32, 8, 128))
+    own = jnp.concatenate([own_z, own_m], 0)
+    turned = [lax.ppermute(own, "l", [(i, (i + n) % 4) for i in range(4)]) for n in (1, 2, 3)]
+    *mats, diag = prepare(f, h)
+    own = jnp.broadcast_to(jnp.stack([own, *turned])[None], (32, 4, 8, 128))
     got = lax.all_to_all(own, PLANE, 0, 0, tiled=True)
-    turned = [got] + [lax.ppermute(got, "l", [(i, (i + n) % 4) for i in range(4)]) for n in (1, 2, 3)]
     weight = weight.reshape(4, 128)
-    x_own, x_end, maps, ends = run_blocks(flags, *turned, f, h, prior.reshape(8, 128), weight)
+    x_own, x_end, maps, ends = run_blocks(flags, got, prior.reshape(8, 128), weight, diag, f, h, *mats)
     s1 = lax.ppermute(x_end, "h", [(0, 1)]).reshape(32, 32)
     s1 = lax.dynamic_slice_in_dim(s1, place, 1, 0)
     part = jnp.sum(s1.reshape(32, 1) * ends[:32], 0) + jnp.where(place == 0, ends[32], 0.0)

time: 207 us -> 208 us (level)
  blocking collectives: 37.8 us -> 20.6 us
  Pallas kernels: 94.1 us -> 103 us
  local copies, waits for them, and re-layouts: 11.3 us -> 18.5 us
  starting transfers between devices: 38.1 us -> 45.2 us
  waiting for transfers between devices: 23.2 us -> 16.6 us
    all_to_all x1 -> x0, blocking collectives: 16 us -> none  [body(): got = lax.all_to_all(own, PLANE, 0, 0, tiled=True)]
    all_to_all x0 -> x1, starting transfers between devices: none -> 9.18 us  [body(): got = lax.all_to_all(own, PLANE, 0, 0, tiled=True)]
    ppermute x3, waiting for transfers between devices: 8.48 us -> 2.02 us  [body(): lax.ppermute(own, 'l', [(i, (i + n) % 4) for i in range(4)])]
    unnamed x34 -> x38, local copies, waits for them, and re-layouts: 9.65 us -> 16 us
    ppermute x1, starting transfers between devices: 23.4 us -> 17.4 us  [body(): s1 = lax.ppermute(x_end, 'h', [(0, 1)]).reshape(32, 32)]
    pallas_call x1, Pallas kernels: 86.1 us -> 91.7 us  [run_blocks(): pl.pallas_call(block_kernel, out_shape=(jax.ShapeDtypeStruct((8, 128), F3...]
    pallas_call x0 -> x1, Pallas kernels: none -> 4.35 us  [prepare(): pl.pallas_call(prepare_kernel, out_shape=(*[jax.ShapeDtypeStruct((1024, 1...]
    all_to_all x1, starting transfers between devices: 5.24 us -> 8.22 us  [body(): s2 = lax.all_to_all(part.reshape(32, 32), PLANE, 0, 0, tiled=True)]
  transfers between devices with their start and end apart: 6 -> 7, of which waited for: 5 -> 5; matrix products, arithmetic and copies ran while one was open for 0% -> 1% of each run, Pallas kernels for 0% -> 2%
where the time goes in v4:
time: 208 us
  Pallas kernels  103 us (50%)
  starting transfers between devices  45.2 us (22%)
  blocking collectives  20.6 us (10%)
  local copies, waits for them, and re-layouts  18.5 us (9%)
  waiting for transfers between devices  16.6 us (8%)
  other arithmetic  3.11 us (1%)
    pallas_call x1, Pallas kernels, run_blocks(): pl.pallas_call(block_kernel, out_shape=(jax.ShapeDtypeStruct((8, 128), F3...  91.7 us
    all_to_all x1, blocking collectives, body(): elements = lax.all_to_all(element, TIME, 0, 0, tiled=True)  20.6 us
    ppermute x1, starting transfers between devices, body(): s1 = lax.ppermute(x_end, 'h', [(0, 1)]).reshape(32, 32)  17.4 us
    unnamed x38, local copies, waits for them, and re-layouts  16 us
    all_to_all x1, starting transfers between devices, body(): got = lax.all_to_all(own, PLANE, 0, 0, tiled=True)  9.18 us
    all_to_all x1, starting transfers between devices, body(): s2 = lax.all_to_all(part.reshape(32, 32), PLANE, 0, 0, tiled=True)  8.22 us
    all_to_all x1, waiting for transfers between devices, body(): lax.all_to_all(run_parts(flags, s1, s2, maps), PLANE, 0, 0, tiled=True)  7.58 us
    all_to_all x1, waiting for transfers between devices, body(): s2 = lax.all_to_all(part.reshape(32, 32), PLANE, 0, 0, tiled=True)  6.9 us
  transfers between devices with their start and end apart: 7, of which 5 were waited for; matrix products, arithmetic and copies ran while one was open for 1% of the time, Pallas kernels for 2%

profile of v4, /device:TPU:1, one launch (start us, length us, event | category | flops | bytes accessed | tf_op | source)
XLA Modules:
  0.0 207.8 jit_solution(655939179284832174)
XLA Ops:
  0.6 0.7 constant_dynamic-slice_fusion.1
  1.3 0.7 dynamic-slice_convert_fusion
  2.1 2.5 %collective-permute-start = (f32[8,128]{1,0:T(8,128)S(1)}, f32[8,128]{1,0:T(8,128)S(1)}, u32[]{:S(2)}, u32[]{:S(2)}) collective-permute-start(f32[8,128]{1,0:T(8,128)S(1)} %get-tuple-element.31), channel_id=1, source_target_pairs={{0,32},{32,64},{64,96},{96,0},{1,33},{33,65},{65,97},{97,1},{2,34}... | collective-permute-start | bytes 12296 | tf_op jit(solution)/shard_map/ppermute | solution.py:373
  4.6 3.0 %collective-permute-start.1 = (f32[8,128]{1,0:T(8,128)S(1)}, f32[8,128]{1,0:T(8,128)S(1)}, u32[]{:S(2)}, u32[]{:S(2)}) collective-permute-start(f32[8,128]{1,0:T(8,128)S(1)} %get-tuple-element.31), channel_id=1, source_target_pairs={{0,64},{32,96},{64,0},{96,32},{1,65},{33,97},{65,1},{97,33},{2,66}... | collective-permute-start | bytes 12296 | tf_op jit(solution)/shard_map/ppermute | solution.py:373
  7.6 0.7 collective-permute-start.2
  8.3 0.0 collective-permute-done
  8.3 0.3 collective-permute-done.1
  8.6 1.8 collective-permute-done.2
  10.3 0.9 broadcast_in_dim.10
  11.2 9.2 %all-to-all-start = ((f32[32,4,8,128]{3,2,1,0:T(8,128)}), f32[32,4,8,128]{3,2,1,0:T(8,128)S(1)}, u32[]{:S(2)}, u32[]{:S(2)}) async-start(f32[32,4,8,128]{3,2,1,0:T(8,128)} %broadcast_in_dim.10), calls=%async_computation | async-start | bytes 1048576 | tf_op jit(solution)/shard_map/all_to_all | solution.py:376
  20.4 0.7 stack.42.at_ref
  21.1 2.2 %copy-done = f32[1024,1024]{1,0:T(8,128)S(1)} copy-done((f32[1024,1024]{1,0:T(8,128)S(1)}, f32[1024,1024]{1,0:T(8,128)}, u32[]{:S(2)}) %copy-start) | copy-done | bytes 4194328
  23.3 1.6 copy-done.2
  24.9 4.4 %prepare.1 = (bf16[1024,1024]{1,0:T(8,128)(2,1)S(1)}, bf16[1024,1024]{1,0:T(8,128)(2,1)S(1)}, bf16[1024,512]{1,0:T(8,128)(2,1)S(1)}, bf16[1024,512]{1,0:T(8,128)...) custom-call(f32[1024,1024]{1,0:T(8,128)S(1)} %copy-done, ...), custom_call_target="tpu_custom_call" | custom-call | flops 3221225472 | bytes 14680064 | tf_op jit(solution)/shard_map/prepare/pallas_call | solution.py:113
  29.2 0.0 copy-start.4
  29.2 1.3 copy-done.4
  30.5 1.3 copy-done.5
  31.8 1.0 copy-done.7
  32.8 1.0 copy-done.8
  33.8 1.1 copy-done.9
  34.9 1.0 copy-done.10
  35.9 0.6 copy-done.14
  36.5 0.0 all-to-all-done.got_ref
  36.5 0.8 copy-done.15
  37.3 0.0 copy-start.3
  37.3 0.0 copy-start.12
  37.3 91.7 %blocks.1 = (f32[8,128]{1,0:T(8,128)}, f32[8,128]{1,0:T(8,128)}, f32[8,40,1024]{2,1,0:T(8,128)}, f32[40,1024]{1,0:T(8,128)}) custom-call(s32[6]{0:T(128)} %stack.42.at_ref, f32[32,4,8,128]{3,2,1,0:T(8,128)} %copy-done.15, f32[8,128]{1,0:T(8,128)} %bitcast.25, f32[4,128]{1,0:T(4,128)} %bitcast.20, f32[1,1024]{1,0:T(1,128)} %copy-done.14, f32[1024,1024]{1,0:T(8,128)} %f_ref.3, ...), custom_call_target="tpu_custom_call" | custom-call | tf_op jit(solution)/shard_map/blocks/pallas_call | solution.py:225
  129.0 17.4 %collective-permute-start.3 = (f32[8,128]{1,0:T(8,128)}, f32[8,128]{1,0:T(8,128)S(1)}, u32[]{:S(2)}, u32[]{:S(2)}) collective-permute-start(f32[8,128]{1,0:T(8,128)} %get-tuple-element.24), channel_id=1, source_target_pairs={{0,128},{1,129},{2,130},{3,131},{4,132},{5,133},{6,134},{7,135},{8... | collective-permute-start | bytes 12296 | tf_op jit(solution)/shard_map/ppermute | solution.py:379
  146.5 0.8 fusion
  147.2 0.1 select_n.38
  147.3 0.1 collective-permute-done.3
  147.4 0.1 reshape.66
  147.5 1.0 multiply_reduce_fusion
  148.5 0.1 reduce_sum.12
  148.6 0.6 add.45
  149.2 8.2 %all-to-all-start.1 = ((f32[32,1,32]{2,1,0:T(1,128)}), f32[32,1,32]{2,1,0:T(1,128)S(1)}, u32[]{:S(2)}, u32[]{:S(2)}) async-start(f32[32,1,32]{2,1,0:T(1,128)} %add.45), calls=%async_computation.1 | async-start | bytes 32768 | tf_op jit(solution)/shard_map/all_to_all | solution.py:382
  157.4 6.9 %all-to-all-done.1 = f32[32,1,32]{2,1,0:T(1,128)S(1)} async-done(((f32[32,1,32]{2,1,0:T(1,128)}), f32[32,1,32]{2,1,0:T(1,128)S(1)}, u32[]{:S(2)}, u32[]{:S(2)}) %all-to-all-start.1) | async-done | bytes 4128 | tf_op jit(solution)/shard_map/all_to_all | solution.py:382
  164.3 1.3 copy-done.6
  165.7 1.4 parts.1
  167.1 4.2 %all-to-all-start.2 = ((f32[32,8,128]{2,1,0:T(8,128)}), f32[32,8,128]{2,1,0:T(8,128)S(1)}, u32[]{:S(2)}, u32[]{:S(2)}) async-start(f32[32,8,128]{2,1,0:T(8,128)} %parts.1), calls=%async_computation.2 | async-start | bytes 262144 | tf_op jit(solution)/shard_map/all_to_all | solution.py:383
  171.3 0.0 copy-done.17
  171.3 7.6 %all-to-all-done.2.got_ref = f32[32,8,128]{2,1,0:T(8,128)S(1)} async-done(((f32[32,8,128]{2,1,0:T(8,128)}), f32[32,8,128]{2,1,0:T(8,128)S(1)}, u32[]{:S(2)}, u32[]{:S(2)}) %all-to-all-start.2) | async-done | bytes 131104 | tf_op jit(solution)/shard_map/all_to_all | solution.py:383
  178.9 0.0 copy-done.12
  178.9 2.2 %copy-done.1 = f32[1024,1024]{1,0:T(8,128)S(1)} copy-done((f32[1024,1024]{1,0:T(8,128)S(1)}, f32[1024,1024]{1,0:T(8,128)}, u32[]{:S(2)}) %copy-start.1) | copy-done | bytes 4194328
  181.1 0.7 copy-done.13
  181.8 3.8 %own_steps.1 = (f32[4,2,128]{2,1,0:T(2,128)S(1)}, f32[4,2,128]{2,1,0:T(2,128)S(1)}, f32[64,4,128]{2,1,0:T(4,128)S(1)}) custom-call(s32[6]{0:T(128)S(1)} %copy-done.11, f32[4,4,128]{2,1,0:T(4,128)S(1)} %reshape.59.z_ref, f32[4,4,128]{2,1,0:T(4,128)S(1)} %reshape.60.m_ref, f32[1024,1024]{1,0:T(8,128)S(1)} %copy-done.1, f32[512,1024]{1,0:T(8,128)S(1)} %copy-done.3, ...), custom_call_target="tpu_custom_call" | custom-call | tf_op jit(solution)/shard_map/own_steps/pallas_call | solution.py:314
  185.6 20.6 %all_to_all.23.parts_ref = f32[64,4,128]{2,1,0:T(4,128)S(1)} all-to-all(f32[64,4,128]{2,1,0:T(4,128)S(1)} %get-tuple-element.27), channel_id=1, replica_groups=mesh['h'=2,'l'=4,'x'=4,'c'=2,'y'=4] {'h','l','x','c'}, dimensions={0} | all-to-all | bytes 262144 | tf_op jit(solution)/shard_map/all_to_all | solution.py:388
  206.2 1.6 smooth_own.1
  (28 shorter events, 0.1 us)
Async XLA Ops:
  2.1 6.3 %collective-permute-start = (f32[8,128]{1,0:T(8,128)S(1)}, f32[8,128]{1,0:T(8,128)S(1)}, u32[]{:S(2)}, u32[]{:S(2)}) collective-permute-start(f32[8,128]{1,0:T(8,128)S(1)} %get-tuple-element.31), channel_id=1, source_target_pairs={{0,32},{32,64},{64,96},{96,0},{1,33},{33,65},{65,97},{97,1},{2,34}... | collective-permute-start | bytes 12296 | tf_op jit(solution)/shard_map/ppermute | solution.py:373
  4.6 4.0 %collective-permute-start.1 = (f32[8,128]{1,0:T(8,128)S(1)}, f32[8,128]{1,0:T(8,128)S(1)}, u32[]{:S(2)}, u32[]{:S(2)}) collective-permute-start(f32[8,128]{1,0:T(8,128)S(1)} %get-tuple-element.31), channel_id=1, source_target_pairs={{0,64},{32,96},{64,0},{96,32},{1,65},{33,97},{65,1},{97,33},{2,66}... | collective-permute-start | bytes 12296 | tf_op jit(solution)/shard_map/ppermute | solution.py:373
  7.6 2.8 %collective-permute-start.2 = (f32[8,128]{1,0:T(8,128)S(1)}, f32[8,128]{1,0:T(8,128)S(1)}, u32[]{:S(2)}, u32[]{:S(2)}) collective-permute-start(f32[8,128]{1,0:T(8,128)S(1)} %get-tuple-element.31), channel_id=1, source_target_pairs={{0,96},{32,0},{64,32},{96,64},{1,97},{33,1},{65,33},{97,65},{2,98}... | collective-permute-start | bytes 12296 | tf_op jit(solution)/shard_map/ppermute | solution.py:373
  11.2 25.2 %all-to-all-start = ((f32[32,4,8,128]{3,2,1,0:T(8,128)}), f32[32,4,8,128]{3,2,1,0:T(8,128)S(1)}, u32[]{:S(2)}, u32[]{:S(2)}) async-start(f32[32,4,8,128]{3,2,1,0:T(8,128)} %broadcast_in_dim.10), calls=%async_computation | async-start | bytes 1048576 | tf_op jit(solution)/shard_map/all_to_all | solution.py:376
  21.1 2.2 %copy-start = (f32[1024,1024]{1,0:T(8,128)S(1)}, f32[1024,1024]{1,0:T(8,128)}, u32[]{:S(2)}) copy-start(f32[1024,1024]{1,0:T(8,128)} %f_ref.3) | copy-start | bytes 12582916
  23.3 1.6 copy-start.2
  29.2 1.3 copy-start.4
  30.5 1.3 copy-start.5
  31.8 1.0 copy-start.7
  32.8 1.0 copy-start.8
  33.8 1.1 copy-start.9
  34.9 1.0 copy-start.10
  35.9 0.6 copy-start.14
  36.5 0.8 copy-start.15
  37.2 127.1 %copy-start.11 = (s32[6]{0:T(128)S(1)}, s32[6]{0:T(128)}, u32[]{:S(2)}) copy-start(s32[6]{0:T(128)} %stack.42.at_ref) | copy-start | bytes 76
  37.3 134.0 %copy-start.16 = (s32[4,512]{1,0:T(4,128)S(1)}, s32[4,512]{1,0:T(4,128)}, u32[]{:S(2)}) copy-start(s32[4,512]{1,0:T(4,128)} %param.8) | copy-start | bytes 24580
  37.3 134.0 %copy-start.17 = (f32[4,512]{1,0:T(4,128)S(1)}, f32[4,512]{1,0:T(4,128)}, u32[]{:S(2)}) copy-start(f32[4,512]{1,0:T(4,128)} %param.7) | copy-start | bytes 24580
  37.3 134.1 %copy-start.18 = (f32[4,256]{1,0:T(4,128)S(1)}, f32[4,256]{1,0:T(4,128)}, u32[]{:S(2)}) copy-start(f32[4,256]{1,0:T(4,128)} %param.12) | copy-start | bytes 12292
  37.3 141.7 %copy-start.3 = (f32[512,1024]{1,0:T(8,128)S(1)}, f32[512,1024]{1,0:T(8,128)}, u32[]{:S(2)}) copy-start(f32[512,1024]{1,0:T(8,128)} %h_ref.3) | copy-start | bytes 6291460
  37.3 141.7 %copy-start.12 = (f32[512]{0:T(512)S(1)}, f32[512]{0:T(512)}, u32[]{:S(2)}) copy-start(f32[512]{0:T(512)} %param.11) | copy-start | bytes 6148
  129.0 18.4 %collective-permute-start.3 = (f32[8,128]{1,0:T(8,128)}, f32[8,128]{1,0:T(8,128)S(1)}, u32[]{:S(2)}, u32[]{:S(2)}) collective-permute-start(f32[8,128]{1,0:T(8,128)} %get-tuple-element.24), channel_id=1, source_target_pairs={{0,128},{1,129},{2,130},{3,131},{4,132},{5,133},{6,134},{7,135},{8... | collective-permute-start | bytes 12296 | tf_op jit(solution)/shard_map/ppermute | solution.py:379
  149.2 15.2 %all-to-all-start.1 = ((f32[32,1,32]{2,1,0:T(1,128)}), f32[32,1,32]{2,1,0:T(1,128)S(1)}, u32[]{:S(2)}, u32[]{:S(2)}) async-start(f32[32,1,32]{2,1,0:T(1,128)} %add.45), calls=%async_computation.1 | async-start | bytes 32768 | tf_op jit(solution)/shard_map/all_to_all | solution.py:382
  164.3 1.3 copy-start.6
  167.1 11.8 %all-to-all-start.2 = ((f32[32,8,128]{2,1,0:T(8,128)}), f32[32,8,128]{2,1,0:T(8,128)S(1)}, u32[]{:S(2)}, u32[]{:S(2)}) async-start(f32[32,8,128]{2,1,0:T(8,128)} %parts.1), calls=%async_computation.2 | async-start | bytes 262144 | tf_op jit(solution)/shard_map/all_to_all | solution.py:383
  178.9 2.2 %copy-start.1 = (f32[1024,1024]{1,0:T(8,128)S(1)}, f32[1024,1024]{1,0:T(8,128)}, u32[]{:S(2)}) copy-start(f32[1024,1024]{1,0:T(8,128)} %f_ref.3) | copy-start | bytes 12582916
  181.1 0.7 copy-start.13

commit v5 on v3

--- a/solution.py
+++ b/solution.py
@@ -14,6 +14,7 @@
 BF16 = jnp.bfloat16
 VMEM = pl.BlockSpec(memory_space=pltpu.VMEM)
 SMEM = pl.BlockSpec(memory_space=pltpu.SMEM)
+ANY = pl.BlockSpec(memory_space=pl.ANY)
 
 
 def wide(row):
@@ -93,11 +94,12 @@
             hw_ref[r, c] = h_ref[r, c] * w
 
 
-def prepare(f_ref, h_ref, gp_hi, gp_lo, gy_hi, gy_lo, h_hi, h_lo, diag_ref, t_hi, t_lo):
+def prepare(f_ref, h_ref, wait_f, gp_hi, gp_lo, gy_hi, gy_lo, h_hi, h_lo, diag_ref, t_hi, t_lo):
     h_hi[...], h_lo[...] = halves(h_ref[...])
     for j in range(8):
         r = slice(128 * j, 128 * j + 128)
         t_hi[r, :], t_lo[r, :] = halves(jnp.transpose(h_ref[:, r]))
+    wait_f()
     for j in range(4):
         r = slice(256 * j, 256 * j + 256)
         ft = jnp.transpose(f_ref[:, r])
@@ -113,13 +115,20 @@
 
 
 def block_kernel(
-    at_ref, got0, got1, got2, got3, f_ref, h_ref, s_ref, weight_ref,
-    x_own, x_end, maps, map_ends, state, bits_ref, hw_ref, got_ref,
-    gp_hi, gp_lo, gy_hi, gy_lo, h_hi, h_lo, diag_ref, t_hi, t_lo,
+    at_ref, got_ref, s_ref, weight_ref, f_any, h_any,
+    x_own, x_end, maps, map_ends, state, bits_ref, hw_ref, f_ref, h_ref,
+    gp_hi, gp_lo, gy_hi, gy_lo, h_hi, h_lo, diag_ref, t_hi, t_lo, sems,
 ):
     second, own, plane, place = at_ref[0], at_ref[1], at_ref[2], at_ref[3]
-    for n, part in enumerate((got0, got1, got2, got3)):
-        got_ref[pl.ds(32 * ((plane + 4 - n) % 4), 32)] = part[...]
+    fetch_h = pltpu.make_async_copy(h_any, h_ref, sems.at[0])
+    fetch_f = pltpu.make_async_copy(f_any, f_ref, sems.at[1])
+    fetch_h.start()
+    fetch_f.start()
+    fetch_h.wait()
+
+    def at_step(k):
+        return got_ref[k % 32, (plane + 4 - k // 32) % 4]
+
 
     @pl.when(second == 0)
     def _():
@@ -127,9 +136,10 @@
         maps[...] = jnp.zeros_like(maps)
         map_ends[...] = jnp.zeros_like(map_ends)
         store_weighted(hw_ref, h_ref, weight_ref[...], diff)
+        fetch_f.wait()
 
         def group(g, x):
-            words = sum(got_ref[16 * g + j][4:8] * float(2**j) for j in range(16))
+            words = sum(at_step(16 * g + j)[4:8] * float(2**j) for j in range(16))
             store_bits(bits_ref, words, diff)
 
             def step(j, x):
@@ -140,17 +150,17 @@
                     x_own[...] = x
 
                 p = propagate(f_ref, x, diff)
-                return update(h_ref, hw_ref, bits_ref, jnp.int32(1) << j, got_ref[k][0:4], p, diff)
+                return update(h_ref, hw_ref, bits_ref, jnp.int32(1) << j, at_step(k)[0:4], p, diff)
 
             return lax.fori_loop(0, 16, step, x)
 
         x_end[...] = lax.fori_loop(0, 8, group, s_ref[...])
 
-    @pl.when(second == 1)
+    @pl.when(second != 0)
     def _():
         x_own[...] = jnp.zeros_like(x_own)
         x_end[...] = jnp.zeros_like(x_end)
-        prepare(f_ref, h_ref, gp_hi, gp_lo, gy_hi, gy_lo, h_hi, h_lo, diag_ref, t_hi, t_lo)
+        prepare(f_ref, h_ref, fetch_f.wait, gp_hi, gp_lo, gy_hi, gy_lo, h_hi, h_lo, diag_ref, t_hi, t_lo)
         unit = (
             lax.broadcasted_iota(jnp.int32, (32, 1024), 1)
             == lax.broadcasted_iota(jnp.int32, (32, 1024), 0) + 32 * place
@@ -161,18 +171,23 @@
         row = lax.broadcasted_iota(jnp.int32, (8, 512), 0)
         weight = flat(weight_ref[...])
 
-        def step(k, carry):
-            @pl.when(jnp.logical_and(k // 32 == plane % 2, k % 4 == 0))
+        early = plane < 2
+
+        def keep(k):
+            k = k - jnp.where(early, 0, 2)
+
+            @pl.when(jnp.logical_and(k >= 0, jnp.logical_and(k // 32 == plane % 2, k % 4 == 0)))
             def _():
                 q = (k % 32) // 4
-                early = plane < 2
                 maps[q, 0:32, :] = jnp.where(early, state[0:32, :], state[32:64, :])
                 maps[q, 32:40, :] = jnp.where(early, state[64:72, :], pltpu.roll(state[64:72, :], 7, 0))
 
+        def step(k, carry):
+            keep(k)
             x = state[...]
             y = product(x, gy_hi, gy_lo)
             p = product(x, gp_hi, gp_lo) + x * diag_ref[...]
-            a, b = got_ref[k], got_ref[64 + k]
+            a, b = at_step(k), at_step(62 + k)
             wa, wb = flat(a[4:8]) * weight, flat(b[4:8]) * weight
             zs = jnp.where(row == 0, flat(a[0:4]), jnp.where(row == 1, flat(b[0:4]), 0.0))
             v = jnp.concatenate(
@@ -186,7 +201,8 @@
             state[...] = p + product(v, h_hi, h_lo)
             return carry
 
-        lax.fori_loop(0, 64, step, 0)
+        lax.fori_loop(0, 62, step, 0)
+        keep(jnp.int32(62))
         map_ends[0:32, :] = state[0:32, :]
         map_ends[32:40, :] = state[64:72, :]
 
@@ -200,20 +216,22 @@
             jax.ShapeDtypeStruct((8, 40, 1024), F32),
             jax.ShapeDtypeStruct((40, 1024), F32),
         ),
-        in_specs=[SMEM] + [VMEM] * 8,
+        in_specs=[SMEM] + [VMEM] * 3 + [ANY] * 2,
         out_specs=(VMEM,) * 4,
         scratch_shapes=[
             pltpu.VMEM((72, 1024), F32),
             pltpu.VMEM((512, 128), jnp.int32),
             pltpu.VMEM((512, 1024), F32),
-            pltpu.VMEM((128, 8, 128), F32),
+            pltpu.VMEM((1024, 1024), F32),
+            pltpu.VMEM((512, 1024), F32),
             *[pltpu.VMEM((1024, 1024), BF16)] * 2,
             *[pltpu.VMEM((1024, 512), BF16)] * 2,
             *[pltpu.VMEM((512, 1024), BF16)] * 2,
             pltpu.VMEM((1, 1024), F32),
             *[pltpu.VMEM((1024, 512), BF16)] * 2,
+            pltpu.SemaphoreType.DMA((2,)),
         ],
-        compiler_params=pltpu.CompilerParams(vmem_limit_bytes=36 * 2**20),
+        compiler_params=pltpu.CompilerParams(vmem_limit_bytes=58 * 2**20),
         name="blocks",
     )(*args)
 
@@ -238,6 +256,7 @@
         out_shape=jax.ShapeDtypeStruct((32, 8, 128), F32),
         in_specs=[SMEM] + [VMEM] * 3,
         out_specs=VMEM,
+        compiler_params=pltpu.CompilerParams(vmem_limit_bytes=6 * 2**20),
         name="parts",
     )(*args)
 
@@ -295,7 +314,7 @@
             pltpu.VMEM((4, 8, 128), F32),
             pltpu.VMEM((4, 8, 128), F32),
         ],
-        compiler_params=pltpu.CompilerParams(vmem_limit_bytes=20 * 2**20),
+        compiler_params=pltpu.CompilerParams(vmem_limit_bytes=12 * 2**20),
         name="own_steps",
     )(*args)
 
@@ -325,6 +344,7 @@
         out_shape=(jax.ShapeDtypeStruct((4, 256), F32),) * 2,
         in_specs=[SMEM] + [VMEM] * 4,
         out_specs=(VMEM, VMEM),
+        compiler_params=pltpu.CompilerParams(vmem_limit_bytes=4 * 2**20),
         name="smooth_own",
     )(*args)
 
@@ -337,11 +357,12 @@
     flags = jnp.stack([h_at, 4 * (at % 32), l_at, place, y, at]).astype(jnp.int32)
     own_z = lax.dynamic_slice_in_dim(z, y, 1, 0).reshape(4, 128)
     own_m = lax.dynamic_slice_in_dim(mask, y, 1, 0).astype(F32).reshape(4, 128)
-    own = jnp.broadcast_to(jnp.concatenate([own_z, own_m], 0)[None], (32, 8, 128))
+    own = jnp.concatenate([own_z, own_m], 0)
+    turned = [lax.ppermute(own, "l", [(i, (i + n) % 4) for i in range(4)]) for n in (1, 2, 3)]
+    own = jnp.broadcast_to(jnp.stack([own, *turned])[None], (32, 4, 8, 128))
     got = lax.all_to_all(own, PLANE, 0, 0, tiled=True)
-    turned = [got] + [lax.ppermute(got, "l", [(i, (i + n) % 4) for i in range(4)]) for n in (1, 2, 3)]
     weight = weight.reshape(4, 128)
-    x_own, x_end, maps, ends = run_blocks(flags, *turned, f, h, prior.reshape(8, 128), weight)
+    x_own, x_end, maps, ends = run_blocks(flags, got, prior.reshape(8, 128), weight, f, h)
     s1 = lax.ppermute(x_end, "h", [(0, 1)]).reshape(32, 32)
     s1 = lax.dynamic_slice_in_dim(s1, place, 1, 0)
     part = jnp.sum(s1.reshape(32, 1) * ends[:32], 0) + jnp.where(place == 0, ends[32], 0.0)

time: 207 us -> 201 us (0.971)
  blocking collectives: 37.8 us -> 20.8 us
  starting transfers between devices: 38.1 us -> 43 us
  Pallas kernels: 94.1 us -> 98.1 us
  waiting for transfers between devices: 23.2 us -> 27 us
  local copies, waits for them, and re-layouts: 11.3 us -> 7.54 us
    all_to_all x1 -> x0, blocking collectives: 16 us -> none  [body(): got = lax.all_to_all(own, PLANE, 0, 0, tiled=True)]
    all_to_all x0 -> x1, waiting for transfers between devices: none -> 10.3 us  [body(): got = lax.all_to_all(own, PLANE, 0, 0, tiled=True)]
    all_to_all x0 -> x1, starting transfers between devices: none -> 9.18 us  [body(): got = lax.all_to_all(own, PLANE, 0, 0, tiled=True)]
    ppermute x3, waiting for transfers between devices: 8.48 us -> 2.02 us  [body(): lax.ppermute(own, 'l', [(i, (i + n) % 4) for i in range(4)])]
    ppermute x1, starting transfers between devices: 23.4 us -> 18 us  [body(): s1 = lax.ppermute(x_end, 'h', [(0, 1)]).reshape(32, 32)]
    pallas_call x1, Pallas kernels: 86.1 us -> 91.3 us  [run_blocks(): pl.pallas_call(block_kernel, out_shape=(jax.ShapeDtypeStruct((8, 128), F3...]
    unnamed x34 -> x20, local copies, waits for them, and re-layouts: 9.65 us -> 5.02 us
  transfers between devices with their start and end apart: 6 -> 7, of which waited for: 5 -> 6; matrix products, arithmetic and copies ran while one was open for 0% -> 1% of each run, Pallas kernels for 0% -> 0%
where the time goes in v5:
time: 201 us; the launch traced here: 200 us
  Pallas kernels  98.1 us (49%)
  starting transfers between devices  43 us (21%)
  waiting for transfers between devices  27 us (13%)
  blocking collectives  20.8 us (10%)
  local copies, waits for them, and re-layouts  7.54 us (4%)
  other arithmetic  3.1 us (2%)
    pallas_call x1, Pallas kernels, run_blocks(): pl.pallas_call(block_kernel, out_shape=(jax.ShapeDtypeStruct((8, 128), F3...  91.3 us
    all_to_all x1, blocking collectives, body(): elements = lax.all_to_all(element, TIME, 0, 0, tiled=True)  20.8 us
    ppermute x1, starting transfers between devices, body(): s1 = lax.ppermute(x_end, 'h', [(0, 1)]).reshape(32, 32)  18 us
    all_to_all x1, waiting for transfers between devices, body(): got = lax.all_to_all(own, PLANE, 0, 0, tiled=True)  10.3 us
    all_to_all x1, starting transfers between devices, body(): got = lax.all_to_all(own, PLANE, 0, 0, tiled=True)  9.18 us
    all_to_all x1, waiting for transfers between devices, body(): lax.all_to_all(run_parts(flags, s1, s2, maps), PLANE, 0, 0, tiled=True)  7.58 us
    all_to_all x1, waiting for transfers between devices, body(): s2 = lax.all_to_all(part.reshape(32, 32), PLANE, 0, 0, tiled=True)  6.91 us
    ppermute x3, starting transfers between devices, body(): lax.ppermute(own, 'l', [(i, (i + n) % 4) for i in range(4)])  6.26 us
  transfers between devices with their start and end apart: 7, of which 6 were waited for; matrix products, arithmetic and copies ran while one was open for 1% of the time, Pallas kernels for 0%

profile of v5, /device:TPU:1, one launch (start us, length us, event | category | flops | bytes accessed | tf_op | source)
XLA Modules:
  0.0 200.4 jit_solution(1168463346786751890)
XLA Ops:
  0.6 0.7 constant_dynamic-slice_fusion.1
  1.3 0.7 dynamic-slice_convert_fusion
  2.1 2.5 %collective-permute-start = (f32[8,128]{1,0:T(8,128)S(1)}, f32[8,128]{1,0:T(8,128)S(1)}, u32[]{:S(2)}, u32[]{:S(2)}) collective-permute-start(f32[8,128]{1,0:T(8,128)S(1)} %get-tuple-element.17), channel_id=1, source_target_pairs={{0,32},{32,64},{64,96},{96,0},{1,33},{33,65},{65,97},{97,1},{2,34}... | collective-permute-start | bytes 12296 | tf_op jit(solution)/shard_map/ppermute | solution.py:361
  4.6 3.0 %collective-permute-start.1 = (f32[8,128]{1,0:T(8,128)S(1)}, f32[8,128]{1,0:T(8,128)S(1)}, u32[]{:S(2)}, u32[]{:S(2)}) collective-permute-start(f32[8,128]{1,0:T(8,128)S(1)} %get-tuple-element.17), channel_id=1, source_target_pairs={{0,64},{32,96},{64,0},{96,32},{1,65},{33,97},{65,1},{97,33},{2,66}... | collective-permute-start | bytes 12296 | tf_op jit(solution)/shard_map/ppermute | solution.py:361
  7.6 0.7 collective-permute-start.2
  8.3 0.0 collective-permute-done
  8.3 0.3 collective-permute-done.1
  8.6 1.8 collective-permute-done.2
  10.3 0.9 broadcast_in_dim.10
  11.2 9.2 %all-to-all-start = ((f32[32,4,8,128]{3,2,1,0:T(8,128)}), f32[32,4,8,128]{3,2,1,0:T(8,128)S(1)}, u32[]{:S(2)}, u32[]{:S(2)}) async-start(f32[32,4,8,128]{3,2,1,0:T(8,128)} %broadcast_in_dim.10), calls=%async_computation | async-start | bytes 1048576 | tf_op jit(solution)/shard_map/all_to_all | solution.py:363
  20.4 0.7 stack.42.at_ref
  21.1 10.3 %all-to-all-done.got_ref = f32[32,4,8,128]{3,2,1,0:T(8,128)S(1)} async-done(((f32[32,4,8,128]{3,2,1,0:T(8,128)}), f32[32,4,8,128]{3,2,1,0:T(8,128)S(1)}, u32[]{:S(2)}, u32[]{:S(2)}) %all-to-all-start) | async-done | bytes 524320 | tf_op jit(solution)/shard_map/all_to_all | solution.py:363
  31.4 0.0 copy-start.6
  31.4 0.8 copy-done.6
  32.2 0.0 copy-start.3
  32.2 0.0 copy-start.7
  32.2 0.0 copy-start.8
  32.2 0.0 copy-start.9
  32.2 0.0 copy-start.1
  32.2 0.0 copy-start.4
  32.3 91.3 %blocks.1 = (f32[8,128]{1,0:T(8,128)}, f32[8,128]{1,0:T(8,128)}, f32[8,40,1024]{2,1,0:T(8,128)}, f32[40,1024]{1,0:T(8,128)}) custom-call(s32[6]{0:T(128)} %stack.42.at_ref, f32[32,4,8,128]{3,2,1,0:T(8,128)} %copy-done.6, f32[8,128]{1,0:T(8,128)} %bitcast.28, f32[4,128]{1,0:T(4,128)} %bitcast.20, f32[1024,1024]{1,0:T(8,128)} %f_ref.1, f32[512,1024]{1,0:T(8,128)} %h_ref.1), custom_call_target="tpu_custom_call" | custom-call | tf_op jit(solution)/shard_map/blocks/pallas_call | solution.py:211
  123.6 18.0 %collective-permute-start.3 = (f32[8,128]{1,0:T(8,128)}, f32[8,128]{1,0:T(8,128)S(1)}, u32[]{:S(2)}, u32[]{:S(2)}) collective-permute-start(f32[8,128]{1,0:T(8,128)} %get-tuple-element.10), channel_id=1, source_target_pairs={{0,128},{1,129},{2,130},{3,131},{4,132},{5,133},{6,134},{7,135},{8... | collective-permute-start | bytes 12296 | tf_op jit(solution)/shard_map/ppermute | solution.py:366
  141.6 0.8 fusion
  142.4 0.1 select_n.38
  142.5 0.1 collective-permute-done.3
  142.6 0.1 reshape.66
  142.7 1.0 multiply_reduce_fusion
  143.6 0.1 reduce_sum.12
  143.7 0.6 add.45
  144.4 5.4 %all-to-all-start.1 = ((f32[32,1,32]{2,1,0:T(1,128)}), f32[32,1,32]{2,1,0:T(1,128)S(1)}, u32[]{:S(2)}, u32[]{:S(2)}) async-start(f32[32,1,32]{2,1,0:T(1,128)} %add.45), calls=%async_computation.1 | async-start | bytes 32768 | tf_op jit(solution)/shard_map/all_to_all | solution.py:369
  149.8 6.9 %all-to-all-done.1 = f32[32,1,32]{2,1,0:T(1,128)S(1)} async-done(((f32[32,1,32]{2,1,0:T(1,128)}), f32[32,1,32]{2,1,0:T(1,128)S(1)}, u32[]{:S(2)}, u32[]{:S(2)}) %all-to-all-start.1) | async-done | bytes 4128 | tf_op jit(solution)/shard_map/all_to_all | solution.py:369
  156.7 0.0 copy-done.3
  156.7 0.0 copy-start.2
  156.7 1.3 copy-done.2
  158.0 1.4 parts.1
  159.4 4.2 %all-to-all-start.2 = ((f32[32,8,128]{2,1,0:T(8,128)}), f32[32,8,128]{2,1,0:T(8,128)S(1)}, u32[]{:S(2)}, u32[]{:S(2)}) async-start(f32[32,8,128]{2,1,0:T(8,128)} %parts.1), calls=%async_computation.2 | async-start | bytes 262144 | tf_op jit(solution)/shard_map/all_to_all | solution.py:370
  163.6 0.0 copy-done.7
  163.6 0.0 copy-done.8
  163.6 0.0 copy-done.9
  163.7 7.6 %all-to-all-done.2.got_ref = f32[32,8,128]{2,1,0:T(8,128)S(1)} async-done(((f32[32,8,128]{2,1,0:T(8,128)}), f32[32,8,128]{2,1,0:T(8,128)S(1)}, u32[]{:S(2)}, u32[]{:S(2)}) %all-to-all-start.2) | async-done | bytes 131104 | tf_op jit(solution)/shard_map/all_to_all | solution.py:370
  171.3 0.0 copy-done.1
  171.3 0.0 copy-done.4
  171.3 0.0 copy-start
  171.3 2.2 %copy-done = f32[1024,1024]{1,0:T(8,128)S(1)} copy-done((f32[1024,1024]{1,0:T(8,128)S(1)}, f32[1024,1024]{1,0:T(8,128)}, u32[]{:S(2)}) %copy-start) | copy-done | bytes 4194328
  173.5 0.7 copy-done.5
  174.1 3.8 %own_steps.1 = (f32[4,2,128]{2,1,0:T(2,128)S(1)}, f32[4,2,128]{2,1,0:T(2,128)S(1)}, f32[64,4,128]{2,1,0:T(4,128)S(1)}) custom-call(s32[6]{0:T(128)S(1)} %copy-done.3, f32[4,4,128]{2,1,0:T(4,128)S(1)} %reshape.59.z_ref, f32[4,4,128]{2,1,0:T(4,128)S(1)} %reshape.60.m_ref, f32[1024,1024]{1,0:T(8,128)S(1)} %copy-done, f32[512,1024]{1,0:T(8,128)S(1)} %copy-done.1, ...), custom_call_target="tpu_custom_call" | custom-call | tf_op jit(solution)/shard_map/own_steps/pallas_call | solution.py:302
  178.0 20.8 %all_to_all.23.parts_ref = f32[64,4,128]{2,1,0:T(4,128)S(1)} all-to-all(f32[64,4,128]{2,1,0:T(4,128)S(1)} %get-tuple-element.13), channel_id=1, replica_groups=mesh['h'=2,'l'=4,'x'=4,'c'=2,'y'=4] {'h','l','x','c'}, dimensions={0} | all-to-all | bytes 262144 | tf_op jit(solution)/shard_map/all_to_all | solution.py:375
  198.8 1.6 smooth_own.1
  (9 shorter events, 0.1 us)
Async XLA Ops:
  2.1 6.3 %collective-permute-start = (f32[8,128]{1,0:T(8,128)S(1)}, f32[8,128]{1,0:T(8,128)S(1)}, u32[]{:S(2)}, u32[]{:S(2)}) collective-permute-start(f32[8,128]{1,0:T(8,128)S(1)} %get-tuple-element.17), channel_id=1, source_target_pairs={{0,32},{32,64},{64,96},{96,0},{1,33},{33,65},{65,97},{97,1},{2,34}... | collective-permute-start | bytes 12296 | tf_op jit(solution)/shard_map/ppermute | solution.py:361
  4.6 4.0 %collective-permute-start.1 = (f32[8,128]{1,0:T(8,128)S(1)}, f32[8,128]{1,0:T(8,128)S(1)}, u32[]{:S(2)}, u32[]{:S(2)}) collective-permute-start(f32[8,128]{1,0:T(8,128)S(1)} %get-tuple-element.17), channel_id=1, source_target_pairs={{0,64},{32,96},{64,0},{96,32},{1,65},{33,97},{65,1},{97,33},{2,66}... | collective-permute-start | bytes 12296 | tf_op jit(solution)/shard_map/ppermute | solution.py:361
  7.6 2.8 %collective-permute-start.2 = (f32[8,128]{1,0:T(8,128)S(1)}, f32[8,128]{1,0:T(8,128)S(1)}, u32[]{:S(2)}, u32[]{:S(2)}) collective-permute-start(f32[8,128]{1,0:T(8,128)S(1)} %get-tuple-element.17), channel_id=1, source_target_pairs={{0,96},{32,0},{64,32},{96,64},{1,97},{33,1},{65,33},{97,65},{2,98}... | collective-permute-start | bytes 12296 | tf_op jit(solution)/shard_map/ppermute | solution.py:361
  11.2 20.2 %all-to-all-start = ((f32[32,4,8,128]{3,2,1,0:T(8,128)}), f32[32,4,8,128]{3,2,1,0:T(8,128)S(1)}, u32[]{:S(2)}, u32[]{:S(2)}) async-start(f32[32,4,8,128]{3,2,1,0:T(8,128)} %broadcast_in_dim.10), calls=%async_computation | async-start | bytes 1048576 | tf_op jit(solution)/shard_map/all_to_all | solution.py:363
  31.4 0.8 copy-start.6
  32.2 124.4 %copy-start.3 = (s32[6]{0:T(128)S(1)}, s32[6]{0:T(128)}, u32[]{:S(2)}) copy-start(s32[6]{0:T(128)} %stack.42.at_ref) | copy-start | bytes 76
  32.2 131.4 %copy-start.7 = (s32[4,512]{1,0:T(4,128)S(1)}, s32[4,512]{1,0:T(4,128)}, u32[]{:S(2)}) copy-start(s32[4,512]{1,0:T(4,128)} %param.8) | copy-start | bytes 24580
  32.2 131.4 %copy-start.8 = (f32[4,512]{1,0:T(4,128)S(1)}, f32[4,512]{1,0:T(4,128)}, u32[]{:S(2)}) copy-start(f32[4,512]{1,0:T(4,128)} %param.7) | copy-start | bytes 24580
  32.2 131.4 %copy-start.9 = (f32[4,256]{1,0:T(4,128)S(1)}, f32[4,256]{1,0:T(4,128)}, u32[]{:S(2)}) copy-start(f32[4,256]{1,0:T(4,128)} %param.12) | copy-start | bytes 12292
  32.2 139.0 %copy-start.1 = (f32[512,1024]{1,0:T(8,128)S(1)}, f32[512,1024]{1,0:T(8,128)}, u32[]{:S(2)}) copy-start(f32[512,1024]{1,0:T(8,128)} %h_ref.1) | copy-start | bytes 6291460
  32.2 139.0 %copy-start.4 = (f32[512]{0:T(512)S(1)}, f32[512]{0:T(512)}, u32[]{:S(2)}) copy-start(f32[512]{0:T(512)} %param.11) | copy-start | bytes 6148
  123.6 19.0 %collective-permute-start.3 = (f32[8,128]{1,0:T(8,128)}, f32[8,128]{1,0:T(8,128)S(1)}, u32[]{:S(2)}, u32[]{:S(2)}) collective-permute-start(f32[8,128]{1,0:T(8,128)} %get-tuple-element.10), channel_id=1, source_target_pairs={{0,128},{1,129},{2,130},{3,131},{4,132},{5,133},{6,134},{7,135},{8... | collective-permute-start | bytes 12296 | tf_op jit(solution)/shard_map/ppermute | solution.py:366
  144.4 12.3 %all-to-all-start.1 = ((f32[32,1,32]{2,1,0:T(1,128)}), f32[32,1,32]{2,1,0:T(1,128)S(1)}, u32[]{:S(2)}, u32[]{:S(2)}) async-start(f32[32,1,32]{2,1,0:T(1,128)} %add.45), calls=%async_computation.1 | async-start | bytes 32768 | tf_op jit(solution)/shard_map/all_to_all | solution.py:369
  156.7 1.3 copy-start.2
  159.4 11.8 %all-to-all-start.2 = ((f32[32,8,128]{2,1,0:T(8,128)}), f32[32,8,128]{2,1,0:T(8,128)S(1)}, u32[]{:S(2)}, u32[]{:S(2)}) async-start(f32[32,8,128]{2,1,0:T(8,128)} %parts.1), calls=%async_computation.2 | async-start | bytes 262144 | tf_op jit(solution)/shard_map/all_to_all | solution.py:370
  171.3 2.2 %copy-start = (f32[1024,1024]{1,0:T(8,128)S(1)}, f32[1024,1024]{1,0:T(8,128)}, u32[]{:S(2)}) copy-start(f32[1024,1024]{1,0:T(8,128)} %f_ref.1) | copy-start | bytes 12582916
  173.5 0.7 copy-start.5

commit v6 on v4

--- a/solution.py
+++ b/solution.py
@@ -94,34 +94,63 @@
             hw_ref[r, c] = h_ref[r, c] * w
 
 
-def prepare_kernel(f_ref, h_ref, gp_hi, gp_lo, gy_hi, gy_lo, h_hi, h_lo, diag_ref, t_hi, t_lo):
-    h_hi[...], h_lo[...] = halves(h_ref[...])
+def prepare_kernel(
+    f_any, h_any, gy_hi, gy_lo, gx_hi, gx_lo, diag_ref,
+    f_ref, h_ref, y_hi, y_lo, x_hi, x_lo, t_hi, t_lo, in_sems, out_sems,
+):
+    fetch_h = pltpu.make_async_copy(h_any, h_ref, in_sems.at[0])
+    fetch_f = pltpu.make_async_copy(f_any, f_ref, in_sems.at[1])
+    fetch_h.start()
+    fetch_f.start()
+    fetch_h.wait()
+    sent = []
+
+    def send(source, target, r):
+        copy = pltpu.make_async_copy(source.at[r], target.at[r], out_sems.at[len(sent)])
+        copy.start()
+        sent.append(copy)
+
+    low = pl.ds(1024, 512)
+    x_hi[low, :], x_lo[low, :] = halves(h_ref[...])
+    send(x_hi, gx_hi, low)
+    send(x_lo, gx_lo, low)
     for j in range(8):
         r = slice(128 * j, 128 * j + 128)
         t_hi[r, :], t_lo[r, :] = halves(jnp.transpose(h_ref[:, r]))
+    fetch_f.wait()
     for j in range(4):
         r = slice(256 * j, 256 * j + 256)
         ft = jnp.transpose(f_ref[:, r])
         row = lax.broadcasted_iota(jnp.int32, ft.shape, 0) + 256 * j
         on = row == lax.broadcasted_iota(jnp.int32, ft.shape, 1)
-        gy_hi[r, :], gy_lo[r, :] = halves(product(ft, t_hi, t_lo))
-        gp_hi[r, :], gp_lo[r, :] = halves(jnp.where(on, 0.0, ft))
+        x_hi[r, :], x_lo[r, :] = halves(jnp.where(on, 0.0, ft))
         diag_ref[:, r] = jnp.sum(jnp.where(on, ft, 0.0), axis=0, keepdims=True)[:, r]
+        block = pl.ds(256 * j, 256)
+        send(x_hi, gx_hi, block)
+        send(x_lo, gx_lo, block)
+        y_hi[r, :], y_lo[r, :] = halves(product(ft, t_hi, t_lo))
+        send(y_hi, gy_hi, block)
+        send(y_lo, gy_lo, block)
+    for copy in sent:
+        copy.wait()
 
 
 def prepare(f, h):
+    outs = [((1024, 512), BF16)] * 2 + [((1536, 1024), BF16)] * 2
     return pl.pallas_call(
         prepare_kernel,
-        out_shape=(
-            *[jax.ShapeDtypeStruct((1024, 1024), BF16)] * 2,
-            *[jax.ShapeDtypeStruct((1024, 512), BF16)] * 2,
-            *[jax.ShapeDtypeStruct((512, 1024), BF16)] * 2,
-            jax.ShapeDtypeStruct((1, 1024), F32),
-        ),
-        in_specs=[VMEM] * 2,
-        out_specs=(VMEM,) * 7,
-        scratch_shapes=[pltpu.VMEM((1024, 512), BF16)] * 2,
-        compiler_params=pltpu.CompilerParams(vmem_limit_bytes=26 * 2**20),
+        out_shape=(*[jax.ShapeDtypeStruct(*o) for o in outs], jax.ShapeDtypeStruct((1, 1024), F32)),
+        in_specs=[ANY] * 2,
+        out_specs=(*[ANY] * 4, VMEM),
+        scratch_shapes=[
+            pltpu.VMEM((1024, 1024), F32),
+            pltpu.VMEM((512, 1024), F32),
+            *[pltpu.VMEM(*o) for o in outs],
+            *[pltpu.VMEM((1024, 512), BF16)] * 2,
+            pltpu.SemaphoreType.DMA((2,)),
+            pltpu.SemaphoreType.DMA((18,)),
+        ],
+        compiler_params=pltpu.CompilerParams(vmem_limit_bytes=58 * 2**20),
         cost_estimate=pl.CostEstimate(flops=3 * 2**30, bytes_accessed=14 * 2**20, transcendentals=0),
         name="prepare",
     )(f, h)
@@ -134,9 +163,9 @@
 def block_kernel(
     at_ref, got_ref, s_ref, weight_ref, diag_ref, f_any, h_any, *rest,
 ):
-    mats_any, (x_own, x_end, maps, map_ends), rest = rest[:6], rest[6:10], rest[10:]
+    mats_any, (x_own, x_end, maps, map_ends), rest = rest[:4], rest[4:8], rest[8:]
     state, bits_ref, hw_ref, f_ref, h_ref, *mats, sems = rest
-    gp_hi, gp_lo, gy_hi, gy_lo, h_hi, h_lo = mats
+    gy_hi, gy_lo, gx_hi, gx_lo = mats
     second, own, plane, place = at_ref[0], at_ref[1], at_ref[2], at_ref[3]
 
     def fetch(pairs):
@@ -176,7 +205,7 @@
 
         x_end[...] = lax.fori_loop(0, 8, group, s_ref[...])
 
-    @pl.when(second == 1)
+    @pl.when(second != 0)
     def _():
         x_own[...] = jnp.zeros_like(x_own)
         x_end[...] = jnp.zeros_like(x_end)
@@ -191,18 +220,25 @@
         row = lax.broadcasted_iota(jnp.int32, (8, 512), 0)
         weight = flat(weight_ref[...])
 
-        def step(k, carry):
-            @pl.when(jnp.logical_and(k // 32 == plane % 2, k % 4 == 0))
+        early = plane < 2
+
+        def keep(k):
+            k = k - jnp.where(early, 0, 2)
+
+            @pl.when(jnp.logical_and(k >= 0, jnp.logical_and(k // 32 == plane % 2, k % 4 == 0)))
             def _():
                 q = (k % 32) // 4
-                early = plane < 2
                 maps[q, 0:32, :] = jnp.where(early, state[0:32, :], state[32:64, :])
                 maps[q, 32:40, :] = jnp.where(early, state[64:72, :], pltpu.roll(state[64:72, :], 7, 0))
 
+        def step(k, carry):
+            keep(k)
             x = state[...]
-            y = product(x, gy_hi, gy_lo)
-            p = product(x, gp_hi, gp_lo) + x * diag_ref[...]
-            a, b = at_step(k), at_step(64 + k)
+            hi, lo = halves(x)
+            both = jnp.concatenate([hi, lo], 0)
+            y = jnp.dot(both, gy_hi[...], preferred_element_type=F32)
+            y = y[:72] + y[72:] + jnp.dot(hi, gy_lo[...], preferred_element_type=F32)
+            a, b = at_step(k), at_step(62 + k)
             wa, wb = flat(a[4:8]) * weight, flat(b[4:8]) * weight
             zs = jnp.where(row == 0, flat(a[0:4]), jnp.where(row == 1, flat(b[0:4]), 0.0))
             v = jnp.concatenate(
@@ -213,10 +249,18 @@
                 ],
                 0,
             )
-            state[...] = p + product(v, h_hi, h_lo)
+            v_hi, v_lo = halves(v)
+            both = jnp.concatenate([both, jnp.concatenate([v_hi, v_lo], 0)], 1)
+            hi = jnp.concatenate([hi, v_hi], 1)
+            for j in range(4):
+                r = slice(256 * j, 256 * j + 256)
+                out = jnp.dot(both, gx_hi[:, r], preferred_element_type=F32)
+                out = out[:72] + out[72:] + jnp.dot(hi, gx_lo[:, r], preferred_element_type=F32)
+                state[:, r] = out + x[:, r] * diag_ref[:, r]
             return carry
 
-        lax.fori_loop(0, 64, step, 0)
+        lax.fori_loop(0, 62, step, 0)
+        keep(jnp.int32(62))
         map_ends[0:32, :] = state[0:32, :]
         map_ends[32:40, :] = state[64:72, :]
 
@@ -230,7 +274,7 @@
             jax.ShapeDtypeStruct((8, 40, 1024), F32),
             jax.ShapeDtypeStruct((40, 1024), F32),
         ),
-        in_specs=[SMEM] + [VMEM] * 4 + [ANY] * 8,
+        in_specs=[SMEM] + [VMEM] * 4 + [ANY] * 6,
         out_specs=(VMEM,) * 4,
         scratch_shapes=[
             pltpu.VMEM((72, 1024), F32),
@@ -238,10 +282,9 @@
             pltpu.VMEM((512, 1024), F32),
             pltpu.VMEM((1024, 1024), F32),
             pltpu.VMEM((512, 1024), F32),
-            *[pltpu.VMEM((1024, 1024), BF16)] * 2,
             *[pltpu.VMEM((1024, 512), BF16)] * 2,
-            *[pltpu.VMEM((512, 1024), BF16)] * 2,
-            pltpu.SemaphoreType.DMA((6,)),
+            *[pltpu.VMEM((1536, 1024), BF16)] * 2,
+            pltpu.SemaphoreType.DMA((4,)),
         ],
         compiler_params=pltpu.CompilerParams(vmem_limit_bytes=58 * 2**20),
         name="blocks",

time: 208 us -> 197 us (0.947)
  local copies, waits for them, and re-layouts: 18.5 us -> 7.45 us
  starting transfers between devices: 45.2 us -> 38.3 us
  Pallas kernels: 103 us -> 106 us
  waiting for transfers between devices: 16.6 us -> 19.1 us
    unnamed x38 -> x20, local copies, waits for them, and re-layouts: 16 us -> 4.99 us
    ppermute x1, starting transfers between devices: 17.4 us -> 13.1 us  [body(): s1 = lax.ppermute(x_end, 'h', [(0, 1)]).reshape(32, 32)]
    pallas_call x1, Pallas kernels: 4.35 us -> 7.91 us  [prepare(): pl.pallas_call(prepare_kernel, out_shape=(*[jax.ShapeDtypeStruct(*o) for...]
    all_to_all x1, starting transfers between devices: 8.22 us -> 5.72 us  [body(): s2 = lax.all_to_all(part.reshape(32, 32), PLANE, 0, 0, tiled=True)]
    all_to_all x1, waiting for transfers between devices: 0.01 us -> 2.5 us  [body(): got = lax.all_to_all(own, PLANE, 0, 0, tiled=True)]
  transfers between devices with their start and end apart: 7 -> 7, of which waited for: 5 -> 6; matrix products, arithmetic and copies ran while one was open for 1% -> 1% of each run, Pallas kernels for 2% -> 4%
where the time goes in v6:
time: 197 us; the launch traced here: 196 us
  Pallas kernels  106 us (54%)
  starting transfers between devices  38.3 us (19%)
  blocking collectives  20.6 us (10%)
  waiting for transfers between devices  19.1 us (10%)
  local copies, waits for them, and re-layouts  7.45 us (4%)
  other arithmetic  3.11 us (2%)
    pallas_call x1, Pallas kernels, run_blocks(): pl.pallas_call(block_kernel, out_shape=(jax.ShapeDtypeStruct((8, 128), F3...  91.7 us
    all_to_all x1, blocking collectives, body(): elements = lax.all_to_all(element, TIME, 0, 0, tiled=True)  20.6 us
    ppermute x1, starting transfers between devices, body(): s1 = lax.ppermute(x_end, 'h', [(0, 1)]).reshape(32, 32)  13.1 us
    all_to_all x1, starting transfers between devices, body(): got = lax.all_to_all(own, PLANE, 0, 0, tiled=True)  9.18 us
    pallas_call x1, Pallas kernels, prepare(): pl.pallas_call(prepare_kernel, out_shape=(*[jax.ShapeDtypeStruct(*o) for...  7.91 us
    all_to_all x1, waiting for transfers between devices, body(): lax.all_to_all(run_parts(flags, s1, s2, maps), PLANE, 0, 0, tiled=True)  7.58 us
    all_to_all x1, waiting for transfers between devices, body(): s2 = lax.all_to_all(part.reshape(32, 32), PLANE, 0, 0, tiled=True)  6.89 us
    ppermute x3, starting transfers between devices, body(): lax.ppermute(own, 'l', [(i, (i + n) % 4) for i in range(4)])  6.26 us
  transfers between devices with their start and end apart: 7, of which 6 were waited for; matrix products, arithmetic and copies ran while one was open for 1% of the time, Pallas kernels for 4%

profile of v6, /device:TPU:1, one launch (start us, length us, event | category | flops | bytes accessed | tf_op | source)
XLA Modules:
  0.0 195.9 jit_solution(145609111148266438)
XLA Ops:
  0.6 0.7 constant_dynamic-slice_fusion.1
  1.3 0.7 dynamic-slice_convert_fusion
  2.1 2.5 %collective-permute-start = (f32[8,128]{1,0:T(8,128)S(1)}, f32[8,128]{1,0:T(8,128)S(1)}, u32[]{:S(2)}, u32[]{:S(2)}) collective-permute-start(f32[8,128]{1,0:T(8,128)S(1)} %get-tuple-element.27), channel_id=1, source_target_pairs={{0,32},{32,64},{64,96},{96,0},{1,33},{33,65},{65,97},{97,1},{2,34}... | collective-permute-start | bytes 12296 | tf_op jit(solution)/shard_map/ppermute | solution.py:416
  4.6 3.0 %collective-permute-start.1 = (f32[8,128]{1,0:T(8,128)S(1)}, f32[8,128]{1,0:T(8,128)S(1)}, u32[]{:S(2)}, u32[]{:S(2)}) collective-permute-start(f32[8,128]{1,0:T(8,128)S(1)} %get-tuple-element.27), channel_id=1, source_target_pairs={{0,64},{32,96},{64,0},{96,32},{1,65},{33,97},{65,1},{97,33},{2,66}... | collective-permute-start | bytes 12296 | tf_op jit(solution)/shard_map/ppermute | solution.py:416
  7.6 0.7 collective-permute-start.2
  8.3 0.0 collective-permute-done
  8.3 0.3 collective-permute-done.1
  8.6 1.8 collective-permute-done.2
  10.3 0.9 broadcast_in_dim.10
  11.2 9.2 %all-to-all-start = ((f32[32,4,8,128]{3,2,1,0:T(8,128)}), f32[32,4,8,128]{3,2,1,0:T(8,128)S(1)}, u32[]{:S(2)}, u32[]{:S(2)}) async-start(f32[32,4,8,128]{3,2,1,0:T(8,128)} %broadcast_in_dim.10), calls=%async_computation | async-start | bytes 1048576 | tf_op jit(solution)/shard_map/all_to_all | solution.py:419
  20.4 0.6 stack.42.at_ref
  21.0 7.9 %prepare.1 = (bf16[1024,512]{1,0:T(8,128)(2,1)}, bf16[1024,512]{1,0:T(8,128)(2,1)}, bf16[1536,1024]{1,0:T(8,128)(2,1)}, bf16[1536,1024]{1,0:T(8,128)(2,1)}, f32[1,1024]{1,0:T(1,128)}) custom-call(f32[1024,1024]{1,0:T(8,128)} %f_ref.1, f32[512,1024]{1,0:T(8,128)} %h_ref.1), custom_call_target="tpu_custom_call" | custom-call | flops 3221225472 | bytes 14680064 | tf_op jit(solution)/shard_map/prepare/pallas_call | solution.py:140
  28.9 2.5 %all-to-all-done.got_ref = f32[32,4,8,128]{3,2,1,0:T(8,128)S(1)} async-done(((f32[32,4,8,128]{3,2,1,0:T(8,128)}), f32[32,4,8,128]{3,2,1,0:T(8,128)S(1)}, u32[]{:S(2)}, u32[]{:S(2)}) %all-to-all-start) | async-done | bytes 524320 | tf_op jit(solution)/shard_map/all_to_all | solution.py:419
  31.4 0.0 copy-start.6
  31.4 0.8 copy-done.6
  32.2 0.0 copy-start.3
  32.2 0.0 copy-start.7
  32.2 0.0 copy-start.8
  32.2 0.0 copy-start.1
  32.2 0.0 copy-start.4
  32.2 91.7 %blocks.1 = (f32[8,128]{1,0:T(8,128)}, f32[8,128]{1,0:T(8,128)}, f32[8,40,1024]{2,1,0:T(8,128)}, f32[40,1024]{1,0:T(8,128)}) custom-call(s32[6]{0:T(128)} %stack.42.at_ref, f32[32,4,8,128]{3,2,1,0:T(8,128)} %copy-done.6, f32[8,128]{1,0:T(8,128)} %bitcast.25, f32[4,128]{1,0:T(4,128)} %bitcast.20, f32[1,1024]{1,0:T(1,128)} %get-tuple-element.14.diag_ref, ...), custom_call_target="tpu_custom_call" | custom-call | tf_op jit(solution)/shard_map/blocks/pallas_call | solution.py:269
  124.0 13.1 %collective-permute-start.3 = (f32[8,128]{1,0:T(8,128)}, f32[8,128]{1,0:T(8,128)S(1)}, u32[]{:S(2)}, u32[]{:S(2)}) collective-permute-start(f32[8,128]{1,0:T(8,128)} %get-tuple-element.20), channel_id=1, source_target_pairs={{0,128},{1,129},{2,130},{3,131},{4,132},{5,133},{6,134},{7,135},{8... | collective-permute-start | bytes 12296 | tf_op jit(solution)/shard_map/ppermute | solution.py:422
  137.1 0.8 fusion
  137.9 0.1 select_n.38
  138.0 0.1 collective-permute-done.3
  138.1 0.1 reshape.66
  138.2 1.0 multiply_reduce_fusion
  139.2 0.1 reduce_sum.12
  139.2 0.6 add.45
  139.9 5.7 %all-to-all-start.1 = ((f32[32,1,32]{2,1,0:T(1,128)}), f32[32,1,32]{2,1,0:T(1,128)S(1)}, u32[]{:S(2)}, u32[]{:S(2)}) async-start(f32[32,1,32]{2,1,0:T(1,128)} %add.45), calls=%async_computation.1 | async-start | bytes 32768 | tf_op jit(solution)/shard_map/all_to_all | solution.py:425
  145.6 6.9 %all-to-all-done.1 = f32[32,1,32]{2,1,0:T(1,128)S(1)} async-done(((f32[32,1,32]{2,1,0:T(1,128)}), f32[32,1,32]{2,1,0:T(1,128)S(1)}, u32[]{:S(2)}, u32[]{:S(2)}) %all-to-all-start.1) | async-done | bytes 4128 | tf_op jit(solution)/shard_map/all_to_all | solution.py:425
  152.5 0.0 copy-done.3
  152.5 0.0 copy-start.2
  152.5 1.3 copy-done.2
  153.8 1.4 parts.1
  155.3 4.0 %all-to-all-start.2 = ((f32[32,8,128]{2,1,0:T(8,128)}), f32[32,8,128]{2,1,0:T(8,128)S(1)}, u32[]{:S(2)}, u32[]{:S(2)}) async-start(f32[32,8,128]{2,1,0:T(8,128)} %parts.1), calls=%async_computation.2 | async-start | bytes 262144 | tf_op jit(solution)/shard_map/all_to_all | solution.py:426
  159.3 0.0 copy-done.7
  159.3 0.0 copy-done.8
  159.4 0.0 copy-done.9
  159.4 7.6 %all-to-all-done.2.got_ref = f32[32,8,128]{2,1,0:T(8,128)S(1)} async-done(((f32[32,8,128]{2,1,0:T(8,128)}), f32[32,8,128]{2,1,0:T(8,128)S(1)}, u32[]{:S(2)}, u32[]{:S(2)}) %all-to-all-start.2) | async-done | bytes 131104 | tf_op jit(solution)/shard_map/all_to_all | solution.py:426
  167.0 0.0 copy-done.1
  167.0 0.0 copy-done.4
  167.0 0.0 copy-start
  167.0 2.2 %copy-done = f32[1024,1024]{1,0:T(8,128)S(1)} copy-done((f32[1024,1024]{1,0:T(8,128)S(1)}, f32[1024,1024]{1,0:T(8,128)}, u32[]{:S(2)}) %copy-start) | copy-done | bytes 4194328
  169.2 0.7 copy-done.5
  169.9 3.8 %own_steps.1 = (f32[4,2,128]{2,1,0:T(2,128)S(1)}, f32[4,2,128]{2,1,0:T(2,128)S(1)}, f32[64,4,128]{2,1,0:T(4,128)S(1)}) custom-call(s32[6]{0:T(128)S(1)} %copy-done.3, f32[4,4,128]{2,1,0:T(4,128)S(1)} %reshape.59.z_ref, f32[4,4,128]{2,1,0:T(4,128)S(1)} %reshape.60.m_ref, f32[1024,1024]{1,0:T(8,128)S(1)} %copy-done, f32[512,1024]{1,0:T(8,128)S(1)} %copy-done.1, ...), custom_call_target="tpu_custom_call" | custom-call | tf_op jit(solution)/shard_map/own_steps/pallas_call | solution.py:357
  173.7 20.6 %all_to_all.23.parts_ref = f32[64,4,128]{2,1,0:T(4,128)S(1)} all-to-all(f32[64,4,128]{2,1,0:T(4,128)S(1)} %get-tuple-element.23), channel_id=1, replica_groups=mesh['h'=2,'l'=4,'x'=4,'c'=2,'y'=4] {'h','l','x','c'}, dimensions={0} | all-to-all | bytes 262144 | tf_op jit(solution)/shard_map/all_to_all | solution.py:431
  194.3 1.6 smooth_own.1
  (10 shorter events, 0.1 us)
Async XLA Ops:
  2.1 6.3 %collective-permute-start = (f32[8,128]{1,0:T(8,128)S(1)}, f32[8,128]{1,0:T(8,128)S(1)}, u32[]{:S(2)}, u32[]{:S(2)}) collective-permute-start(f32[8,128]{1,0:T(8,128)S(1)} %get-tuple-element.27), channel_id=1, source_target_pairs={{0,32},{32,64},{64,96},{96,0},{1,33},{33,65},{65,97},{97,1},{2,34}... | collective-permute-start | bytes 12296 | tf_op jit(solution)/shard_map/ppermute | solution.py:416
  4.6 4.0 %collective-permute-start.1 = (f32[8,128]{1,0:T(8,128)S(1)}, f32[8,128]{1,0:T(8,128)S(1)}, u32[]{:S(2)}, u32[]{:S(2)}) collective-permute-start(f32[8,128]{1,0:T(8,128)S(1)} %get-tuple-element.27), channel_id=1, source_target_pairs={{0,64},{32,96},{64,0},{96,32},{1,65},{33,97},{65,1},{97,33},{2,66}... | collective-permute-start | bytes 12296 | tf_op jit(solution)/shard_map/ppermute | solution.py:416
  7.6 2.8 %collective-permute-start.2 = (f32[8,128]{1,0:T(8,128)S(1)}, f32[8,128]{1,0:T(8,128)S(1)}, u32[]{:S(2)}, u32[]{:S(2)}) collective-permute-start(f32[8,128]{1,0:T(8,128)S(1)} %get-tuple-element.27), channel_id=1, source_target_pairs={{0,96},{32,0},{64,32},{96,64},{1,97},{33,1},{65,33},{97,65},{2,98}... | collective-permute-start | bytes 12296 | tf_op jit(solution)/shard_map/ppermute | solution.py:416
  11.2 20.2 %all-to-all-start = ((f32[32,4,8,128]{3,2,1,0:T(8,128)}), f32[32,4,8,128]{3,2,1,0:T(8,128)S(1)}, u32[]{:S(2)}, u32[]{:S(2)}) async-start(f32[32,4,8,128]{3,2,1,0:T(8,128)} %broadcast_in_dim.10), calls=%async_computation | async-start | bytes 1048576 | tf_op jit(solution)/shard_map/all_to_all | solution.py:419
  31.4 0.8 copy-start.6
  32.2 120.3 %copy-start.3 = (s32[6]{0:T(128)S(1)}, s32[6]{0:T(128)}, u32[]{:S(2)}) copy-start(s32[6]{0:T(128)} %stack.42.at_ref) | copy-start | bytes 76
  32.2 127.1 %copy-start.7 = (s32[4,512]{1,0:T(4,128)S(1)}, s32[4,512]{1,0:T(4,128)}, u32[]{:S(2)}) copy-start(s32[4,512]{1,0:T(4,128)} %param.8) | copy-start | bytes 24580
  32.2 127.1 %copy-start.8 = (f32[4,512]{1,0:T(4,128)S(1)}, f32[4,512]{1,0:T(4,128)}, u32[]{:S(2)}) copy-start(f32[4,512]{1,0:T(4,128)} %param.7) | copy-start | bytes 24580
  32.2 127.1 %copy-start.9 = (f32[4,256]{1,0:T(4,128)S(1)}, f32[4,256]{1,0:T(4,128)}, u32[]{:S(2)}) copy-start(f32[4,256]{1,0:T(4,128)} %param.12) | copy-start | bytes 12292
  32.2 134.8 %copy-start.1 = (f32[512,1024]{1,0:T(8,128)S(1)}, f32[512,1024]{1,0:T(8,128)}, u32[]{:S(2)}) copy-start(f32[512,1024]{1,0:T(8,128)} %h_ref.1) | copy-start | bytes 6291460
  32.2 134.8 %copy-start.4 = (f32[512]{0:T(512)S(1)}, f32[512]{0:T(512)}, u32[]{:S(2)}) copy-start(f32[512]{0:T(512)} %param.11) | copy-start | bytes 6148
  124.0 14.1 %collective-permute-start.3 = (f32[8,128]{1,0:T(8,128)}, f32[8,128]{1,0:T(8,128)S(1)}, u32[]{:S(2)}, u32[]{:S(2)}) collective-permute-start(f32[8,128]{1,0:T(8,128)} %get-tuple-element.20), channel_id=1, source_target_pairs={{0,128},{1,129},{2,130},{3,131},{4,132},{5,133},{6,134},{7,135},{8... | collective-permute-start | bytes 12296 | tf_op jit(solution)/shard_map/ppermute | solution.py:422
  139.9 12.6 %all-to-all-start.1 = ((f32[32,1,32]{2,1,0:T(1,128)}), f32[32,1,32]{2,1,0:T(1,128)S(1)}, u32[]{:S(2)}, u32[]{:S(2)}) async-start(f32[32,1,32]{2,1,0:T(1,128)} %add.45), calls=%async_computation.1 | async-start | bytes 32768 | tf_op jit(solution)/shard_map/all_to_all | solution.py:425
  152.5 1.3 copy-start.2
  155.3 11.7 %all-to-all-start.2 = ((f32[32,8,128]{2,1,0:T(8,128)}), f32[32,8,128]{2,1,0:T(8,128)S(1)}, u32[]{:S(2)}, u32[]{:S(2)}) async-start(f32[32,8,128]{2,1,0:T(8,128)} %parts.1), calls=%async_computation.2 | async-start | bytes 262144 | tf_op jit(solution)/shard_map/all_to_all | solution.py:426
  167.0 2.2 %copy-start = (f32[1024,1024]{1,0:T(8,128)S(1)}, f32[1024,1024]{1,0:T(8,128)}, u32[]{:S(2)}) copy-start(f32[1024,1024]{1,0:T(8,128)} %f_ref.1) | copy-start | bytes 12582916
  169.2 0.7 copy-start.5

commit v7 on v6

--- a/solution.py
+++ b/solution.py
@@ -317,12 +317,18 @@
 
 
 def own_kernel(
-    at_ref, z_ref, m_ref, f_ref, h_ref, weight_ref, d_ref, x_own, got_ref,
-    x_out, f_out, e_out, bits_ref, hw_ref, xs, fs,
+    at_ref, z_ref, m_ref, f_any, h_any, weight_ref, d_ref, x_own, got_ref,
+    x_out, f_out, e_out, bits_ref, hw_ref, xs, fs, f_ref, h_ref, sems,
 ):
+    fetch_h = pltpu.make_async_copy(h_any, h_ref, sems.at[0])
+    fetch_f = pltpu.make_async_copy(f_any, f_ref, sems.at[1])
+    fetch_h.start()
+    fetch_f.start()
     diff = spread_index()
+    store_bits(bits_ref, sum(m_ref[j] * float(2**j) for j in range(4)), diff)
+    fetch_h.wait()
     store_weighted(hw_ref, h_ref, weight_ref[...], diff)
-    store_bits(bits_ref, sum(m_ref[j] * float(2**j) for j in range(4)), diff)
+    fetch_f.wait()
 
     def step(k, x):
         p = propagate(f_ref, x, diff)
@@ -361,15 +367,18 @@
             jax.ShapeDtypeStruct((4, 2, 128), F32),
             jax.ShapeDtypeStruct((64, 4, 128), F32),
         ),
-        in_specs=[SMEM] + [VMEM] * 8,
+        in_specs=[SMEM] + [VMEM] * 2 + [ANY] * 2 + [VMEM] * 4,
         out_specs=(VMEM,) * 3,
         scratch_shapes=[
             pltpu.VMEM((512, 128), jnp.int32),
             pltpu.VMEM((512, 1024), F32),
             pltpu.VMEM((4, 8, 128), F32),
             pltpu.VMEM((4, 8, 128), F32),
+            pltpu.VMEM((1024, 1024), F32),
+            pltpu.VMEM((512, 1024), F32),
+            pltpu.SemaphoreType.DMA((2,)),
         ],
-        compiler_params=pltpu.CompilerParams(vmem_limit_bytes=12 * 2**20),
+        compiler_params=pltpu.CompilerParams(vmem_limit_bytes=58 * 2**20),
         name="own_steps",
     )(*args)
 

time: 197 us -> 199 us (1.010)
  Pallas kernels: 106 us -> 110 us
    pallas_call x1, Pallas kernels: 3.83 us -> 7.54 us  [run_own(): pl.pallas_call(own_kernel, out_shape=(jax.ShapeDtypeStruct((4, 2, 128), F...]
    unnamed x20 -> x22, local copies, waits for them, and re-layouts: 4.99 us -> 4.11 us
  transfers between devices with their start and end apart: 7 -> 7, of which waited for: 6 -> 6; matrix products, arithmetic and copies ran while one was open for 1% -> 2% of each run, Pallas kernels for 4% -> 4%
where the time goes in v7:
time: 199 us
  Pallas kernels  110 us (55%)
  starting transfers between devices  38.3 us (19%)
  blocking collectives  20.8 us (10%)
  waiting for transfers between devices  17.3 us (9%)
  local copies, waits for them, and re-layouts  8.37 us (4%)
  other arithmetic  3.1 us (2%)
    pallas_call x1, Pallas kernels, run_blocks(): pl.pallas_call(block_kernel, out_shape=(jax.ShapeDtypeStruct((8, 128), F3...  91.6 us
    all_to_all x1, blocking collectives, body(): elements = lax.all_to_all(element, TIME, 0, 0, tiled=True)  20.8 us
    ppermute x1, starting transfers between devices, body(): s1 = lax.ppermute(x_end, 'h', [(0, 1)]).reshape(32, 32)  13.1 us
    all_to_all x1, starting transfers between devices, body(): got = lax.all_to_all(own, PLANE, 0, 0, tiled=True)  9.18 us
    pallas_call x1, Pallas kernels, prepare(): pl.pallas_call(prepare_kernel, out_shape=(*[jax.ShapeDtypeStruct(*o) for...  7.89 us
    pallas_call x1, Pallas kernels, run_own(): pl.pallas_call(own_kernel, out_shape=(jax.ShapeDtypeStruct((4, 2, 128), F...  7.54 us
    all_to_all x1, waiting for transfers between devices, body(): s2 = lax.all_to_all(part.reshape(32, 32), PLANE, 0, 0, tiled=True)  6.89 us
    ppermute x3, starting transfers between devices, body(): lax.ppermute(own, 'l', [(i, (i + n) % 4) for i in range(4)])  6.26 us
  transfers between devices with their start and end apart: 7, of which 6 were waited for; matrix products, arithmetic and copies ran while one was open for 2% of the time, Pallas kernels for 4%

profile of v7, /device:TPU:1, one launch (start us, length us, event | category | flops | bytes accessed | tf_op | source)
XLA Modules:
  0.0 198.8 jit_solution(14456200325845845601)
XLA Ops:
  0.6 0.7 constant_dynamic-slice_fusion.1
  1.3 0.7 dynamic-slice_convert_fusion
  2.1 2.5 %collective-permute-start = (f32[8,128]{1,0:T(8,128)S(1)}, f32[8,128]{1,0:T(8,128)S(1)}, u32[]{:S(2)}, u32[]{:S(2)}) collective-permute-start(f32[8,128]{1,0:T(8,128)S(1)} %get-tuple-element.27), channel_id=1, source_target_pairs={{0,32},{32,64},{64,96},{96,0},{1,33},{33,65},{65,97},{97,1},{2,34}... | collective-permute-start | bytes 12296 | tf_op jit(solution)/shard_map/ppermute | solution.py:425
  4.6 3.0 %collective-permute-start.1 = (f32[8,128]{1,0:T(8,128)S(1)}, f32[8,128]{1,0:T(8,128)S(1)}, u32[]{:S(2)}, u32[]{:S(2)}) collective-permute-start(f32[8,128]{1,0:T(8,128)S(1)} %get-tuple-element.27), channel_id=1, source_target_pairs={{0,64},{32,96},{64,0},{96,32},{1,65},{33,97},{65,1},{97,33},{2,66}... | collective-permute-start | bytes 12296 | tf_op jit(solution)/shard_map/ppermute | solution.py:425
  7.6 0.7 collective-permute-start.2
  8.3 0.0 collective-permute-done
  8.3 0.3 collective-permute-done.1
  8.6 1.8 collective-permute-done.2
  10.3 0.9 broadcast_in_dim.10
  11.2 9.2 %all-to-all-start = ((f32[32,4,8,128]{3,2,1,0:T(8,128)}), f32[32,4,8,128]{3,2,1,0:T(8,128)S(1)}, u32[]{:S(2)}, u32[]{:S(2)}) async-start(f32[32,4,8,128]{3,2,1,0:T(8,128)} %broadcast_in_dim.10), calls=%async_computation | async-start | bytes 1048576 | tf_op jit(solution)/shard_map/all_to_all | solution.py:428
  20.4 0.6 stack.42.at_ref
  21.0 7.9 %prepare.1 = (bf16[1024,512]{1,0:T(8,128)(2,1)}, bf16[1024,512]{1,0:T(8,128)(2,1)}, bf16[1536,1024]{1,0:T(8,128)(2,1)}, bf16[1536,1024]{1,0:T(8,128)(2,1)}, f32[1,1024]{1,0:T(1,128)}) custom-call(f32[1024,1024]{1,0:T(8,128)} %f_any.5, f32[512,1024]{1,0:T(8,128)} %h_any.5), custom_call_target="tpu_custom_call" | custom-call | flops 3221225472 | bytes 14680064 | tf_op jit(solution)/shard_map/prepare/pallas_call | solution.py:140
  28.9 2.5 %all-to-all-done.got_ref = f32[32,4,8,128]{3,2,1,0:T(8,128)S(1)} async-done(((f32[32,4,8,128]{3,2,1,0:T(8,128)}), f32[32,4,8,128]{3,2,1,0:T(8,128)S(1)}, u32[]{:S(2)}, u32[]{:S(2)}) %all-to-all-start) | async-done | bytes 524320 | tf_op jit(solution)/shard_map/all_to_all | solution.py:428
  31.4 0.0 copy-start.6
  31.4 0.8 copy-done.6
  32.2 0.0 copy-start.2
  32.2 0.0 copy-start.8
  32.2 0.0 copy-start.9
  32.2 91.6 %blocks.1 = (f32[8,128]{1,0:T(8,128)}, f32[8,128]{1,0:T(8,128)}, f32[8,40,1024]{2,1,0:T(8,128)}, f32[40,1024]{1,0:T(8,128)}) custom-call(s32[6]{0:T(128)} %stack.42.at_ref, f32[32,4,8,128]{3,2,1,0:T(8,128)} %copy-done.6, f32[8,128]{1,0:T(8,128)} %bitcast.25, f32[4,128]{1,0:T(4,128)} %bitcast.21, f32[1,1024]{1,0:T(1,128)} %get-tuple-element.14.diag_ref, ...), custom_call_target="tpu_custom_call" | custom-call | tf_op jit(solution)/shard_map/blocks/pallas_call | solution.py:269
  123.8 13.1 %collective-permute-start.3 = (f32[8,128]{1,0:T(8,128)}, f32[8,128]{1,0:T(8,128)S(1)}, u32[]{:S(2)}, u32[]{:S(2)}) collective-permute-start(f32[8,128]{1,0:T(8,128)} %get-tuple-element.20), channel_id=1, source_target_pairs={{0,128},{1,129},{2,130},{3,131},{4,132},{5,133},{6,134},{7,135},{8... | collective-permute-start | bytes 12296 | tf_op jit(solution)/shard_map/ppermute | solution.py:431
  137.0 0.8 fusion
  137.8 0.1 select_n.38
  137.8 0.1 collective-permute-done.3
  137.9 0.1 reshape.66
  138.0 1.0 multiply_reduce_fusion
  139.0 0.1 reduce_sum.12
  139.1 0.6 add.45
  139.7 5.7 %all-to-all-start.1 = ((f32[32,1,32]{2,1,0:T(1,128)}), f32[32,1,32]{2,1,0:T(1,128)S(1)}, u32[]{:S(2)}, u32[]{:S(2)}) async-start(f32[32,1,32]{2,1,0:T(1,128)} %add.45), calls=%async_computation.1 | async-start | bytes 32768 | tf_op jit(solution)/shard_map/all_to_all | solution.py:434
  145.5 6.9 %all-to-all-done.1 = f32[32,1,32]{2,1,0:T(1,128)S(1)} async-done(((f32[32,1,32]{2,1,0:T(1,128)}), f32[32,1,32]{2,1,0:T(1,128)S(1)}, u32[]{:S(2)}, u32[]{:S(2)}) %all-to-all-start.1) | async-done | bytes 4128 | tf_op jit(solution)/shard_map/all_to_all | solution.py:434
  152.4 0.0 copy-done.2
  152.4 1.3 copy-done
  153.7 1.4 parts.1
  155.1 4.0 %all-to-all-start.2 = ((f32[32,8,128]{2,1,0:T(8,128)}), f32[32,8,128]{2,1,0:T(8,128)S(1)}, u32[]{:S(2)}, u32[]{:S(2)}) async-start(f32[32,8,128]{2,1,0:T(8,128)} %parts.1), calls=%async_computation.2 | async-start | bytes 262144 | tf_op jit(solution)/shard_map/all_to_all | solution.py:435
  159.2 0.0 copy-done.8
  159.2 0.0 copy-done.9
  159.2 0.6 reshape.59.z_ref
  159.8 0.0 copy-done.10
  159.8 0.6 reshape.62.d_ref
  160.4 0.6 reshape.60.m_ref
  161.0 5.8 %all-to-all-done.2.got_ref = f32[32,8,128]{2,1,0:T(8,128)S(1)} async-done(((f32[32,8,128]{2,1,0:T(8,128)}), f32[32,8,128]{2,1,0:T(8,128)S(1)}, u32[]{:S(2)}, u32[]{:S(2)}) %all-to-all-start.2) | async-done | bytes 131104 | tf_op jit(solution)/shard_map/all_to_all | solution.py:435
  166.8 0.7 copy-done.7
  167.5 7.5 %own_steps.1 = (f32[4,2,128]{2,1,0:T(2,128)}, f32[4,2,128]{2,1,0:T(2,128)}, f32[64,4,128]{2,1,0:T(4,128)}) custom-call(s32[6]{0:T(128)} %stack.42.at_ref, f32[4,4,128]{2,1,0:T(4,128)} %reshape.59.z_ref, f32[4,4,128]{2,1,0:T(4,128)} %reshape.60.m_ref, f32[1024,1024]{1,0:T(8,128)} %f_any.5, f32[512,1024]{1,0:T(8,128)} %h_any.5, f32[4,128]{1,0:T(4,128)} %bitcast.22, ...), custom_call_target="tpu_custom_call" | custom-call | tf_op jit(solution)/shard_map/own_steps/pallas_call | solution.py:363
  175.0 20.8 %all_to_all.23.parts_ref = f32[64,4,128]{2,1,0:T(4,128)S(1)} all-to-all(f32[64,4,128]{2,1,0:T(4,128)} %get-tuple-element.23), channel_id=1, replica_groups=mesh['h'=2,'l'=4,'x'=4,'c'=2,'y'=4] {'h','l','x','c'}, dimensions={0} | all-to-all | bytes 262144 | tf_op jit(solution)/shard_map/all_to_all | solution.py:440
  195.8 0.0 copy-done.1
  195.8 0.0 copy-done.3
  195.9 0.7 copy-done.4
  196.5 0.7 copy-done.5
  197.2 1.6 smooth_own.1
  (12 shorter events, 0.0 us)
Async XLA Ops:
  2.1 6.3 %collective-permute-start = (f32[8,128]{1,0:T(8,128)S(1)}, f32[8,128]{1,0:T(8,128)S(1)}, u32[]{:S(2)}, u32[]{:S(2)}) collective-permute-start(f32[8,128]{1,0:T(8,128)S(1)} %get-tuple-element.27), channel_id=1, source_target_pairs={{0,32},{32,64},{64,96},{96,0},{1,33},{33,65},{65,97},{97,1},{2,34}... | collective-permute-start | bytes 12296 | tf_op jit(solution)/shard_map/ppermute | solution.py:425
  4.6 4.0 %collective-permute-start.1 = (f32[8,128]{1,0:T(8,128)S(1)}, f32[8,128]{1,0:T(8,128)S(1)}, u32[]{:S(2)}, u32[]{:S(2)}) collective-permute-start(f32[8,128]{1,0:T(8,128)S(1)} %get-tuple-element.27), channel_id=1, source_target_pairs={{0,64},{32,96},{64,0},{96,32},{1,65},{33,97},{65,1},{97,33},{2,66}... | collective-permute-start | bytes 12296 | tf_op jit(solution)/shard_map/ppermute | solution.py:425
  7.6 2.8 %collective-permute-start.2 = (f32[8,128]{1,0:T(8,128)S(1)}, f32[8,128]{1,0:T(8,128)S(1)}, u32[]{:S(2)}, u32[]{:S(2)}) collective-permute-start(f32[8,128]{1,0:T(8,128)S(1)} %get-tuple-element.27), channel_id=1, source_target_pairs={{0,96},{32,0},{64,32},{96,64},{1,97},{33,1},{65,33},{97,65},{2,98}... | collective-permute-start | bytes 12296 | tf_op jit(solution)/shard_map/ppermute | solution.py:425
  11.2 20.2 %all-to-all-start = ((f32[32,4,8,128]{3,2,1,0:T(8,128)}), f32[32,4,8,128]{3,2,1,0:T(8,128)S(1)}, u32[]{:S(2)}, u32[]{:S(2)}) async-start(f32[32,4,8,128]{3,2,1,0:T(8,128)} %broadcast_in_dim.10), calls=%async_computation | async-start | bytes 1048576 | tf_op jit(solution)/shard_map/all_to_all | solution.py:428
  31.4 0.8 copy-start.6
  32.2 120.2 %copy-start.2 = (s32[6]{0:T(128)S(1)}, s32[6]{0:T(128)}, u32[]{:S(2)}) copy-start(s32[6]{0:T(128)} %stack.42.at_ref) | copy-start | bytes 76
  32.2 126.9 %copy-start.8 = (s32[4,512]{1,0:T(4,128)S(1)}, s32[4,512]{1,0:T(4,128)}, u32[]{:S(2)}) copy-start(s32[4,512]{1,0:T(4,128)} %param.8) | copy-start | bytes 24580
  32.2 127.0 %copy-start.9 = (f32[4,512]{1,0:T(4,128)S(1)}, f32[4,512]{1,0:T(4,128)}, u32[]{:S(2)}) copy-start(f32[4,512]{1,0:T(4,128)} %param.7) | copy-start | bytes 24580
  32.2 127.6 %copy-start.10 = (f32[4,256]{1,0:T(4,128)S(1)}, f32[4,256]{1,0:T(4,128)}, u32[]{:S(2)}) copy-start(f32[4,256]{1,0:T(4,128)} %param.12) | copy-start | bytes 12292
  123.8 14.1 %collective-permute-start.3 = (f32[8,128]{1,0:T(8,128)}, f32[8,128]{1,0:T(8,128)S(1)}, u32[]{:S(2)}, u32[]{:S(2)}) collective-permute-start(f32[8,128]{1,0:T(8,128)} %get-tuple-element.20), channel_id=1, source_target_pairs={{0,128},{1,129},{2,130},{3,131},{4,132},{5,133},{6,134},{7,135},{8... | collective-permute-start | bytes 12296 | tf_op jit(solution)/shard_map/ppermute | solution.py:431
  139.7 12.7 %all-to-all-start.1 = ((f32[32,1,32]{2,1,0:T(1,128)}), f32[32,1,32]{2,1,0:T(1,128)S(1)}, u32[]{:S(2)}, u32[]{:S(2)}) async-start(f32[32,1,32]{2,1,0:T(1,128)} %add.45), calls=%async_computation.1 | async-start | bytes 32768 | tf_op jit(solution)/shard_map/all_to_all | solution.py:434
  152.4 1.3 copy-start
  155.1 11.7 %all-to-all-start.2 = ((f32[32,8,128]{2,1,0:T(8,128)}), f32[32,8,128]{2,1,0:T(8,128)S(1)}, u32[]{:S(2)}, u32[]{:S(2)}) async-start(f32[32,8,128]{2,1,0:T(8,128)} %parts.1), calls=%async_computation.2 | async-start | bytes 262144 | tf_op jit(solution)/shard_map/all_to_all | solution.py:435
  166.8 0.7 copy-start.7
  167.5 28.4 %copy-start.1 = (f32[4,2,128]{2,1,0:T(2,128)S(1)}, f32[4,2,128]{2,1,0:T(2,128)}, u32[]{:S(2)}) copy-start(f32[4,2,128]{2,1,0:T(2,128)} %reshape.62.d_ref) | copy-start | bytes 12292
  167.5 28.4 %copy-start.3 = (s32[6]{0:T(128)S(1)}, s32[6]{0:T(128)}, u32[]{:S(2)}) copy-start(s32[6]{0:T(128)} %stack.42.at_ref) | copy-start | bytes 76
  195.9 0.7 copy-start.4
  196.5 0.7 copy-start.5
